TPU v7x, 128 devices: a whole 4x4x4 slice. The times are simulated.
128 devices in a mesh: row: 8 (over x_hi, y), col: 16 (over z, x_lo, core).
Axes of the slice: x: 4 (x_hi: 2, x_lo: 2; x = x_hi * 2 + x_lo), y: 4, z: 4, core: 2. Of those that a mesh axis runs over, the one named last changes fastest.
Arguments:
- val_band: int32 [2048], P(('row', 'col')), may hold values from 0 to 1023, as said below
- cond_band: int32 [2048], P(('row', 'col')), may hold values from 0 to 1023, as said below
- val_orbitals: bfloat16 [1024, 524288], P(('row', 'col')), may hold values from -6 to 6
- cond_orbitals: bfloat16 [1024, 524288], P(('row', 'col')), may hold values from -6 to 6
- val_energy: float32 [1024], replicated, may hold values from -14 to -2
- cond_energy: float32 [1024], replicated, may hold values from 0.5 to 12
- gvec_index: int32 [10240], replicated, may hold values from 0 to 524287, as said below
Outputs:
- chi_real: float32 [10240, 10240], P('row', 'col')
- chi_imag: float32 [10240, 10240], P('row', 'col')
Inputs may be any that keep to these rules, and one draw needn't show every extreme that they name: `val_band`: pair p's valence band lies in the block of 8 bands that starts at (p // 16) * 8. `cond_band`: pair p's conduction band lies in the block of 8 bands that starts at (p // 16) * 8. `gvec_index`: all entries differ; each is (kx * 64 + ky) * 128 + kz with kx in 0 to 15 or 48 to 63, ky in 0 to 15 or 48 to 63, and kz in 0 to 31 or 96 to 127.
All inputs are finite; a program needn't handle non-finite values.
Results may differ from a plain program's by a relative error of at most 0.0041.
Values may be sent and summed in bfloat16 or wider, within the bound.
No kernel may reach another device: no remote copies, remote signals or barrier semaphores. Data moves between devices by JAX's collectives and lax.ppermute only.
A program may use at most 192 MiB of HBM per device.

v0:
```python
import math

import jax
import jax.numpy as jnp
from jax import lax
from jax.sharding import PartitionSpec as P

GX = 64
GY = 64
GZ = 128
HX = 16
HZ = 32


triple = lax.Precision.HIGH


def freq_tables(length, half):
    positions = jnp.arange(length, dtype=jnp.int32)
    kept = jnp.concatenate(
        [jnp.arange(half, dtype=jnp.int32), length - half + jnp.arange(half, dtype=jnp.int32)]
    )
    angle = (positions[:, None] * kept[None, :] % length).astype(jnp.float32) * (
        2.0 * math.pi / length
    )
    return (jnp.cos(angle), jnp.sin(angle))


def select_rows(rows, table):
    choose = (rows[:, None] == jnp.arange(table.shape[0], dtype=jnp.int32)[None, :]).astype(
        jnp.bfloat16
    )
    return jnp.dot(choose, table, preferred_element_type=jnp.float32)


def pick_values(indices, values):
    match = indices[:, None] == jnp.arange(values.shape[0], dtype=jnp.int32)[None, :]
    return jnp.sum(jnp.where(match, values[None, :], 0.0), axis=1)


def pair_elements(val_band, cond_band, val_orbitals, cond_orbitals, gvec_index):
    pair_dev = val_band.shape[0]
    num_gvec = gvec_index.shape[0]
    val_local = val_band % val_orbitals.shape[0]
    cond_local = cond_band % cond_orbitals.shape[0]
    cos_z, sin_z = freq_tables(GZ, HZ)
    cos_y, sin_y = freq_tables(GY, HX)
    grid_x = gvec_index // (GY * GZ)
    grid_y = gvec_index // GZ % GY
    grid_z = gvec_index % GZ
    box_y = jnp.where(grid_y < HX, grid_y, grid_y - (GY - 2 * HX))
    box_z = jnp.where(grid_z < HZ, grid_z, grid_z - (GZ - 2 * HZ))
    plane_index = box_y * (2 * HZ) + box_z
    x_angle = (grid_x[:, None] * jnp.arange(GX, dtype=jnp.int32)[None, :] % GX).astype(
        jnp.float32
    ) * (2.0 * math.pi / GX)
    cos_g = jnp.cos(x_angle)[:, None, :]
    sin_g = jnp.sin(x_angle)[:, None, :]
    inv_root = 1.0 / math.sqrt(GX * GY * GZ)
    block_size = math.gcd(pair_dev, 4)

    def one_block(indices):
        val_rows, cond_rows = indices
        density = select_rows(val_rows, val_orbitals) * select_rows(cond_rows, cond_orbitals)
        density = density.reshape(-1, GZ)
        first_real = jnp.dot(density, cos_z, precision=triple).reshape(block_size, GX, GY, 2 * HZ)
        first_imag = -jnp.dot(density, sin_z, precision=triple).reshape(block_size, GX, GY, 2 * HZ)
        second_real = jnp.einsum("bxyk,yj->bxjk", first_real, cos_y, precision=triple) + jnp.einsum(
            "bxyk,yj->bxjk", first_imag, sin_y, precision=triple
        )
        second_imag = jnp.einsum("bxyk,yj->bxjk", first_imag, cos_y, precision=triple) - jnp.einsum(
            "bxyk,yj->bxjk", first_real, sin_y, precision=triple
        )
        stacked = jnp.concatenate([second_real, second_imag], axis=0)
        columns = stacked.reshape(2 * block_size * GX, 4 * HX * HZ).T
        picked = jnp.take(columns, plane_index, axis=0).reshape(num_gvec, 2, block_size, GX)
        part_real = picked[:, 0]
        part_imag = picked[:, 1]
        real_pick = jnp.sum(part_real * cos_g + part_imag * sin_g, axis=2) * inv_root
        imag_pick = jnp.sum(part_imag * cos_g - part_real * sin_g, axis=2) * inv_root
        return (real_pick.T, imag_pick.T)

    real_all, imag_all = lax.map(
        one_block, (val_local.reshape(-1, block_size), cond_local.reshape(-1, block_size))
    )
    return jnp.stack([real_all.reshape(pair_dev, num_gvec), imag_all.reshape(pair_dev, num_gvec)])


def panel_product(left_block, right_real, right_imag):
    count = left_block.shape[1]
    left_side = left_block.reshape(2 * count, left_block.shape[2])
    dims = (((0,), (0,)), ((), ()))
    real_part = lax.dot_general(
        left_side, right_real.reshape(2 * count, -1), dims, preferred_element_type=jnp.float32
    )
    imag_part = lax.dot_general(
        left_side, right_imag.reshape(2 * count, -1), dims, preferred_element_type=jnp.float32
    )
    return jnp.stack([real_part, imag_part])


def local(val_band, cond_band, val_orbitals, cond_orbitals, val_energy, cond_energy, gvec_index):
    row_count = lax.axis_size("row")
    col_count = lax.axis_size("col")
    pair_dev = val_band.shape[0]
    pairs_all = pair_dev * row_count * col_count
    num_gvec = gvec_index.shape[0]
    elements = pair_elements(val_band, cond_band, val_orbitals, cond_orbitals, gvec_index)
    energy_gap = pick_values(cond_band, cond_energy) - pick_values(val_band, val_energy)
    factor = -4.0 / (math.sqrt(pairs_all) * energy_gap)
    plain_elems = elements.astype(jnp.bfloat16)
    weighted = (elements * factor[None, :, None]).astype(jnp.bfloat16)
    slice_len = num_gvec // (row_count * col_count)
    col_order = (
        weighted.reshape(2, pair_dev, col_count, row_count, slice_len)
        .transpose(0, 1, 3, 2, 4)
        .reshape(2, pair_dev, num_gvec)
    )
    rows_recv, cols_recv = (
        lax.all_to_all(plain_elems, ("row", "col"), split_axis=2, concat_axis=1, tiled=True),
        lax.all_to_all(col_order, ("row", "col"), split_axis=2, concat_axis=1, tiled=True),
    )
    col_block = lax.all_gather(cols_recv, "row", axis=2, tiled=True)
    right_imag = jnp.stack([-col_block[1], col_block[0]])
    result = panel_product(
        lax.all_gather(rows_recv, "col", axis=2, tiled=True), col_block, right_imag
    )
    return (result[0], result[1])


def solution(mesh):
    return jax.shard_map(
        local,
        mesh=mesh,
        in_specs=(
            P(("row", "col")),
            P(("row", "col")),
            P(("row", "col"), None),
            P(("row", "col"), None),
            P(),
            P(),
            P(),
        ),
        out_specs=(P("row", "col"), P("row", "col")),
        check_vma=False,
    )
```

profile of v0, /device:TPU:1, one launch (start us, length us, event | category | flops | bytes accessed | tf_op | source)
XLA Modules:
  0.0 885.7 jit_solution(17305879783579680399)
XLA Ops:
  9.8 626.6 %while.14 = (s32[]{:T(128)}, f32[4,4,10240]{2,1,0:T(4,128)S(1)}, f32[4,4,10240]{2,1,0:T(4,128)S(1)}, s32[10240]{0:T(1024)S(1)}, s32[4,4]{1,0:T(4,128)S(1)}, /*in...) while((s32[]{:T(128)}, f32[4,4,10240]{2,1,0:T(4,128)S(1)}, ...), condition=%wide.region_3.4_spmd.clone.clone, body=%wide.region_0.3_spmd.clone.clone.sunk | while | flops 2525155328 | bytes 305378528 | solution.py:83
  19.0 11.4 %fusion.153 = f32[1,4,4096,128]{3,1,2,0:T(4,128)} fusion(f32[4,524288]{1,0:T(4,128)} %fusion.151, bf16[8,524288]{1,0:T(8,128)(2,1)} %get-tuple-element.297, s32[4]{0:T(128)S(1)} %fusion.152), kind=kOutput, calls=%fused_computation.18.clone.1 | convolution fusion | flops 35651616 | bytes 25165840 | tf_op jit(solution)/shard_map/while/body/eval_jaxpr/dot_general | solution.py:33
  75.5 45.6 %gather_fusion = f32[10240,512]{1,0:T(8,128)} fusion(f32[2048,512]{1,0:T(8,128)} %bitcast.148, s32[10240]{0:T(1024)S(1)} %broadcast_clamp_fusion.2), kind=kCustom, calls=%fused_computation.clone.clone.clone.1 | custom fusion | bytes 41984000 | tf_op jit(solution)/shard_map/while/body/eval_jaxpr/jit(_take)/gather | solution.py:76
  121.1 19.9 %copy.77 = f32[10240,512]{0,1:T(8,128)} copy(f32[10240,512]{1,0:T(8,128)} %gather_fusion) | data formatting | bytes 41943040 | tf_op jit(solution)/shard_map/while/body/eval_jaxpr/jit(_take)/gather | solution.py:76
  149.3 10.1 %cosine_bitcast_fusion.2 = (f32[10240,64]{0,1:T(8,128)S(1)}, f32[10240,64]{0,1:T(8,128)S(1)}) fusion(s32[10240]{0:T(1024)S(1)} %get-tuple-element.300), kind=kLoop, calls=%fused_computation.28.clone.1 | loop fusion | flops 9175040 | bytes 5283840 | tf_op jit(solution)/shard_map/while/body/eval_jaxpr/mul | solution.py:79
  174.1 11.4 %fusion.153 = f32[1,4,4096,128]{3,1,2,0:T(4,128)} fusion(f32[4,524288]{1,0:T(4,128)} %fusion.151, bf16[8,524288]{1,0:T(8,128)(2,1)} %get-tuple-element.297, s32[4]{0:T(128)S(1)} %fusion.152), kind=kOutput, calls=%fused_computation.18.clone.1 | convolution fusion | flops 35651616 | bytes 25165840 | tf_op jit(solution)/shard_map/while/body/eval_jaxpr/dot_general | solution.py:33
  230.4 45.6 %gather_fusion = f32[10240,512]{1,0:T(8,128)} fusion(f32[2048,512]{1,0:T(8,128)} %bitcast.148, s32[10240]{0:T(1024)S(1)} %broadcast_clamp_fusion.2), kind=kCustom, calls=%fused_computation.clone.clone.clone.1 | custom fusion | bytes 41984000 | tf_op jit(solution)/shard_map/while/body/eval_jaxpr/jit(_take)/gather | solution.py:76
  276.0 19.9 %copy.77 = f32[10240,512]{0,1:T(8,128)} copy(f32[10240,512]{1,0:T(8,128)} %gather_fusion) | data formatting | bytes 41943040 | tf_op jit(solution)/shard_map/while/body/eval_jaxpr/jit(_take)/gather | solution.py:76
  304.4 10.1 %cosine_bitcast_fusion.2 = (f32[10240,64]{0,1:T(8,128)S(1)}, f32[10240,64]{0,1:T(8,128)S(1)}) fusion(s32[10240]{0:T(1024)S(1)} %get-tuple-element.300), kind=kLoop, calls=%fused_computation.28.clone.1 | loop fusion | flops 9175040 | bytes 5283840 | tf_op jit(solution)/shard_map/while/body/eval_jaxpr/mul | solution.py:79
  329.0 11.4 %fusion.153 = f32[1,4,4096,128]{3,1,2,0:T(4,128)} fusion(f32[4,524288]{1,0:T(4,128)} %fusion.151, bf16[8,524288]{1,0:T(8,128)(2,1)} %get-tuple-element.297, s32[4]{0:T(128)S(1)} %fusion.152), kind=kOutput, calls=%fused_computation.18.clone.1 | convolution fusion | flops 35651616 | bytes 25165840 | tf_op jit(solution)/shard_map/while/body/eval_jaxpr/dot_general | solution.py:33
  385.5 45.6 %gather_fusion = f32[10240,512]{1,0:T(8,128)} fusion(f32[2048,512]{1,0:T(8,128)} %bitcast.148, s32[10240]{0:T(1024)S(1)} %broadcast_clamp_fusion.2), kind=kCustom, calls=%fused_computation.clone.clone.clone.1 | custom fusion | bytes 41984000 | tf_op jit(solution)/shard_map/while/body/eval_jaxpr/jit(_take)/gather | solution.py:76
  431.1 19.9 %copy.77 = f32[10240,512]{0,1:T(8,128)} copy(f32[10240,512]{1,0:T(8,128)} %gather_fusion) | data formatting | bytes 41943040 | tf_op jit(solution)/shard_map/while/body/eval_jaxpr/jit(_take)/gather | solution.py:76
  459.3 10.1 %cosine_bitcast_fusion.2 = (f32[10240,64]{0,1:T(8,128)S(1)}, f32[10240,64]{0,1:T(8,128)S(1)}) fusion(s32[10240]{0:T(1024)S(1)} %get-tuple-element.300), kind=kLoop, calls=%fused_computation.28.clone.1 | loop fusion | flops 9175040 | bytes 5283840 | tf_op jit(solution)/shard_map/while/body/eval_jaxpr/mul | solution.py:79
  484.1 11.4 %fusion.153 = f32[1,4,4096,128]{3,1,2,0:T(4,128)} fusion(f32[4,524288]{1,0:T(4,128)} %fusion.151, bf16[8,524288]{1,0:T(8,128)(2,1)} %get-tuple-element.297, s32[4]{0:T(128)S(1)} %fusion.152), kind=kOutput, calls=%fused_computation.18.clone.1 | convolution fusion | flops 35651616 | bytes 25165840 | tf_op jit(solution)/shard_map/while/body/eval_jaxpr/dot_general | solution.py:33
  540.4 45.6 %gather_fusion = f32[10240,512]{1,0:T(8,128)} fusion(f32[2048,512]{1,0:T(8,128)} %bitcast.148, s32[10240]{0:T(1024)S(1)} %broadcast_clamp_fusion.2), kind=kCustom, calls=%fused_computation.clone.clone.clone.1 | custom fusion | bytes 41984000 | tf_op jit(solution)/shard_map/while/body/eval_jaxpr/jit(_take)/gather | solution.py:76
  586.0 19.9 %copy.77 = f32[10240,512]{0,1:T(8,128)} copy(f32[10240,512]{1,0:T(8,128)} %gather_fusion) | data formatting | bytes 41943040 | tf_op jit(solution)/shard_map/while/body/eval_jaxpr/jit(_take)/gather | solution.py:76
  614.5 10.1 %cosine_bitcast_fusion.2 = (f32[10240,64]{0,1:T(8,128)S(1)}, f32[10240,64]{0,1:T(8,128)S(1)}) fusion(s32[10240]{0:T(1024)S(1)} %get-tuple-element.300), kind=kLoop, calls=%fused_computation.28.clone.1 | loop fusion | flops 9175040 | bytes 5283840 | tf_op jit(solution)/shard_map/while/body/eval_jaxpr/mul | solution.py:79
  646.6 15.1 %reshape.194 = bf16[128,2,1280]{2,1,0:T(2,128)(2,1)S(1)} reshape(bf16[10240,2,16]{2,1,0:T(2,128)(2,1)} %bitcast.152) | data formatting | bytes 1310720
  661.6 26.1 %all_to_all.36 = bf16[128,2,1280]{2,1,0:T(2,128)(2,1)S(1)} all-to-all(bf16[128,2,1280]{2,1,0:T(2,128)(2,1)S(1)} %reshape.194), channel_id=1, replica_groups=mesh['row'=8,'col'=16] {'row','col'}, dimensions={0} | all-to-all | bytes 1310720 | tf_op jit(solution)/shard_map/all_to_all | solution.py:121
  704.2 19.5 %copy.50 = bf16[2,16,10240]{1,0,2:T(2,128)(2,1)} copy(bf16[2,16,10240]{2,1,0:T(8,128)(2,1)S(1)} %pad_maximum_fusion.1) | data formatting | bytes 1310720 | tf_op jit(solution)/shard_map/stack | solution.py:86
  723.8 15.1 %reshape.192 = bf16[128,2,1280]{2,1,0:T(2,128)(2,1)S(1)} reshape(bf16[10240,2,16]{2,1,0:T(2,128)(2,1)} %bitcast.154) | data formatting | bytes 1310720
  738.8 26.7 %all_to_all.37 = bf16[128,2,1280]{2,1,0:T(2,128)(2,1)S(1)} all-to-all(bf16[128,2,1280]{2,1,0:T(2,128)(2,1)S(1)} %reshape.192), channel_id=1, replica_groups=mesh['row'=8,'col'=16] {'row','col'}, dimensions={0} | all-to-all | bytes 1310720 | tf_op jit(solution)/shard_map/all_to_all | solution.py:120
  791.3 63.3 %all-gather.3.cloned.1.call-done = bf16[2,2048,1280]{1,2,0:T(8,128)(2,1)} async-done(((bf16[2,2048,80]{1,2,0:T(8,128)(2,1)}), bf16[2,2048,1280]{1,2,0:T(8,128)(2,1)}) %all-gather.3.cloned.1.call-update) | async-done | bytes 10485776 | tf_op jit(solution)/shard_map/all_gather | solution.py:126
  854.7 13.9 %convolution_bitcast_fusion = f32[1280,640]{1,0:T(8,128)} fusion(bf16[2,2048,1280]{1,2,0:T(8,128)(2,1)} %all-gather.3.cloned.1.call-done, bf16[2,2048,640]{1,2,0:T(8,128)(2,1)} %all-gather.5.cloned.1.call-done), kind=kOutput, calls=%fused_computation.108 | convolution fusion | flops 6710886400 | bytes 19005440 | tf_op jit(solution)/shard_map/dot_general | solution.py:93
  (135 shorter events, 335.2 us)
Async XLA Ops:
  7.2 779.8 %all-gather.5.cloned.1.call-start = ((), (), s32[]{:S(2)}) async-start(), calls=%async_computation.3 | async-start | bytes 5898240 | tf_op jit(solution)/shard_map/all_gather | solution.py:123
  51.5 4.3 copy-start
  206.4 4.3 copy-start
  361.5 4.3 copy-start
  516.4 4.3 copy-start
  636.4 1.7 copy-start.2
  636.4 1.7 copy-start.3
  636.4 1.7 copy-start.4
  636.4 1.7 copy-start.5
  703.7 151.0 %all-gather.3.cloned.1.call-start = ((), (), s32[]{:S(2)}) async-start(), calls=%async_computation.2 | async-start | bytes 11141120 | tf_op jit(solution)/shard_map/all_gather | solution.py:126
  854.7 13.9 %copy-start.1 = (bf16[1,2048,640]{1,2,0:T(8,128)(2,1)S(1)}, bf16[1,2048,640]{1,2,0:T(8,128)(2,1)}, u32[]{:S(2)}) copy-start(bf16[1,2048,640]{1,2,0:T(8,128)(2,1)} %get-tuple-element.182) | copy-start | bytes 7864324
  854.7 13.9 %copy-start.6 = (bf16[2,2048,1280]{1,2,0:T(8,128)(2,1)S(1)}, bf16[2,2048,1280]{1,2,0:T(8,128)(2,1)}, u32[]{:S(2)}) copy-start(bf16[2,2048,1280]{1,2,0:T(8,128)(2,1)} %all-gather.3.cloned.1.call-done) | copy-start | bytes 31457284
Sparse Core Ops, SparseCore 0:
  703.8 83.0 all-gather.4
  789.2 65.4 all-gather.2
where the time goes:
time: 888 us; the launch traced here: 886 us
  local copies, waits for them, and re-layouts  422 us (48%)
  matrix products  191 us (22%)
  other arithmetic  128 us (14%)
  waiting for transfers between devices  68.9 us (8%)
  blocking collectives  52.8 us (6%)
  between operations  14.4 us (2%)
    gather x8, local copies, waits for them, and re-layouts, one_block(): jnp.take(columns, plane_index, axis=0).reshape(num_gvec, 2, block_size, GX)  262 us
    dot_general x8, matrix products, select_rows(): return jnp.dot(choose, table, preferred_element_type=jnp.float32)  81.5 us
    all_gather x1, waiting for transfers between devices, local(): lax.all_gather(rows_recv, 'col', axis=2, tiled=True)  63.3 us
    reshape x8, local copies, waits for them, and re-layouts, one_block(): columns = stacked.reshape(2 * block_size * GX, 4 * HX * HZ).T  52.8 us
    mul x4, other arithmetic, one_block(): part_real * cos_g + part_imag * sin_g  40.5 us
    unnamed x16, local copies, waits for them, and re-layouts  40.2 us
    select_n x8, other arithmetic, one_block(): jnp.take(columns, plane_index, axis=0).reshape(num_gvec, 2, block_size, GX)  33.7 us
    all_to_all x1, blocking collectives, local(): lax.all_to_all(plain_elems, ('row', 'col'), split_axis=2, concat_axis=1,...  26.7 us
  transfers between devices with their start and end apart: 2, of which 2 were waited for; matrix products, arithmetic and copies ran while one was open for 6% of the time, Pallas kernels for 0%

commit v1 on v0

v1 whole, which is shorter than its diff:
```python
import functools
import math

import jax
import jax.numpy as jnp
import ml_dtypes
import numpy as np
from jax import lax
from jax.experimental import pallas as pl
from jax.experimental.pallas import tpu as pltpu
from jax.sharding import PartitionSpec as P

GX, GY, GZ = 64, 64, 128
HX, HZ = 16, 32
BANDS = 8
GROUP = 8
NKY = HX + 1
ROWS1 = 40
KXP = 40
OCTS = KXP // 8
KZP = 72
SLOTS = NKY * OCTS + 1
XCH = 8
STEPS = GX // XCH
LANES = 128


def split_table(table):
    hi = table.astype(ml_dtypes.bfloat16)
    lo = (table - hi.astype(np.float64)).astype(ml_dtypes.bfloat16)
    return hi, lo


def tables():
    ky = np.arange(NKY)
    ang = 2.0 * np.pi * ((ky[:, None] * np.arange(GY)[None, :]) % GY) / GY
    first = np.zeros((ROWS1, GY))
    first[:NKY] = np.cos(ang)
    first[NKY : 2 * NKY] = -np.sin(ang)
    hi, lo = split_table(first)
    t1 = np.concatenate(
        [np.concatenate([hi, hi], 1), np.concatenate([lo, np.zeros_like(lo)], 1)], 0
    )
    kx = np.arange(2 * HX + 1) - HX
    ang = 2.0 * np.pi * ((kx[:, None] * np.arange(GX)[None, :]) % GX) / GX
    second = np.zeros((2 * KXP, 2 * GX))
    second[: 2 * HX + 1] = np.concatenate([np.cos(ang), np.sin(ang)], 1)
    second[KXP : KXP + 2 * HX + 1] = np.concatenate([-np.sin(ang), np.cos(ang)], 1)
    hi, lo = split_table(second)
    t2 = np.concatenate(
        [np.concatenate([hi, hi], 1), np.concatenate([lo, np.zeros_like(lo)], 1)], 0
    )
    kz = np.arange(2 * HZ + 1) - HZ
    ang = 2.0 * np.pi * ((kz[:, None] * np.arange(GZ)[None, :]) % GZ) / GZ
    third = np.zeros((2 * KZP, GZ))
    third[: 2 * HZ + 1] = np.cos(ang)
    third[KZP : KZP + 2 * HZ + 1] = np.sin(ang)
    hi, lo = split_table(third)
    t3 = np.concatenate(
        [np.concatenate([hi, hi], 1), np.concatenate([lo, np.zeros_like(lo)], 1)], 0
    )
    perm = np.zeros((LANES, LANES))
    for sub in range(8):
        for rp in range(2 * GROUP):
            perm[sub * 2 * GROUP + rp, rp * 8 + sub] = 1.0
    return t1, t2, t3, perm.astype(ml_dtypes.bfloat16)


def split_value(value):
    hi = value.astype(jnp.bfloat16)
    lo = (value - hi.astype(jnp.float32)).astype(jnp.bfloat16)
    return hi, lo


NN = (((1,), (0,)), ((), ()))
NT = (((1,), (1,)), ((), ()))


def mm(a, b, dims):
    return lax.dot_general(a, b, dims, preferred_element_type=jnp.float32)


def elements_kernel(
    row_blocks,
    col_blocks,
    num_gvec,
    val_rows,
    cond_rows,
    where_row,
    val_ref,
    cond_ref,
    t1_ref,
    t2_ref,
    t3_ref,
    perm_ref,
    scale_ref,
    sub_ref,
    sign_ref,
    rows_ref,
    cols_ref,
    uval,
    ucond,
    first,
    second,
    spectrum,
    picked,
):
    step = pl.program_id(0)

    def unpack(i, carry):
        for j in range(16):
            at = i * 16 + j
            columns = pl.ds(pl.multiple_of(at * LANES, LANES), LANES)
            rows = pl.ds(pl.multiple_of(at * BANDS, BANDS), BANDS)
            uval[rows, :] = val_ref[:, columns].astype(jnp.float32)
            ucond[rows, :] = cond_ref[:, columns].astype(jnp.float32)
        return carry

    lax.fori_loop(0, XCH * GY // 16, unpack, 0)

    def pair_first(p, carry):
        vb = val_rows[p]
        cb = cond_rows[p]
        for half in range(XCH // 2):
            parts = []
            for x in (2 * half, 2 * half + 1):
                base = x * GY * BANDS
                density = (
                    uval[pl.ds(base + vb, GY, stride=BANDS), :]
                    * ucond[pl.ds(base + cb, GY, stride=BANDS), :]
                )
                hi, lo = split_value(density)
                parts.append(jnp.concatenate([hi, lo], axis=0))
            out = mm(t1_ref[...], jnp.concatenate(parts, axis=1), NN)
            out = out[:ROWS1] + out[ROWS1:]
            for k in range(2):
                at = (p * GX + step * XCH + 2 * half + k) * ROWS1
                first[pl.ds(pl.multiple_of(at, 8), ROWS1), :] = out[:, k * LANES : (k + 1) * LANES]
        return carry

    lax.fori_loop(0, GROUP, pair_first, 0)

    @pl.when(step == STEPS - 1)
    def _():
        def second_stage(ky, carry):
            for duo in range(GROUP // 2):
                parts = []
                for p in (2 * duo, 2 * duo + 1):
                    base = p * GX * ROWS1
                    real = first[pl.ds(base + ky, GX, stride=ROWS1), :]
                    imag = first[pl.ds(base + NKY + ky, GX, stride=ROWS1), :]
                    rhi, rlo = split_value(real)
                    ihi, ilo = split_value(imag)
                    parts.append(jnp.concatenate([rhi, ihi, rlo, ilo], axis=0))
                out = mm(t2_ref[...], jnp.concatenate(parts, axis=1), NN)
                out = out[: 2 * KXP] + out[2 * KXP :]
                for k in range(2):
                    for o in range(OCTS):
                        for ri in range(2):
                            at = (ky * OCTS + o) * LANES + (ri * GROUP + 2 * duo + k) * 8
                            second[pl.ds(pl.multiple_of(at, 8), 8), :] = out[
                                ri * KXP + o * 8 : ri * KXP + o * 8 + 8,
                                k * LANES : (k + 1) * LANES,
                            ]
            return carry

        lax.fori_loop(0, NKY, second_stage, 0)
        second[(SLOTS - 1) * LANES :, :] = jnp.zeros((LANES, LANES), jnp.float32)

        lane = lax.broadcasted_iota(jnp.int32, (1, LANES), 1)
        scale = scale_ref[...]
        swapped = jnp.where(lane < LANES // 2, scale, -scale)

        def third_stage(b, carry):
            value = second[pl.ds(pl.multiple_of(b * 2 * LANES, 2 * LANES), 2 * LANES), :]
            hi, lo = split_value(value)
            out = mm(t3_ref[...], jnp.concatenate([hi, lo], axis=1), NT)
            out = out[: 2 * KZP] + out[2 * KZP :]
            for k in range(2):
                cos_part = out[:KZP, k * LANES : (k + 1) * LANES]
                sin_part = out[KZP:, k * LANES : (k + 1) * LANES]
                done = cos_part * scale + pltpu.roll(sin_part, LANES // 2, 1) * swapped
                at = (2 * b + k) * KZP
                spectrum[pl.ds(pl.multiple_of(at, 8), KZP), :] = done
            return carry

        lax.fori_loop(0, SLOTS // 2, third_stage, 0)

        block = num_gvec // col_blocks
        per_row = col_blocks // row_blocks

        for b in range(col_blocks):

            def pick(i, carry):
                for j in range(16):
                    at = i * 16 + j
                    picked[pl.ds(at, 1), :] = spectrum[pl.ds(where_row[b * block + at], 1), :]
                return carry

            lax.fori_loop(0, block // 16, pick, 0)
            turned = mm(perm_ref[...], picked[...].astype(jnp.bfloat16), NT)
            sub = sub_ref[:, b * block : (b + 1) * block]
            total = jnp.zeros((2 * GROUP, block), jnp.float32)
            for s in range(8):
                total = jnp.where(sub == s, turned[s * 2 * GROUP : (s + 1) * 2 * GROUP], total)
            sign = sign_ref[:, b * block : (b + 1) * block]
            total = jnp.concatenate([total[:GROUP], total[GROUP:] * sign], axis=0)
            total = total.astype(jnp.bfloat16)
            cols_ref[b] = total
            rows_ref[b // per_row, :, (b % per_row) * block : (b % per_row + 1) * block] = total


def pair_elements(val_rows, cond_rows, scale, val, cond, gvec, row_blocks, col_blocks):
    num_gvec = gvec.shape[0]
    kx = gvec // (GY * GZ)
    ky = gvec // GZ % GY
    kz = gvec % GZ
    kx = jnp.where(kx < GX // 2, kx, kx - GX)
    ky = jnp.where(ky < GY // 2, ky, ky - GY)
    kz = jnp.where(kz < GZ // 2, kz, kz - GZ)
    flip = jnp.where(ky < 0, -1, 1)
    kx, ky, kz = kx * flip + HX, ky * flip, kz * flip + HZ
    where_row = (ky * OCTS + kx // 8) * KZP + kz
    sub = (kx % 8)[None, :]
    sign = flip.astype(jnp.float32)[None, :]
    lanes = jnp.tile(jnp.repeat(scale, 8), 2)[None, :]
    t1, t2, t3, perm = tables()
    whole = lambda shape: pl.BlockSpec(shape, lambda i, *_: (0,) * len(shape))
    width = XCH * GY * GZ
    outs = [
        jax.ShapeDtypeStruct((row_blocks, 2 * GROUP, num_gvec // row_blocks), jnp.bfloat16),
        jax.ShapeDtypeStruct((col_blocks, 2 * GROUP, num_gvec // col_blocks), jnp.bfloat16),
    ]
    return pl.pallas_call(
        functools.partial(elements_kernel, row_blocks, col_blocks, num_gvec),
        out_shape=outs,
        grid_spec=pltpu.PrefetchScalarGridSpec(
            num_scalar_prefetch=3,
            grid=(STEPS,),
            in_specs=[
                pl.BlockSpec((BANDS, width), lambda i, *_: (0, i)),
                pl.BlockSpec((BANDS, width), lambda i, *_: (0, i)),
                whole(t1.shape),
                whole(t2.shape),
                whole(t3.shape),
                whole(perm.shape),
                whole((1, LANES)),
                whole((1, num_gvec)),
                whole((1, num_gvec)),
            ],
            out_specs=[whole(o.shape) for o in outs],
            scratch_shapes=[
                pltpu.VMEM((XCH * GY * BANDS, LANES), jnp.float32),
                pltpu.VMEM((XCH * GY * BANDS, LANES), jnp.float32),
                pltpu.VMEM((GROUP * GX * ROWS1, LANES), jnp.float32),
                pltpu.VMEM((SLOTS * LANES, LANES), jnp.float32),
                pltpu.VMEM((SLOTS * KZP, LANES), jnp.float32),
                pltpu.VMEM((num_gvec // col_blocks, LANES), jnp.float32),
            ],
        ),
        compiler_params=pltpu.CompilerParams(vmem_limit_bytes=56 * 1024 * 1024),
    )(val_rows, cond_rows, where_row, val, cond, t1, t2, t3, perm, lanes, sub, sign)


def pick_values(indices, values):
    match = indices[:, None] == jnp.arange(values.shape[0], dtype=jnp.int32)[None, :]
    return jnp.sum(jnp.where(match, values[None, :], 0.0), axis=1)


def local(val_band, cond_band, val_orbitals, cond_orbitals, val_energy, cond_energy, gvec_index):
    row_count = lax.axis_size("row")
    col_count = lax.axis_size("col")
    pair_dev = val_band.shape[0]
    pairs_all = pair_dev * row_count * col_count
    energy_gap = pick_values(cond_band, cond_energy) - pick_values(val_band, val_energy)
    factor = 4.0 / (math.sqrt(pairs_all) * energy_gap)
    scale = jnp.sqrt(factor) / math.sqrt(GX * GY * GZ)
    val_rows = val_band % val_orbitals.shape[0]
    cond_rows = cond_band % cond_orbitals.shape[0]
    left, right = [], []
    for start in range(0, pair_dev, GROUP):
        part = slice(start, start + GROUP)
        rows_part, cols_part = pair_elements(
            val_rows[part],
            cond_rows[part],
            scale[part],
            val_orbitals,
            cond_orbitals,
            gvec_index,
            row_count,
            col_count,
        )
        rows_recv = lax.all_to_all(rows_part, "row", split_axis=0, concat_axis=0, tiled=True)
        cols_recv = lax.all_to_all(cols_part, "col", split_axis=0, concat_axis=0, tiled=True)
        left.append(lax.all_gather(rows_recv, "col", axis=0, tiled=True))
        right.append(lax.all_gather(cols_recv, "row", axis=0, tiled=True))
    real = imag = 0.0
    dims = (((0,), (0,)), ((), ()))
    for lhs, rhs in zip(left, right):
        lhs = lhs.reshape(-1, lhs.shape[-1])
        rhs = rhs.reshape(row_count, col_count, 2, GROUP, -1).transpose(1, 0, 2, 3, 4)
        flipped = jnp.stack([rhs[:, :, 1], -rhs[:, :, 0]], axis=2)
        rhs = -rhs.reshape(lhs.shape[0], -1)
        flipped = flipped.reshape(lhs.shape[0], -1)
        real = real + lax.dot_general(lhs, rhs, dims, preferred_element_type=jnp.float32)
        imag = imag + lax.dot_general(lhs, flipped, dims, preferred_element_type=jnp.float32)
    return (real, imag)


def solution(mesh):
    return jax.shard_map(
        local,
        mesh=mesh,
        in_specs=(
            P(("row", "col")),
            P(("row", "col")),
            P(("row", "col"), None),
            P(("row", "col"), None),
            P(),
            P(),
            P(),
        ),
        out_specs=(P("row", "col"), P("row", "col")),
        check_vma=False,
    )
```

time: 888 us -> 333 us (0.38)
  local copies, waits for them, and re-layouts: 422 us -> 10.5 us
  matrix products: 191 us -> 32.1 us
  Pallas kernels: 0 us -> 126 us
  other arithmetic: 128 us -> 10.7 us
  waiting for transfers between devices: 68.9 us -> 83.7 us
    gather x8 -> x0, local copies, waits for them, and re-layouts: 262 us -> none  [one_block(): jnp.take(columns, plane_index, axis=0).reshape(num_gvec, 2, block_size, GX)]
    dot_general x34 -> x4, matrix products: 191 us -> 32.1 us  [the longest x2 16.7 us: local(): lax.dot_general(lhs, rhs, dims, preferred_element_type=jnp.float32)]
    pallas_call x0 -> x2, Pallas kernels: none -> 126 us  [pair_elements(): pl.pallas_call(functools.partial(elements_kernel, row_blocks, col_blocks,...]
    reshape x11 -> x0, local copies, waits for them, and re-layouts: 60.8 us -> none  [the longest x8 52.8 us: one_block(): columns = stacked.reshape(2 * block_size * GX, 4 * HX * HZ).T]
    mul x4 -> x0, other arithmetic: 40.5 us -> none  [one_block(): part_real * cos_g + part_imag * sin_g]
    unnamed x16 -> x14, local copies, waits for them, and re-layouts: 40.2 us -> 2.22 us
    select_n x11 -> x3, other arithmetic: 35.9 us -> 2.86 us  [the longest x1 1.53 us: pair_elements(): sub = (kx % 8)[None, :]]
    concatenate x6 -> x0, other arithmetic: 26 us -> none  [the longest x4 25.8 us: one_block(): stacked = jnp.concatenate([second_real, second_imag], axis=0)]
  transfers between devices with their start and end apart: 2 -> 4, of which waited for: 2 -> 3; matrix products, arithmetic and copies ran while one was open for 6% -> 8% of each run, Pallas kernels for 0% -> 19%
where the time goes in v1:
time: 333 us; the launch traced here: 332 us
  Pallas kernels  126 us (38%)
  waiting for transfers between devices  83.7 us (25%)
  blocking collectives  55.1 us (17%)
  matrix products  32.1 us (10%)
  between operations  13.9 us (4%)
  other arithmetic  10.7 us (3%)
  local copies, waits for them, and re-layouts  10.5 us (3%)
    pallas_call x2, Pallas kernels, pair_elements(): pl.pallas_call(functools.partial(elements_kernel, row_blocks, col_blocks,...  126 us
    all_gather x2, waiting for transfers between devices, local(): left.append(lax.all_gather(rows_recv, 'col', axis=0, tiled=True))  58.1 us
    all_to_all x2, blocking collectives, local(): lax.all_to_all(cols_part, 'col', split_axis=0, concat_axis=0, tiled=True)  28.5 us
    all_to_all x2, blocking collectives, local(): lax.all_to_all(rows_part, 'row', split_axis=0, concat_axis=0, tiled=True)  26.6 us
    all_gather x2, waiting for transfers between devices, local(): right.append(lax.all_gather(cols_recv, 'row', axis=0, tiled=True))  25.5 us
    dot_general x2, matrix products, local(): lax.dot_general(lhs, rhs, dims, preferred_element_type=jnp.float32)  16.7 us
    dot_general x2, matrix products, local(): lax.dot_general(lhs, flipped, dims, preferred_element_type=jnp.float32)  15.4 us
  transfers between devices with their start and end apart: 4, of which 3 were waited for; matrix products, arithmetic and copies ran while one was open for 8% of the time, Pallas kernels for 19%

profile of v1, /device:TPU:1, one launch (start us, length us, event | category | flops | bytes accessed | tf_op | source)
XLA Modules:
  0.0 332.3 jit_solution(14315673939967845330)
XLA Ops:
  8.5 0.9 select_reduce_fusion
  10.3 1.4 select_convert_fusion
  11.8 1.5 add_select_fusion
  14.0 63.0 %shard_map.158 = (bf16[8,16,1280]{2,1,0:T(8,128)(2,1)}, bf16[16,16,640]{2,1,0:T(8,128)(2,1)}) custom-call(s32[8]{0:T(128)} %get-tuple-element.26.val_rows, s32[8]{0:T(128)} %get-tuple-element.21.cond_rows, s32[10240]{0:T(1024)} %get-tuple-element.17.where_row, bf16[8,524288]{1,0:T(8,128)(2,1)} %val_ref.3, bf16[8,524288]{1,0:T(8,128)(2,1)} %cond_ref.3, ...), custom_call_target="tpu_custom_call" | custom-call | tf_op jit(solution)/shard_map/pallas_call | solution.py:234
  77.0 15.5 %all_to_all.20 = bf16[16,16,640]{2,1,0:T(8,128)(2,1)} all-to-all(bf16[16,16,640]{2,1,0:T(8,128)(2,1)} %get-tuple-element.7), channel_id=1, replica_groups=mesh['row'=8,'col'=16] {'col'}, dimensions={0} | all-to-all | bytes 655360 | tf_op jit(solution)/shard_map/all_to_all | solution.py:294
  92.8 0.7 broadcast_in_dim_tile.7.scale_ref
  93.5 63.2 %shard_map.159 = (bf16[8,16,1280]{2,1,0:T(8,128)(2,1)}, bf16[16,16,640]{2,1,0:T(8,128)(2,1)}) custom-call(s32[8]{0:T(128)} %get-tuple-element.27.val_rows, s32[8]{0:T(128)} %get-tuple-element.20.cond_rows, s32[10240]{0:T(1024)} %get-tuple-element.17.where_row, bf16[8,524288]{1,0:T(8,128)(2,1)} %val_ref.3, bf16[8,524288]{1,0:T(8,128)(2,1)} %cond_ref.3, ...), custom_call_target="tpu_custom_call" | custom-call | tf_op jit(solution)/shard_map/pallas_call | solution.py:234
  156.7 12.9 %all_to_all.21 = bf16[16,16,640]{2,1,0:T(8,128)(2,1)} all-to-all(bf16[16,16,640]{2,1,0:T(8,128)(2,1)} %get-tuple-element.9), channel_id=1, replica_groups=mesh['row'=8,'col'=16] {'col'}, dimensions={0} | all-to-all | bytes 655360 | tf_op jit(solution)/shard_map/all_to_all | solution.py:294
  169.7 14.4 %all_to_all.22 = bf16[8,16,1280]{2,1,0:T(8,128)(2,1)} all-to-all(bf16[8,16,1280]{2,1,0:T(8,128)(2,1)S(1)} %copy-done.3), channel_id=1, replica_groups=mesh['row'=8,'col'=16] {'row'}, dimensions={0} | all-to-all | bytes 655360 | tf_op jit(solution)/shard_map/all_to_all | solution.py:293
  184.2 12.2 %all_to_all.23 = bf16[8,16,1280]{2,1,0:T(8,128)(2,1)} all-to-all(bf16[8,16,1280]{2,1,0:T(8,128)(2,1)} %get-tuple-element.8), channel_id=1, replica_groups=mesh['row'=8,'col'=16] {'row'}, dimensions={0} | all-to-all | bytes 655360 | tf_op jit(solution)/shard_map/all_to_all | solution.py:293
  196.4 2.2 neg.20
  199.0 1.4 copy-done
  200.9 1.8 copy.25
  202.8 25.5 %all-gather.11.cloned.1.call-done = bf16[128,16,640]{2,1,0:T(8,128)(2,1)} async-done(((bf16[16,16,640]{2,1,0:T(8,128)(2,1)}), bf16[128,16,640]{2,1,0:T(8,128)(2,1)}) %all-gather.11.cloned.1.call-update) | async-done | bytes 2621456 | tf_op jit(solution)/shard_map/all_gather | solution.py:296
  228.3 2.2 neg.22
  230.5 1.9 copy.24
  232.4 0.8 copy-done.1
  233.7 1.9 copy.26
  235.6 32.6 %all-gather.5.cloned.1.call-done = bf16[128,16,1280]{2,1,0:T(8,128)(2,1)} async-done(((bf16[8,16,1280]{2,1,0:T(8,128)(2,1)}), bf16[128,16,1280]{2,1,0:T(8,128)(2,1)}) %all-gather.5.cloned.1.call-update) | async-done | bytes 5242896 | tf_op jit(solution)/shard_map/all_gather | solution.py:295
  268.1 9.4 %fusion.20 = f32[1280,640]{1,0:T(8,128)} fusion(bf16[2048,1280]{1,0:T(8,128)(2,1)} %bitcast.34, bf16[2048,640]{1,0:T(8,128)(2,1)} %bitcast.28), kind=kOutput, calls=%fused_computation.63 | convolution fusion | flops 3355443200 | bytes 11141120 | tf_op jit(solution)/shard_map/dot_general | solution.py:306
  277.5 6.1 %fusion.19 = f32[1280,640]{1,0:T(8,128)} fusion(bf16[2048,1280]{1,0:T(8,128)(2,1)S(1)} %bitcast.35, bf16[2048,640]{1,0:T(8,128)(2,1)S(1)} %bitcast.26), kind=kOutput, calls=%fused_computation.62 | convolution fusion | flops 3355443200 | bytes 11141120 | tf_op jit(solution)/shard_map/dot_general | solution.py:305
  283.6 25.5 %all-gather.9.cloned.1.call-done = bf16[128,16,1280]{2,1,0:T(8,128)(2,1)} async-done(((bf16[8,16,1280]{2,1,0:T(8,128)(2,1)}), bf16[128,16,1280]{2,1,0:T(8,128)(2,1)}) %all-gather.9.cloned.1.call-update) | async-done | bytes 5242896 | tf_op jit(solution)/shard_map/all_gather | solution.py:295
  309.2 10.6 %convolution_add_fusion.1 = f32[1280,640]{1,0:T(8,128)} fusion(f32[1280,640]{1,0:T(8,128)} %fusion.19, bf16[2048,1280]{1,0:T(8,128)(2,1)} %bitcast.36, bf16[2048,640]{1,0:T(8,128)(2,1)} %bitcast.27), kind=kOutput, calls=%fused_computation.1 | convolution fusion | flops 3356262400 | bytes 14417920 | tf_op jit(solution)/shard_map/dot_general | solution.py:305
  319.8 6.0 %convolution_add_fusion = f32[1280,640]{1,0:T(8,128)} fusion(f32[1280,640]{1,0:T(8,128)S(1)} %copy-done.6, bf16[2048,1280]{1,0:T(8,128)(2,1)S(1)} %bitcast.37, bf16[2048,640]{1,0:T(8,128)(2,1)S(1)} %bitcast.29), kind=kOutput, calls=%fused_computation | convolution fusion | flops 3356262400 | bytes 14417920 | tf_op jit(solution)/shard_map/dot_general | solution.py:306
  (38 shorter events, 4.7 us)
Async XLA Ops:
  7.2 189.3 %all-gather.7.cloned.1.call-start = ((), (), s32[]{:S(2)}) async-start(), calls=%async_computation.5 | async-start | bytes 2949120 | tf_op jit(solution)/shard_map/all_gather | solution.py:296
  92.6 135.7 %all-gather.11.cloned.1.call-start = ((), (), s32[]{:S(2)}) async-start(), calls=%async_computation.7 | async-start | bytes 2949120 | tf_op jit(solution)/shard_map/all_gather | solution.py:296
  93.5 76.2 %copy-start.3 = (bf16[8,16,1280]{2,1,0:T(8,128)(2,1)S(1)}, bf16[8,16,1280]{2,1,0:T(8,128)(2,1)}, u32[]{:S(2)}) copy-start(bf16[8,16,1280]{2,1,0:T(8,128)(2,1)} %get-tuple-element.6) | copy-start | bytes 983044
  169.7 98.5 %all-gather.5.cloned.1.call-start = ((), (), s32[]{:S(2)}) async-start(), calls=%async_computation.4 | async-start | bytes 5570560 | tf_op jit(solution)/shard_map/all_gather | solution.py:295
  184.2 125.0 %all-gather.9.cloned.1.call-start = ((), (), s32[]{:S(2)}) async-start(), calls=%async_computation.6 | async-start | bytes 5570560 | tf_op jit(solution)/shard_map/all_gather | solution.py:295
  198.7 1.7 copy-start
  230.5 2.7 copy-start.1
  268.1 9.4 %copy-start.4 = (bf16[128,16,1280]{2,1,0:T(8,128)(2,1)S(1)}, bf16[128,16,1280]{2,1,0:T(8,128)(2,1)}, u32[]{:S(2)}) copy-start(bf16[128,16,1280]{2,1,0:T(8,128)(2,1)} %all-gather.5.cloned.1.call-done) | copy-start | bytes 15728644
  309.2 10.6 %copy-start.2 = (bf16[16,8,2,8,640]{4,3,2,1,0:T(8,128)(2,1)S(1)}, bf16[16,8,2,8,640]{4,3,2,1,0:T(8,128)(2,1)}, u32[]{:S(2)}) copy-start(bf16[16,8,2,8,640]{4,3,2,1,0:T(8,128)(2,1)} %copy.26) | copy-start | bytes 7864324
  309.2 10.6 %copy-start.5 = (bf16[128,16,1280]{2,1,0:T(8,128)(2,1)S(1)}, bf16[128,16,1280]{2,1,0:T(8,128)(2,1)}, u32[]{:S(2)}) copy-start(bf16[128,16,1280]{2,1,0:T(8,128)(2,1)} %all-gather.9.cloned.1.call-done) | copy-start | bytes 15728644
  309.2 10.6 %copy-start.6 = (f32[1280,640]{1,0:T(8,128)S(1)}, f32[1280,640]{1,0:T(8,128)}, u32[]{:S(2)}) copy-start(f32[1280,640]{1,0:T(8,128)} %fusion.20) | copy-start | bytes 9830404
Sparse Core Ops, SparseCore 0:
  92.7 57.3 all-gather.6
  169.8 58.4 all-gather.10
  230.0 38.0 all-gather.4
  269.7 39.4 all-gather.8

commit v2 on v1

v2 whole, which is shorter than its diff:
```python
import functools
import math

import jax
import jax.numpy as jnp
import ml_dtypes
import numpy as np
from jax import lax
from jax.experimental import pallas as pl
from jax.experimental.pallas import tpu as pltpu
from jax.sharding import PartitionSpec as P

GX, GY, GZ = 64, 64, 128
HX, HZ = 16, 32
BANDS = 8
GROUP = 8
GROUPS = 2
PAIR_DEV = GROUP * GROUPS
NKY = HX + 1
ROWS1 = 40
KXP = 40
OCTS = KXP // 8
KZP = 40
SLOTS = NKY * OCTS
XCH = 8
STEPS = GX // XCH
SPAN = XCH * GY + 8
LANES = 128


def split_table(table):
    hi = table.astype(ml_dtypes.bfloat16)
    lo = (table - hi.astype(np.float64)).astype(ml_dtypes.bfloat16)
    return hi, lo


def tables():
    ky = np.arange(NKY)
    ang = 2.0 * np.pi * ((ky[:, None] * np.arange(GY)[None, :]) % GY) / GY
    first = np.zeros((ROWS1, GY))
    first[:NKY] = np.cos(ang)
    first[NKY : 2 * NKY] = -np.sin(ang)
    hi, lo = split_table(first)
    t1 = np.concatenate(
        [np.concatenate([hi, hi], 1), np.concatenate([lo, np.zeros_like(lo)], 1)], 0
    )
    kx = np.arange(2 * HX + 1) - HX
    ang = 2.0 * np.pi * ((kx[:, None] * np.arange(GX)[None, :]) % GX) / GX
    second = np.zeros((2 * KXP, 2 * GX))
    second[: 2 * HX + 1] = np.concatenate([np.cos(ang), np.sin(ang)], 1)
    second[KXP : KXP + 2 * HX + 1] = np.concatenate([-np.sin(ang), np.cos(ang)], 1)
    hi, lo = split_table(second)
    t2 = np.concatenate(
        [np.concatenate([hi, hi], 1), np.concatenate([lo, np.zeros_like(lo)], 1)], 0
    )
    kz = np.arange(HZ + 1)
    ang = 2.0 * np.pi * ((kz[:, None] * np.arange(GZ)[None, :]) % GZ) / GZ
    third = np.zeros((2 * KZP, GZ))
    third[: HZ + 1] = np.cos(ang)
    third[KZP : KZP + HZ + 1] = np.sin(ang)
    hi, lo = split_table(third)
    t3 = np.concatenate(
        [np.concatenate([hi, hi], 1), np.concatenate([lo, np.zeros_like(lo)], 1)], 0
    )
    perm = np.zeros((LANES, LANES))
    for sub in range(8):
        for rp in range(2 * GROUP):
            perm[sub * 2 * GROUP + rp, rp * 8 + sub] = 1.0
    return t1, t2, t3, perm.astype(ml_dtypes.bfloat16)


def split_value(value):
    hi = value.astype(jnp.bfloat16)
    lo = (value - hi.astype(jnp.float32)).astype(jnp.bfloat16)
    return hi, lo


NN = (((1,), (0,)), ((), ()))
NT = (((1,), (1,)), ((), ()))


def mm(a, b, dims):
    return lax.dot_general(a, b, dims, preferred_element_type=jnp.float32)


def elements_kernel(
    row_blocks,
    col_blocks,
    num_gvec,
    val_rows,
    cond_rows,
    where_row,
    val_ref,
    cond_ref,
    t1_ref,
    t2_ref,
    t3_ref,
    perm_ref,
    scale_ref,
    sub_ref,
    sign_ref,
    rows_ref,
    cols_ref,
    uval,
    ucond,
    first,
    second,
    spectrum,
    picked,
):
    step = pl.program_id(0)

    def unpack(i, carry):
        for j in range(16):
            at = i * 16 + j
            columns = pl.ds(pl.multiple_of(at * LANES, LANES), LANES)
            rows = pl.ds(at, BANDS, stride=SPAN)
            uval[rows, :] = val_ref[:, columns].astype(jnp.float32)
            ucond[rows, :] = cond_ref[:, columns].astype(jnp.float32)
        return carry

    lax.fori_loop(0, XCH * GY // 16, unpack, 0)

    def pair_first(p, carry):
        vb = val_rows[p]
        cb = cond_rows[p]
        for half in range(XCH // 2):
            parts = []
            for x in (2 * half, 2 * half + 1):
                base = x * GY
                density = (
                    uval[pl.ds(pl.multiple_of(vb * SPAN + base, 8), GY), :]
                    * ucond[pl.ds(pl.multiple_of(cb * SPAN + base, 8), GY), :]
                )
                hi, lo = split_value(density)
                parts.append(jnp.concatenate([hi, lo], axis=0))
            out = mm(t1_ref[...], jnp.concatenate(parts, axis=1), NN)
            out = out[:ROWS1] + out[ROWS1:]
            for k in range(2):
                at = (p * GX + step * XCH + 2 * half + k) * ROWS1
                first[pl.ds(pl.multiple_of(at, 8), ROWS1), :] = out[:, k * LANES : (k + 1) * LANES]
        return carry

    lax.fori_loop(0, PAIR_DEV, pair_first, 0, unroll=2)

    @pl.when(step == STEPS - 1)
    def _():
        def second_stage(ky, carry):
            for duo in range(PAIR_DEV // 2):
                parts = []
                for p in (2 * duo, 2 * duo + 1):
                    base = p * GX * ROWS1
                    real = first[pl.ds(base + ky, GX, stride=ROWS1), :]
                    imag = first[pl.ds(base + NKY + ky, GX, stride=ROWS1), :]
                    rhi, rlo = split_value(real)
                    ihi, ilo = split_value(imag)
                    parts.append(jnp.concatenate([rhi, ihi, rlo, ilo], axis=0))
                out = mm(t2_ref[...], jnp.concatenate(parts, axis=1), NN)
                out = out[: 2 * KXP] + out[2 * KXP :]
                for k in range(2):
                    for o in range(OCTS):
                        for ri in range(2):
                            group, p = divmod(2 * duo + k, GROUP)
                            at = (ky * OCTS + o) * GROUPS + group
                            at = at * LANES + (ri * GROUP + p) * 8
                            second[pl.ds(pl.multiple_of(at, 8), 8), :] = out[
                                ri * KXP + o * 8 : ri * KXP + o * 8 + 8,
                                k * LANES : (k + 1) * LANES,
                            ]
            return carry

        lax.fori_loop(0, NKY, second_stage, 0)

        lane = lax.broadcasted_iota(jnp.int32, (1, GROUPS * LANES), 1) % LANES
        scale = scale_ref[...]
        swapped = jnp.where(lane < LANES // 2, scale, -scale)

        def third_stage(b, carry):
            value = second[pl.ds(pl.multiple_of(b * 2 * LANES, 2 * LANES), 2 * LANES), :]
            hi, lo = split_value(value)
            out = mm(t3_ref[...], jnp.concatenate([hi, lo], axis=1), NT)
            out = out[: 2 * KZP] + out[2 * KZP :]
            cos_part = out[:KZP] * scale
            sin_part = jnp.concatenate(
                [
                    pltpu.roll(out[KZP:, k * LANES : (k + 1) * LANES], LANES // 2, 1)
                    for k in range(GROUPS)
                ],
                axis=1,
            )
            sin_part = sin_part * swapped
            at = b * 2 * KZP
            plus = cos_part + sin_part
            minus = cos_part - sin_part
            for k in range(GROUPS):
                part = slice(k * LANES, (k + 1) * LANES)
                spectrum[k, pl.ds(pl.multiple_of(at, 8), KZP), :] = plus[:, part]
                spectrum[k, pl.ds(pl.multiple_of(at + KZP, 8), KZP), :] = minus[:, part]
            return carry

        lax.fori_loop(0, SLOTS, third_stage, 0, unroll=5)

        block = num_gvec // col_blocks
        per_row = col_blocks // row_blocks

        for b in range(col_blocks):

            def pick(i, carry):
                for j in range(64):
                    at = i * 64 + j
                    row = where_row[b * block + at]
                    for k in range(GROUPS):
                        picked[k, pl.ds(at, 1), :] = spectrum[k, pl.ds(row, 1), :]
                return carry

            lax.fori_loop(0, block // 64, pick, 0)
            sub = sub_ref[:, b * block : (b + 1) * block]
            sign = sign_ref[:, b * block : (b + 1) * block]
            real, imag = [], []
            for k in range(GROUPS):
                part = picked[k].astype(jnp.bfloat16)
                turned = mm(perm_ref[...], part, NT)
                total = turned[: 2 * GROUP]
                for s in range(1, 8):
                    total = jnp.where(sub == s, turned[s * 2 * GROUP : (s + 1) * 2 * GROUP], total)
                real.append(total[:GROUP])
                imag.append(total[GROUP:] * sign)
            total = jnp.concatenate(real + imag, axis=0).astype(jnp.bfloat16)
            cols_ref[b] = total
            rows_ref[b // per_row, :, (b % per_row) * block : (b % per_row + 1) * block] = total


def pair_elements(val_rows, cond_rows, scale, val, cond, gvec, row_blocks, col_blocks):
    num_gvec = gvec.shape[0]
    kx = gvec // (GY * GZ)
    ky = gvec // GZ % GY
    kz = gvec % GZ
    kx = jnp.where(kx < GX // 2, kx, kx - GX)
    ky = jnp.where(ky < GY // 2, ky, ky - GY)
    kz = jnp.where(kz < GZ // 2, kz, kz - GZ)
    flip = jnp.where(ky < 0, -1, 1)
    kx, ky, kz = kx * flip + HX, ky * flip, kz * flip
    where_row = (ky * OCTS + kx // 8) * 2 * KZP + jnp.where(kz < 0, KZP - kz, kz)
    sub = (kx % 8)[None, :]
    sign = flip.astype(jnp.float32)[None, :]
    lanes = jnp.repeat(scale, 8).reshape(GROUPS, 1, -1)
    lanes = jnp.tile(lanes, (1, 2, 1)).reshape(1, -1)
    t1, t2, t3, perm = tables()
    whole = lambda shape: pl.BlockSpec(shape, lambda i, *_: (0,) * len(shape))
    width = XCH * GY * GZ
    outs = [
        jax.ShapeDtypeStruct((row_blocks, 2 * PAIR_DEV, num_gvec // row_blocks), jnp.bfloat16),
        jax.ShapeDtypeStruct((col_blocks, 2 * PAIR_DEV, num_gvec // col_blocks), jnp.bfloat16),
    ]
    return pl.pallas_call(
        functools.partial(elements_kernel, row_blocks, col_blocks, num_gvec),
        out_shape=outs,
        grid_spec=pltpu.PrefetchScalarGridSpec(
            num_scalar_prefetch=3,
            grid=(STEPS,),
            in_specs=[
                pl.BlockSpec((BANDS, width), lambda i, *_: (0, i)),
                pl.BlockSpec((BANDS, width), lambda i, *_: (0, i)),
                whole(t1.shape),
                whole(t2.shape),
                whole(t3.shape),
                whole(perm.shape),
                whole((1, GROUPS * LANES)),
                whole((1, num_gvec)),
                whole((1, num_gvec)),
            ],
            out_specs=[whole(o.shape) for o in outs],
            scratch_shapes=[
                pltpu.VMEM((SPAN * BANDS, LANES), jnp.float32),
                pltpu.VMEM((SPAN * BANDS, LANES), jnp.float32),
                pltpu.VMEM((PAIR_DEV * GX * ROWS1, LANES), jnp.float32),
                pltpu.VMEM((SLOTS * GROUPS * LANES, LANES), jnp.float32),
                pltpu.VMEM((GROUPS, SLOTS * 2 * KZP, LANES), jnp.float32),
                pltpu.VMEM((GROUPS, num_gvec // col_blocks, LANES), jnp.float32),
            ],
        ),
        compiler_params=pltpu.CompilerParams(vmem_limit_bytes=60 * 1024 * 1024),
    )(val_rows, cond_rows, where_row, val, cond, t1, t2, t3, perm, lanes, sub, sign)


def product_kernel(chunk_row, chunk_col, *refs):
    lefts = refs[: len(LEFT)]
    rights = refs[len(LEFT) : len(LEFT) + len(RIGHT)]
    real_ref, imag_ref, table = refs[len(LEFT) + len(RIGHT) :]
    width = rights[0].shape[2]
    rows = 2 * PAIR_DEV

    @pl.when(pl.program_id(0) == 0)
    def _():
        def fill(i, carry):
            for k, right in enumerate(rights):
                value = right[chunk_col[i]]
                at = (i * len(RIGHT) + chunk_row[k]) * rows
                first = pl.ds(pl.multiple_of(at, rows), PAIR_DEV)
                last = pl.ds(pl.multiple_of(at + PAIR_DEV, PAIR_DEV), PAIR_DEV)
                table[first, :width] = -value[:PAIR_DEV]
                table[last, :width] = -value[PAIR_DEV:]
                table[first, width:] = value[PAIR_DEV:]
                table[last, width:] = -value[:PAIR_DEV]
            return carry

        lax.fori_loop(0, len(LEFT), fill, 0)

    left = jnp.concatenate([ref[...].reshape(-1, ref.shape[2]) for ref in lefts], axis=0)
    out = mm(left, table[...], (((0,), (0,)), ((), ())))
    real_ref[...] = out[:, :width]
    imag_ref[...] = out[:, width:]


HALF = [(0, 0), (0, 1), (-1, 0), (1, 0), (-1, 1), (1, 1), (2, 0), (2, 1)]
LEFT = [(dz, dx, core) for core in range(2) for dz, dx in HALF]
RIGHT = [(dx, dy) for dy, dx in HALF]
TILE = 256


def panel_product(lefts, rights):
    row, col = lax.axis_index("row"), lax.axis_index("col")
    chunk_col = jnp.stack(
        [(col // 4 + dz) % 4 * 4 + (col // 2 % 2 ^ dx) * 2 + (col % 2 ^ dc) for dz, dx, dc in LEFT]
    )
    chunk_row = jnp.stack([(row // 4 ^ dx) * 4 + (row % 4 + dy) % 4 for dx, dy in RIGHT])
    sources, rows, height = lefts[0].shape
    width = rights[0].shape[2]
    depth = len(lefts) * sources * rows
    out = jax.ShapeDtypeStruct((height, width), jnp.float32)
    return pl.pallas_call(
        product_kernel,
        out_shape=[out, out],
        grid_spec=pltpu.PrefetchScalarGridSpec(
            num_scalar_prefetch=2,
            grid=(height // TILE,),
            in_specs=[pl.BlockSpec((sources, rows, TILE), lambda m, *_: (0, 0, m))] * len(lefts)
            + [pl.BlockSpec(rights[0].shape, lambda m, *_: (0, 0, 0))] * len(rights),
            out_specs=[pl.BlockSpec((TILE, width), lambda m, *_: (m, 0))] * 2,
            scratch_shapes=[pltpu.VMEM((depth, 2 * width), jnp.bfloat16)],
        ),
        compiler_params=pltpu.CompilerParams(vmem_limit_bytes=60 * 1024 * 1024),
    )(chunk_row, chunk_col, *lefts, *rights)


def ring_chunks(own, axis, ring, swap):
    send = lambda value, perm: lax.ppermute(value, axis, perm)
    near = (send(own, ring(1)), send(own, ring(-1)))
    other = send(own, swap)
    far = (send(other, ring(1)), send(other, ring(-1)))
    ends = (send(near[0], ring(1)), send(far[1], ring(-1)))
    return [own, other, *near, *far, *ends]


def ring_z(step):
    return [(c, (c // 4 + step) % 4 * 4 + c % 4) for c in range(16)]


def ring_y(step):
    return [(r, r // 4 * 4 + (r + step) % 4) for r in range(8)]


def pick_values(indices, values):
    match = indices[:, None] == jnp.arange(values.shape[0], dtype=jnp.int32)[None, :]
    return jnp.sum(jnp.where(match, values[None, :], 0.0), axis=1)


def local(val_band, cond_band, val_orbitals, cond_orbitals, val_energy, cond_energy, gvec_index):
    row_count = lax.axis_size("row")
    col_count = lax.axis_size("col")
    pair_dev = val_band.shape[0]
    pairs_all = pair_dev * row_count * col_count
    energy_gap = pick_values(cond_band, cond_energy) - pick_values(val_band, val_energy)
    factor = 4.0 / (math.sqrt(pairs_all) * energy_gap)
    scale = jnp.sqrt(factor) / math.sqrt(GX * GY * GZ)
    val_rows = val_band % val_orbitals.shape[0]
    cond_rows = cond_band % cond_orbitals.shape[0]
    rows_part, cols_part = pair_elements(
        val_rows, cond_rows, scale, val_orbitals, cond_orbitals, gvec_index, row_count, col_count
    )
    rows_recv = lax.all_to_all(rows_part, "row", split_axis=0, concat_axis=0, tiled=True)
    cols_part, rows_recv = lax.optimization_barrier((cols_part, rows_recv))
    lefts = ring_chunks(rows_recv, "col", ring_z, [(c, c ^ 2) for c in range(16)])
    cols_recv = lax.all_to_all(cols_part, "col", split_axis=0, concat_axis=0, tiled=True)
    rights = ring_chunks(cols_recv, "row", ring_y, [(r, r ^ 4) for r in range(8)])
    lefts += [lax.ppermute(left, "col", [(c, c ^ 1) for c in range(16)]) for left in lefts]
    real, imag = panel_product(lefts, rights)
    return (real, imag)


def solution(mesh):
    return jax.shard_map(
        local,
        mesh=mesh,
        in_specs=(
            P(("row", "col")),
            P(("row", "col")),
            P(("row", "col"), None),
            P(("row", "col"), None),
            P(),
            P(),
            P(),
        ),
        out_specs=(P("row", "col"), P("row", "col")),
        check_vma=False,
    )
```

time: 333 us -> 205 us (0.62)
  Pallas kernels: 126 us -> 82.7 us
  blocking collectives: 55.1 us -> 18.7 us
  starting transfers between devices: 0.16 us -> 35 us
  matrix products: 32.1 us -> 0 us
  waiting for transfers between devices: 83.7 us -> 58.7 us
  between operations: 13.9 us -> 0.89 us
  local copies, waits for them, and re-layouts: 10.5 us -> 2.28 us
  other arithmetic: 10.7 us -> 5.18 us
    all_gather x4 -> x0, waiting for transfers between devices: 83.6 us -> none  [the longest x2 58.1 us: local(): left.append(lax.all_gather(rows_recv, 'col', axis=0, tiled=True))]
    pallas_call x2 -> x1, Pallas kernels: 126 us -> 61.9 us  [pair_elements(): pl.pallas_call(functools.partial(elements_kernel, row_blocks, col_blocks,...]
    ppermute x0 -> x22, waiting for transfers between devices: none -> 43.7 us  [the longest x14 43.7 us: ring_chunks(): send = lambda value, perm: lax.ppermute(value, axis, perm)]
    dot_general x4 -> x0, matrix products: 32.1 us -> none  [the longest x2 16.7 us: local(): lax.dot_general(lhs, rhs, dims, preferred_element_type=jnp.float32)]
    ppermute x0 -> x22, starting transfers between devices: none -> 31.3 us  [the longest x14 21.4 us: ring_chunks(): send = lambda value, perm: lax.ppermute(value, axis, perm)]
    all_to_all x2 -> x0, blocking collectives: 28.5 us -> none  [local(): lax.all_to_all(cols_part, 'col', split_axis=0, concat_axis=0, tiled=True)]
    pallas_call x0 -> x1, Pallas kernels: none -> 20.8 us  [panel_product(): pl.pallas_call(product_kernel, out_shape=[out, out], grid_spec=pltpu.Pref...]
    all_to_all x0 -> x1, waiting for transfers between devices: none -> 15 us  [local(): lax.all_to_all(cols_part, 'col', split_axis=0, concat_axis=0, tiled=True)]
  transfers between devices with their start and end apart: 4 -> 23, of which waited for: 3 -> 8; matrix products, arithmetic and copies ran while one was open for 8% -> 1% of each run, Pallas kernels for 19% -> 0%
where the time goes in v2:
time: 205 us; the launch traced here: 203 us
  Pallas kernels  82.7 us (40%)
  waiting for transfers between devices  58.7 us (29%)
  starting transfers between devices  35 us (17%)
  blocking collectives  18.7 us (9%)
  other arithmetic  5.18 us (3%)
  local copies, waits for them, and re-layouts  2.28 us (1%)
    pallas_call x1, Pallas kernels, pair_elements(): pl.pallas_call(functools.partial(elements_kernel, row_blocks, col_blocks,...  61.9 us
    ppermute x14, waiting for transfers between devices, ring_chunks(): send = lambda value, perm: lax.ppermute(value, axis, perm)  43.7 us
    ppermute x14, starting transfers between devices, ring_chunks(): send = lambda value, perm: lax.ppermute(value, axis, perm)  21.4 us
    pallas_call x1, Pallas kernels, panel_product(): pl.pallas_call(product_kernel, out_shape=[out, out], grid_spec=pltpu.Pref...  20.8 us
    all_to_all x1, blocking collectives, local(): lax.all_to_all(rows_part, 'row', split_axis=0, concat_axis=0, tiled=True)  18.7 us
    all_to_all x1, waiting for transfers between devices, local(): lax.all_to_all(cols_part, 'col', split_axis=0, concat_axis=0, tiled=True)  15 us
    ppermute x8, starting transfers between devices, local(): lax.ppermute(left, 'col', [(c, c ^ 1) for c in range(16)])  9.89 us
  transfers between devices with their start and end apart: 23, of which 8 were waited for; matrix products, arithmetic and copies ran while one was open for 1% of the time, Pallas kernels for 0%

profile of v2, /device:TPU:1, one launch (start us, length us, event | category | flops | bytes accessed | tf_op | source)
XLA Modules:
  0.0 203.4 jit_solution(1096137328803806334)
XLA Ops:
  3.7 1.4 select_convert_fusion
  5.2 1.5 add_select_fusion
  6.7 61.9 %shard_map.122 = (bf16[8,32,1280]{2,1,0:T(8,128)(2,1)}, bf16[16,32,640]{2,1,0:T(8,128)(2,1)}) custom-call(s32[16]{0:T(128)} %get-tuple-element.17.val_rows, s32[16]{0:T(128)} %get-tuple-element.16.cond_rows, s32[10240]{0:T(1024)} %get-tuple-element.13.where_row, bf16[8,524288]{1,0:T(8,128)(2,1)} %val_ref.1, bf16[8,524288]{1,0:T(8,128)(2,1)} %cond_ref.1, ...), custom_call_target="tpu_custom_call" | custom-call | tf_op jit(solution)/shard_map/pallas_call | solution.py:255
  68.6 18.7 %all_to_all.10.refs_0_ = bf16[8,32,1280]{2,1,0:T(8,128)(2,1)S(1)} all-to-all(bf16[8,32,1280]{2,1,0:T(8,128)(2,1)} %get-tuple-element.7), channel_id=1, replica_groups=mesh['row'=8,'col'=16] {'row'}, dimensions={0} | all-to-all | bytes 1310720 | tf_op jit(solution)/shard_map/all_to_all | solution.py:381
  87.3 2.6 %collective-permute-start.7 = (bf16[8,32,1280]{2,1,0:T(8,128)(2,1)S(1)}, bf16[8,32,1280]{2,1,0:T(8,128)(2,1)S(1)}, u32[]{:S(2)}, u32[]{:S(2)}) collective-permute-start(bf16[8,32,1280]{2,1,0:T(8,128)(2,1)S(1)} %all_to_all.10.refs_0_), channel_id=1, source_target_pairs={{0,1},{1,0},{2,3},{3,2},{4,5},{5,4},{6,7},{7,6},{8,9},{9,8},{10,11... | collective-permute-start | bytes 1966088 | tf_op jit(solution)/shard_map/ppermute | solution.py:386
  89.9 3.9 %collective-permute-start.2 = (bf16[8,32,1280]{2,1,0:T(8,128)(2,1)S(1)}, bf16[8,32,1280]{2,1,0:T(8,128)(2,1)S(1)}, u32[]{:S(2)}, u32[]{:S(2)}) collective-permute-start(bf16[8,32,1280]{2,1,0:T(8,128)(2,1)S(1)} %all_to_all.10.refs_0_), channel_id=1, source_target_pairs={{0,12},{1,13},{2,14},{3,15},{4,0},{5,1},{6,2},{7,3},{8,4},{9,5},{1... | collective-permute-start | bytes 1966088 | tf_op jit(solution)/shard_map/ppermute | solution.py:347
  93.8 3.7 %all-to-all-start.1 = ((bf16[16,32,640]{2,1,0:T(8,128)(2,1)}), bf16[16,32,640]{2,1,0:T(8,128)(2,1)S(1)}, u32[]{:S(2)}, u32[]{:S(2)}) async-start(bf16[16,32,640]{2,1,0:T(8,128)(2,1)} %get-tuple-element.9), calls=%async_computation.1 | async-start | bytes 1310720 | tf_op jit(solution)/shard_map/all_to_all | solution.py:384
  97.4 1.4 collective-permute-start.1
  100.0 15.0 %all-to-all-done.1.refs_16_ = bf16[16,32,640]{2,1,0:T(8,128)(2,1)S(1)} async-done(((bf16[16,32,640]{2,1,0:T(8,128)(2,1)}), bf16[16,32,640]{2,1,0:T(8,128)(2,1)S(1)}, u32[]{:S(2)}, u32[]{:S(2)}) %all-to-all-start.1) | async-done | bytes 655392 | tf_op jit(solution)/shard_map/all_to_all | solution.py:384
  116.9 5.2 %collective-permute-done.1.refs_2_ = bf16[8,32,1280]{2,1,0:T(8,128)(2,1)S(1)} collective-permute-done((bf16[8,32,1280]{2,1,0:T(8,128)(2,1)S(1)}, bf16[8,32,1280]{2,1,0:T(8,128)(2,1)S(1)}, u32[]{:S(2)}, u32[]{:S(2)}) %collective-permute-start.1) | collective-permute-done | bytes 655392 | tf_op jit(solution)/shard_map/ppermute | solution.py:347
  123.1 7.4 %collective-permute-done.17.refs_19_ = bf16[16,32,640]{2,1,0:T(8,128)(2,1)S(1)} collective-permute-done((bf16[16,32,640]{2,1,0:T(8,128)(2,1)S(1)}, bf16[16,32,640]{2,1,0:T(8,128)(2,1)S(1)}, u32[]{:S(2)}, u32[]{:S(2)}) %collective-permute-start.17) | collective-permute-done | bytes 655392 | tf_op jit(solution)/shard_map/ppermute | solution.py:347
  130.5 2.0 collective-permute-start.5
  132.5 1.7 collective-permute-start.8
  134.3 3.4 %collective-permute-start.4 = (bf16[8,32,1280]{2,1,0:T(8,128)(2,1)}, bf16[8,32,1280]{2,1,0:T(8,128)(2,1)}, u32[]{:S(2)}, u32[]{:S(2)}) collective-permute-start(bf16[8,32,1280]{2,1,0:T(8,128)(2,1)} %collective-permute-done.refs_1_), channel_id=1, source_target_pairs={{0,12},{1,13},{2,14},{3,15},{4,0},{5,1},{6,2},{7,3},{8,4},{9,5},{1... | collective-permute-start | bytes 1966088 | tf_op jit(solution)/shard_map/ppermute | solution.py:347
  137.8 10.8 %collective-permute-done.5.refs_6_ = bf16[8,32,1280]{2,1,0:T(8,128)(2,1)} collective-permute-done((bf16[8,32,1280]{2,1,0:T(8,128)(2,1)S(1)}, bf16[8,32,1280]{2,1,0:T(8,128)(2,1)}, u32[]{:S(2)}, u32[]{:S(2)}) %collective-permute-start.5) | collective-permute-done | bytes 655392 | tf_op jit(solution)/shard_map/ppermute | solution.py:347
  148.5 2.0 %collective-permute-start.19 = (bf16[16,32,640]{2,1,0:T(8,128)(2,1)S(1)}, bf16[16,32,640]{2,1,0:T(8,128)(2,1)}, u32[]{:S(2)}, u32[]{:S(2)}) collective-permute-start(bf16[16,32,640]{2,1,0:T(8,128)(2,1)S(1)} %collective-permute-done.15.refs_17_), channel_id=1, source_target_pairs={{0,48},{16,0},{32,16},{48,32},{64,112},{80,64},{96,80},{112,96},{1... | collective-permute-start | bytes 1966088 | tf_op jit(solution)/shard_map/ppermute | solution.py:347
  151.1 3.4 %collective-permute-start.6 = (bf16[8,32,1280]{2,1,0:T(8,128)(2,1)}, bf16[8,32,1280]{2,1,0:T(8,128)(2,1)}, u32[]{:S(2)}, u32[]{:S(2)}) collective-permute-start(bf16[8,32,1280]{2,1,0:T(8,128)(2,1)} %collective-permute-done.4.refs_5_), channel_id=1, source_target_pairs={{0,12},{1,13},{2,14},{3,15},{4,0},{5,1},{6,2},{7,3},{8,4},{9,5},{1... | collective-permute-start | bytes 1966088 | tf_op jit(solution)/shard_map/ppermute | solution.py:347
  154.5 8.1 %collective-permute-done.3.refs_4_ = bf16[8,32,1280]{2,1,0:T(8,128)(2,1)} collective-permute-done((bf16[8,32,1280]{2,1,0:T(8,128)(2,1)}, bf16[8,32,1280]{2,1,0:T(8,128)(2,1)}, u32[]{:S(2)}, u32[]{:S(2)}) %collective-permute-start.3) | collective-permute-done | bytes 655392 | tf_op jit(solution)/shard_map/ppermute | solution.py:347
  162.6 1.7 collective-permute-start.12
  164.4 1.4 collective-permute-start.11
  167.0 2.1 %collective-permute-start.21 = (bf16[16,32,640]{2,1,0:T(8,128)(2,1)}, bf16[16,32,640]{2,1,0:T(8,128)(2,1)}, u32[]{:S(2)}, u32[]{:S(2)}) collective-permute-start(bf16[16,32,640]{2,1,0:T(8,128)(2,1)} %collective-permute-done.19.refs_21_), channel_id=1, source_target_pairs={{0,48},{16,0},{32,16},{48,32},{64,112},{80,64},{96,80},{112,96},{1... | collective-permute-start | bytes 1966088 | tf_op jit(solution)/shard_map/ppermute | solution.py:347
  169.1 1.4 collective-permute-start.14
  171.9 10.6 %collective-permute-done.21.refs_23_ = bf16[16,32,640]{2,1,0:T(8,128)(2,1)} collective-permute-done((bf16[16,32,640]{2,1,0:T(8,128)(2,1)}, bf16[16,32,640]{2,1,0:T(8,128)(2,1)}, u32[]{:S(2)}, u32[]{:S(2)}) %collective-permute-start.21) | collective-permute-done | bytes 655392 | tf_op jit(solution)/shard_map/ppermute | solution.py:347
  182.5 20.8 %shard_map.123 = (f32[1280,640]{1,0:T(8,128)}, f32[1280,640]{1,0:T(8,128)}) custom-call(s32[8]{0:T(128)} %stack.86.chunk_row, s32[16]{0:T(128)} %stack.103.chunk_col, bf16[8,32,1280]{2,1,0:T(8,128)(2,1)} %copy-done, bf16[8,32,1280]{2,1,0:T(8,128)(2,1)} %collective-permute-done.refs_1_, bf16[8,32,1280]{2,1,0:T(8,128)(2,1)} %copy-done.4, ...), custom_call_target="tpu_custom_call" | custom-call | tf_op jit(solution)/shard_map/pallas_call | solution.py:331
  (63 shorter events, 10.4 us)
Async XLA Ops:
  87.3 95.2 %copy-start = (bf16[8,32,1280]{2,1,0:T(8,128)(2,1)}, bf16[8,32,1280]{2,1,0:T(8,128)(2,1)S(1)}, u32[]{:S(2)}) copy-start(bf16[8,32,1280]{2,1,0:T(8,128)(2,1)S(1)} %all_to_all.10.refs_0_) | copy-start | bytes 1966084
  87.3 28.6 %collective-permute-start.7 = (bf16[8,32,1280]{2,1,0:T(8,128)(2,1)S(1)}, bf16[8,32,1280]{2,1,0:T(8,128)(2,1)S(1)}, u32[]{:S(2)}, u32[]{:S(2)}) collective-permute-start(bf16[8,32,1280]{2,1,0:T(8,128)(2,1)S(1)} %all_to_all.10.refs_0_), channel_id=1, source_target_pairs={{0,1},{1,0},{2,3},{3,2},{4,5},{5,4},{6,7},{7,6},{8,9},{9,8},{10,11... | collective-permute-start | bytes 1966088 | tf_op jit(solution)/shard_map/ppermute | solution.py:386
  89.9 26.7 %collective-permute-start.2 = (bf16[8,32,1280]{2,1,0:T(8,128)(2,1)S(1)}, bf16[8,32,1280]{2,1,0:T(8,128)(2,1)S(1)}, u32[]{:S(2)}, u32[]{:S(2)}) collective-permute-start(bf16[8,32,1280]{2,1,0:T(8,128)(2,1)S(1)} %all_to_all.10.refs_0_), channel_id=1, source_target_pairs={{0,12},{1,13},{2,14},{3,15},{4,0},{5,1},{6,2},{7,3},{8,4},{9,5},{1... | collective-permute-start | bytes 1966088 | tf_op jit(solution)/shard_map/ppermute | solution.py:347
  93.8 21.3 %all-to-all-start.1 = ((bf16[16,32,640]{2,1,0:T(8,128)(2,1)}), bf16[16,32,640]{2,1,0:T(8,128)(2,1)S(1)}, u32[]{:S(2)}, u32[]{:S(2)}) async-start(bf16[16,32,640]{2,1,0:T(8,128)(2,1)} %get-tuple-element.9), calls=%async_computation.1 | async-start | bytes 1310720 | tf_op jit(solution)/shard_map/all_to_all | solution.py:384
  97.4 24.7 %collective-permute-start.1 = (bf16[8,32,1280]{2,1,0:T(8,128)(2,1)S(1)}, bf16[8,32,1280]{2,1,0:T(8,128)(2,1)S(1)}, u32[]{:S(2)}, u32[]{:S(2)}) collective-permute-start(bf16[8,32,1280]{2,1,0:T(8,128)(2,1)S(1)} %all_to_all.10.refs_0_), channel_id=1, source_target_pairs={{0,4},{1,5},{2,6},{3,7},{4,8},{5,9},{6,10},{7,11},{8,12},{9,13},{1... | collective-permute-start | bytes 1966088 | tf_op jit(solution)/shard_map/ppermute | solution.py:347
  98.8 24.2 %collective-permute-start = (bf16[8,32,1280]{2,1,0:T(8,128)(2,1)S(1)}, bf16[8,32,1280]{2,1,0:T(8,128)(2,1)}, u32[]{:S(2)}, u32[]{:S(2)}) collective-permute-start(bf16[8,32,1280]{2,1,0:T(8,128)(2,1)S(1)} %all_to_all.10.refs_0_), channel_id=1, source_target_pairs={{0,2},{1,3},{2,0},{3,1},{4,6},{5,7},{6,4},{7,5},{8,10},{9,11},{10,... | collective-permute-start | bytes 1966088 | tf_op jit(solution)/shard_map/ppermute | solution.py:347
  115.0 15.5 %collective-permute-start.17 = (bf16[16,32,640]{2,1,0:T(8,128)(2,1)S(1)}, bf16[16,32,640]{2,1,0:T(8,128)(2,1)S(1)}, u32[]{:S(2)}, u32[]{:S(2)}) collective-permute-start(bf16[16,32,640]{2,1,0:T(8,128)(2,1)S(1)} %all-to-all-done.1.refs_16_), channel_id=1, source_target_pairs={{0,48},{16,0},{32,16},{48,32},{64,112},{80,64},{96,80},{112,96},{1... | collective-permute-start | bytes 1966088 | tf_op jit(solution)/shard_map/ppermute | solution.py:347
  115.9 16.6 %collective-permute-start.16 = (bf16[16,32,640]{2,1,0:T(8,128)(2,1)S(1)}, bf16[16,32,640]{2,1,0:T(8,128)(2,1)S(1)}, u32[]{:S(2)}, u32[]{:S(2)}) collective-permute-start(bf16[16,32,640]{2,1,0:T(8,128)(2,1)S(1)} %all-to-all-done.1.refs_16_), channel_id=1, source_target_pairs={{0,16},{16,32},{32,48},{48,0},{64,80},{80,96},{96,112},{112,64},{1... | collective-permute-start | bytes 1966088 | tf_op jit(solution)/shard_map/ppermute | solution.py:347
  116.5 17.7 %collective-permute-start.15 = (bf16[16,32,640]{2,1,0:T(8,128)(2,1)S(1)}, bf16[16,32,640]{2,1,0:T(8,128)(2,1)S(1)}, u32[]{:S(2)}, u32[]{:S(2)}) collective-permute-start(bf16[16,32,640]{2,1,0:T(8,128)(2,1)S(1)} %all-to-all-done.1.refs_16_), channel_id=1, source_target_pairs={{0,64},{16,80},{32,96},{48,112},{64,0},{80,16},{96,32},{112,48},{1... | collective-permute-start | bytes 1966088 | tf_op jit(solution)/shard_map/ppermute | solution.py:347
  122.1 15.5 %collective-permute-start.10 = (bf16[8,32,1280]{2,1,0:T(8,128)(2,1)S(1)}, bf16[8,32,1280]{2,1,0:T(8,128)(2,1)S(1)}, u32[]{:S(2)}, u32[]{:S(2)}) collective-permute-start(bf16[8,32,1280]{2,1,0:T(8,128)(2,1)S(1)} %collective-permute-done.2.refs_3_), channel_id=1, source_target_pairs={{0,1},{1,0},{2,3},{3,2},{4,5},{5,4},{6,7},{7,6},{8,9},{9,8},{10,11... | collective-permute-start | bytes 1966088 | tf_op jit(solution)/shard_map/ppermute | solution.py:386
  123.0 14.7 %collective-permute-start.9 = (bf16[8,32,1280]{2,1,0:T(8,128)(2,1)S(1)}, bf16[8,32,1280]{2,1,0:T(8,128)(2,1)S(1)}, u32[]{:S(2)}, u32[]{:S(2)}) collective-permute-start(bf16[8,32,1280]{2,1,0:T(8,128)(2,1)S(1)} %collective-permute-done.1.refs_2_), channel_id=1, source_target_pairs={{0,1},{1,0},{2,3},{3,2},{4,5},{5,4},{6,7},{7,6},{8,9},{9,8},{10,11... | collective-permute-start | bytes 1966088 | tf_op jit(solution)/shard_map/ppermute | solution.py:386
  130.5 18.0 %collective-permute-start.5 = (bf16[8,32,1280]{2,1,0:T(8,128)(2,1)S(1)}, bf16[8,32,1280]{2,1,0:T(8,128)(2,1)}, u32[]{:S(2)}, u32[]{:S(2)}) collective-permute-start(bf16[8,32,1280]{2,1,0:T(8,128)(2,1)S(1)} %collective-permute-done.1.refs_2_), channel_id=1, source_target_pairs={{0,4},{1,5},{2,6},{3,7},{4,8},{5,9},{6,10},{7,11},{8,12},{9,13},{1... | collective-permute-start | bytes 1966088 | tf_op jit(solution)/shard_map/ppermute | solution.py:347
  132.5 18.1 %collective-permute-start.8 = (bf16[8,32,1280]{2,1,0:T(8,128)(2,1)}, bf16[8,32,1280]{2,1,0:T(8,128)(2,1)S(1)}, u32[]{:S(2)}, u32[]{:S(2)}) collective-permute-start(bf16[8,32,1280]{2,1,0:T(8,128)(2,1)} %collective-permute-done.refs_1_), channel_id=1, source_target_pairs={{0,1},{1,0},{2,3},{3,2},{4,5},{5,4},{6,7},{7,6},{8,9},{9,8},{10,11... | collective-permute-start | bytes 1966088 | tf_op jit(solution)/shard_map/ppermute | solution.py:386
  134.3 16.8 %collective-permute-start.4 = (bf16[8,32,1280]{2,1,0:T(8,128)(2,1)}, bf16[8,32,1280]{2,1,0:T(8,128)(2,1)}, u32[]{:S(2)}, u32[]{:S(2)}) collective-permute-start(bf16[8,32,1280]{2,1,0:T(8,128)(2,1)} %collective-permute-done.refs_1_), channel_id=1, source_target_pairs={{0,12},{1,13},{2,14},{3,15},{4,0},{5,1},{6,2},{7,3},{8,4},{9,5},{1... | collective-permute-start | bytes 1966088 | tf_op jit(solution)/shard_map/ppermute | solution.py:347
  137.7 24.9 %collective-permute-start.3 = (bf16[8,32,1280]{2,1,0:T(8,128)(2,1)}, bf16[8,32,1280]{2,1,0:T(8,128)(2,1)}, u32[]{:S(2)}, u32[]{:S(2)}) collective-permute-start(bf16[8,32,1280]{2,1,0:T(8,128)(2,1)} %collective-permute-done.refs_1_), channel_id=1, source_target_pairs={{0,4},{1,5},{2,6},{3,7},{4,8},{5,9},{6,10},{7,11},{8,12},{9,13},{1... | collective-permute-start | bytes 1966088 | tf_op jit(solution)/shard_map/ppermute | solution.py:347
  137.7 26.6 %collective-permute-start.20 = (bf16[16,32,640]{2,1,0:T(8,128)(2,1)S(1)}, bf16[16,32,640]{2,1,0:T(8,128)(2,1)S(1)}, u32[]{:S(2)}, u32[]{:S(2)}) collective-permute-start(bf16[16,32,640]{2,1,0:T(8,128)(2,1)S(1)} %collective-permute-done.16.refs_18_), channel_id=1, source_target_pairs={{0,16},{16,32},{32,48},{48,0},{64,80},{80,96},{96,112},{112,64},{1... | collective-permute-start | bytes 1966088 | tf_op jit(solution)/shard_map/ppermute | solution.py:347
  148.5 15.9 %collective-permute-start.19 = (bf16[16,32,640]{2,1,0:T(8,128)(2,1)S(1)}, bf16[16,32,640]{2,1,0:T(8,128)(2,1)}, u32[]{:S(2)}, u32[]{:S(2)}) collective-permute-start(bf16[16,32,640]{2,1,0:T(8,128)(2,1)S(1)} %collective-permute-done.15.refs_17_), channel_id=1, source_target_pairs={{0,48},{16,0},{32,16},{48,32},{64,112},{80,64},{96,80},{112,96},{1... | collective-permute-start | bytes 1966088 | tf_op jit(solution)/shard_map/ppermute | solution.py:347
  150.6 16.4 %collective-permute-start.18 = (bf16[16,32,640]{2,1,0:T(8,128)(2,1)S(1)}, bf16[16,32,640]{2,1,0:T(8,128)(2,1)S(1)}, u32[]{:S(2)}, u32[]{:S(2)}) collective-permute-start(bf16[16,32,640]{2,1,0:T(8,128)(2,1)S(1)} %collective-permute-done.15.refs_17_), channel_id=1, source_target_pairs={{0,16},{16,32},{32,48},{48,0},{64,80},{80,96},{96,112},{112,64},{1... | collective-permute-start | bytes 1966088 | tf_op jit(solution)/shard_map/ppermute | solution.py:347
  151.1 18.1 %collective-permute-start.6 = (bf16[8,32,1280]{2,1,0:T(8,128)(2,1)}, bf16[8,32,1280]{2,1,0:T(8,128)(2,1)}, u32[]{:S(2)}, u32[]{:S(2)}) collective-permute-start(bf16[8,32,1280]{2,1,0:T(8,128)(2,1)} %collective-permute-done.4.refs_5_), channel_id=1, source_target_pairs={{0,12},{1,13},{2,14},{3,15},{4,0},{5,1},{6,2},{7,3},{8,4},{9,5},{1... | collective-permute-start | bytes 1966088 | tf_op jit(solution)/shard_map/ppermute | solution.py:347
  162.6 9.3 %collective-permute-start.12 = (bf16[8,32,1280]{2,1,0:T(8,128)(2,1)}, bf16[8,32,1280]{2,1,0:T(8,128)(2,1)}, u32[]{:S(2)}, u32[]{:S(2)}) collective-permute-start(bf16[8,32,1280]{2,1,0:T(8,128)(2,1)} %collective-permute-done.4.refs_5_), channel_id=1, source_target_pairs={{0,1},{1,0},{2,3},{3,2},{4,5},{5,4},{6,7},{7,6},{8,9},{9,8},{10,11... | collective-permute-start | bytes 1966088 | tf_op jit(solution)/shard_map/ppermute | solution.py:386
  164.3 7.5 %collective-permute-start.13 = (bf16[8,32,1280]{2,1,0:T(8,128)(2,1)}, bf16[8,32,1280]{2,1,0:T(8,128)(2,1)}, u32[]{:S(2)}, u32[]{:S(2)}) collective-permute-start(bf16[8,32,1280]{2,1,0:T(8,128)(2,1)} %collective-permute-done.5.refs_6_), channel_id=1, source_target_pairs={{0,1},{1,0},{2,3},{3,2},{4,5},{5,4},{6,7},{7,6},{8,9},{9,8},{10,11... | collective-permute-start | bytes 1966088 | tf_op jit(solution)/shard_map/ppermute | solution.py:386
  164.4 7.4 %collective-permute-start.11 = (bf16[8,32,1280]{2,1,0:T(8,128)(2,1)}, bf16[8,32,1280]{2,1,0:T(8,128)(2,1)}, u32[]{:S(2)}, u32[]{:S(2)}) collective-permute-start(bf16[8,32,1280]{2,1,0:T(8,128)(2,1)} %collective-permute-done.3.refs_4_), channel_id=1, source_target_pairs={{0,1},{1,0},{2,3},{3,2},{4,5},{5,4},{6,7},{7,6},{8,9},{9,8},{10,11... | collective-permute-start | bytes 1966088 | tf_op jit(solution)/shard_map/ppermute | solution.py:386
  167.0 15.4 %collective-permute-start.21 = (bf16[16,32,640]{2,1,0:T(8,128)(2,1)}, bf16[16,32,640]{2,1,0:T(8,128)(2,1)}, u32[]{:S(2)}, u32[]{:S(2)}) collective-permute-start(bf16[16,32,640]{2,1,0:T(8,128)(2,1)} %collective-permute-done.19.refs_21_), channel_id=1, source_target_pairs={{0,48},{16,0},{32,16},{48,32},{64,112},{80,64},{96,80},{112,96},{1... | collective-permute-start | bytes 1966088 | tf_op jit(solution)/shard_map/ppermute | solution.py:347
  169.1 13.3 %collective-permute-start.14 = (bf16[8,32,1280]{2,1,0:T(8,128)(2,1)}, bf16[8,32,1280]{2,1,0:T(8,128)(2,1)}, u32[]{:S(2)}, u32[]{:S(2)}) collective-permute-start(bf16[8,32,1280]{2,1,0:T(8,128)(2,1)} %collective-permute-done.6.refs_7_), channel_id=1, source_target_pairs={{0,1},{1,0},{2,3},{3,2},{4,5},{5,4},{6,7},{7,6},{8,9},{9,8},{10,11... | collective-permute-start | bytes 1966088 | tf_op jit(solution)/shard_map/ppermute | solution.py:386
  (12 other events, 415.4 us)

commit v3 on v2

--- a/solution.py
+++ b/solution.py
@@ -97,8 +97,7 @@
     t3_ref,
     perm_ref,
     scale_ref,
-    sub_ref,
-    sign_ref,
+    gvec_ref,
     rows_ref,
     cols_ref,
     uval,
@@ -214,8 +213,9 @@
                 return carry
 
             lax.fori_loop(0, block // 64, pick, 0)
-            sub = sub_ref[:, b * block : (b + 1) * block]
-            sign = sign_ref[:, b * block : (b + 1) * block]
+            kx, _, _, flip = signed_parts(gvec_ref[:, b * block : (b + 1) * block])
+            sub = kx & 7
+            sign = flip.astype(jnp.float32)
             real, imag = [], []
             for k in range(GROUPS):
                 part = picked[k].astype(jnp.bfloat16)
@@ -230,19 +230,21 @@
             rows_ref[b // per_row, :, (b % per_row) * block : (b % per_row + 1) * block] = total
 
 
-def pair_elements(val_rows, cond_rows, scale, val, cond, gvec, row_blocks, col_blocks):
-    num_gvec = gvec.shape[0]
-    kx = gvec // (GY * GZ)
-    ky = gvec // GZ % GY
-    kz = gvec % GZ
+def signed_parts(gvec):
+    kx = gvec >> 13
+    ky = (gvec >> 7) & (GY - 1)
+    kz = gvec & (GZ - 1)
     kx = jnp.where(kx < GX // 2, kx, kx - GX)
     ky = jnp.where(ky < GY // 2, ky, ky - GY)
     kz = jnp.where(kz < GZ // 2, kz, kz - GZ)
     flip = jnp.where(ky < 0, -1, 1)
-    kx, ky, kz = kx * flip + HX, ky * flip, kz * flip
-    where_row = (ky * OCTS + kx // 8) * 2 * KZP + jnp.where(kz < 0, KZP - kz, kz)
-    sub = (kx % 8)[None, :]
-    sign = flip.astype(jnp.float32)[None, :]
+    return kx * flip + HX, ky * flip, kz * flip, flip
+
+
+def pair_elements(val_rows, cond_rows, scale, val, cond, gvec, row_blocks, col_blocks):
+    num_gvec = gvec.shape[0]
+    kx, ky, kz, _ = signed_parts(gvec)
+    where_row = (ky * OCTS + (kx >> 3)) * 2 * KZP + jnp.where(kz < 0, KZP - kz, kz)
     lanes = jnp.repeat(scale, 8).reshape(GROUPS, 1, -1)
     lanes = jnp.tile(lanes, (1, 2, 1)).reshape(1, -1)
     t1, t2, t3, perm = tables()
@@ -267,7 +269,6 @@
                 whole(perm.shape),
                 whole((1, GROUPS * LANES)),
                 whole((1, num_gvec)),
-                whole((1, num_gvec)),
             ],
             out_specs=[whole(o.shape) for o in outs],
             scratch_shapes=[
@@ -280,76 +281,89 @@
             ],
         ),
         compiler_params=pltpu.CompilerParams(vmem_limit_bytes=60 * 1024 * 1024),
-    )(val_rows, cond_rows, where_row, val, cond, t1, t2, t3, perm, lanes, sub, sign)
-
-
-def product_kernel(chunk_row, chunk_col, *refs):
-    lefts = refs[: len(LEFT)]
-    rights = refs[len(LEFT) : len(LEFT) + len(RIGHT)]
-    real_ref, imag_ref, table = refs[len(LEFT) + len(RIGHT) :]
+    )(val_rows, cond_rows, where_row, val, cond, t1, t2, t3, perm, lanes, gvec[None, :])
+
+
+def product_kernel(pairs, chunk_row, chunk_col, *refs):
+    lefts, rights, before = refs[: len(LEFT)], refs[len(LEFT) : COUNT], refs[COUNT:-4]
+    real_ref, imag_ref, lhs, table = refs[-4:]
     width = rights[0].shape[2]
     rows = 2 * PAIR_DEV
 
     @pl.when(pl.program_id(0) == 0)
     def _():
-        def fill(i, carry):
-            for k, right in enumerate(rights):
-                value = right[chunk_col[i]]
-                at = (i * len(RIGHT) + chunk_row[k]) * rows
-                first = pl.ds(pl.multiple_of(at, rows), PAIR_DEV)
-                last = pl.ds(pl.multiple_of(at + PAIR_DEV, PAIR_DEV), PAIR_DEV)
-                table[first, :width] = -value[:PAIR_DEV]
-                table[last, :width] = -value[PAIR_DEV:]
-                table[first, width:] = value[PAIR_DEV:]
-                table[last, width:] = -value[:PAIR_DEV]
-            return carry
-
-        lax.fori_loop(0, len(LEFT), fill, 0)
-
-    left = jnp.concatenate([ref[...].reshape(-1, ref.shape[2]) for ref in lefts], axis=0)
-    out = mm(left, table[...], (((0,), (0,)), ((), ())))
-    real_ref[...] = out[:, :width]
-    imag_ref[...] = out[:, width:]
+        for at, (i, k) in enumerate(pairs):
+            value = rights[k][chunk_col[i]]
+            first = slice(at * rows, at * rows + PAIR_DEV)
+            last = slice(at * rows + PAIR_DEV, (at + 1) * rows)
+            table[first, :width] = -value[:PAIR_DEV]
+            table[last, :width] = -value[PAIR_DEV:]
+            table[first, width:] = value[PAIR_DEV:]
+            table[last, width:] = -value[:PAIR_DEV]
+
+    for at, (i, k) in enumerate(pairs):
+        lhs[at * rows : (at + 1) * rows, :] = lefts[i][chunk_row[k]]
+    out = mm(lhs[...], table[...], (((0,), (0,)), ((), ())))
+    real, imag = out[:, :width], out[:, width:]
+    if before:
+        real += before[0][...]
+        imag += before[1][...]
+    real_ref[...] = real
+    imag_ref[...] = imag
 
 
 HALF = [(0, 0), (0, 1), (-1, 0), (1, 0), (-1, 1), (1, 1), (2, 0), (2, 1)]
 LEFT = [(dz, dx, core) for core in range(2) for dz, dx in HALF]
 RIGHT = [(dx, dy) for dy, dx in HALF]
+COUNT = len(LEFT) + len(RIGHT)
 TILE = 256
 
 
-def panel_product(lefts, rights):
+def panel_product(lefts, rights, pairs, before=()):
     row, col = lax.axis_index("row"), lax.axis_index("col")
     chunk_col = jnp.stack(
         [(col // 4 + dz) % 4 * 4 + (col // 2 % 2 ^ dx) * 2 + (col % 2 ^ dc) for dz, dx, dc in LEFT]
     )
     chunk_row = jnp.stack([(row // 4 ^ dx) * 4 + (row % 4 + dy) % 4 for dx, dy in RIGHT])
+    left_at, right_at = sorted({i for i, _ in pairs}), sorted({k for _, k in pairs})
     sources, rows, height = lefts[0].shape
     width = rights[0].shape[2]
-    depth = len(lefts) * sources * rows
+    depth = len(pairs) * rows
     out = jax.ShapeDtypeStruct((height, width), jnp.float32)
+    out_spec = pl.BlockSpec((TILE, width), lambda m, *_: (m, 0))
+
+    def kernel(chunk_row, chunk_col, *refs):
+        left_refs = dict(zip(left_at, refs))
+        refs = refs[len(left_at) :]
+        right_refs = dict(zip(right_at, refs))
+        refs = refs[len(right_at) :]
+        all_left = [left_refs.get(i) for i in range(len(LEFT))]
+        all_right = [right_refs.get(k) for k in range(len(RIGHT))]
+        product_kernel(pairs, chunk_row, chunk_col, *all_left, *all_right, *refs)
+
     return pl.pallas_call(
-        product_kernel,
+        kernel,
         out_shape=[out, out],
         grid_spec=pltpu.PrefetchScalarGridSpec(
             num_scalar_prefetch=2,
             grid=(height // TILE,),
-            in_specs=[pl.BlockSpec((sources, rows, TILE), lambda m, *_: (0, 0, m))] * len(lefts)
-            + [pl.BlockSpec(rights[0].shape, lambda m, *_: (0, 0, 0))] * len(rights),
-            out_specs=[pl.BlockSpec((TILE, width), lambda m, *_: (m, 0))] * 2,
-            scratch_shapes=[pltpu.VMEM((depth, 2 * width), jnp.bfloat16)],
+            in_specs=[pl.BlockSpec((sources, rows, TILE), lambda m, *_: (0, 0, m))] * len(left_at)
+            + [pl.BlockSpec(rights[0].shape, lambda m, *_: (0, 0, 0))] * len(right_at)
+            + [out_spec] * len(before),
+            out_specs=[out_spec] * 2,
+            scratch_shapes=[
+                pltpu.VMEM((depth, TILE), jnp.bfloat16),
+                pltpu.VMEM((depth, 2 * width), jnp.bfloat16),
+            ],
         ),
         compiler_params=pltpu.CompilerParams(vmem_limit_bytes=60 * 1024 * 1024),
-    )(chunk_row, chunk_col, *lefts, *rights)
-
-
-def ring_chunks(own, axis, ring, swap):
-    send = lambda value, perm: lax.ppermute(value, axis, perm)
-    near = (send(own, ring(1)), send(own, ring(-1)))
-    other = send(own, swap)
-    far = (send(other, ring(1)), send(other, ring(-1)))
-    ends = (send(near[0], ring(1)), send(far[1], ring(-1)))
-    return [own, other, *near, *far, *ends]
+    )(
+        chunk_row,
+        chunk_col,
+        *[lefts[i] for i in left_at],
+        *[rights[k] for k in right_at],
+        *before,
+    )
 
 
 def ring_z(step):
@@ -378,13 +392,34 @@
     rows_part, cols_part = pair_elements(
         val_rows, cond_rows, scale, val_orbitals, cond_orbitals, gvec_index, row_count, col_count
     )
-    rows_recv = lax.all_to_all(rows_part, "row", split_axis=0, concat_axis=0, tiled=True)
-    cols_part, rows_recv = lax.optimization_barrier((cols_part, rows_recv))
-    lefts = ring_chunks(rows_recv, "col", ring_z, [(c, c ^ 2) for c in range(16)])
-    cols_recv = lax.all_to_all(cols_part, "col", split_axis=0, concat_axis=0, tiled=True)
-    rights = ring_chunks(cols_recv, "row", ring_y, [(r, r ^ 4) for r in range(8)])
-    lefts += [lax.ppermute(left, "col", [(c, c ^ 1) for c in range(16)]) for left in lefts]
-    real, imag = panel_product(lefts, rights)
+    swap_core = [(c, c ^ 1) for c in range(col_count)]
+    swap_low = [(c, c ^ 2) for c in range(col_count)]
+    swap_high = [(r, r ^ 4) for r in range(row_count)]
+    along_z = lambda value, step: lax.ppermute(value, "col", ring_z(step))
+    along_y = lambda value, step: lax.ppermute(value, "row", ring_y(step))
+    cross = lambda value: lax.ppermute(value, "col", swap_core)
+    fence = lax.optimization_barrier
+
+    left = [lax.all_to_all(rows_part, "row", split_axis=0, concat_axis=0, tiled=True)]
+    cols_part, left = fence((cols_part, left))
+    low = lax.ppermute(left[0], "col", swap_low)
+    left_near = [along_z(left[0], 1), along_z(left[0], -1)]
+    right = [lax.all_to_all(cols_part, "col", split_axis=0, concat_axis=0, tiled=True)]
+    left, right = fence((left + [low] + left_near, right))
+    left_far = [along_z(left[1], 1), along_z(left[1], -1)]
+    right_near = [along_y(right[0], 1), along_y(right[0], -1)]
+    high = lax.ppermute(right[0], "row", swap_high)
+    left, right = fence((left + left_far, right + [high] + right_near))
+    right_far = [along_y(right[1], 1), along_y(right[1], -1)]
+    left_ends = [along_z(left[2], 1), along_z(left[5], -1)]
+    crossed = [cross(value) for value in left[:4]]
+    left, right, crossed = fence((left + left_ends, right + right_far, crossed))
+    right_ends = [along_y(right[2], 1), along_y(right[5], -1)]
+    crossed_last = [cross(value) for value in left[4:]]
+    early = [(i, k) for i in range(12) for k in range(6)]
+    late = [(i, k) for i in range(16) for k in range(8) if (i, k) not in early]
+    partial = panel_product(left + crossed, right, early)
+    real, imag = panel_product(left + crossed + crossed_last, right + right_ends, late, partial)
     return (real, imag)
 
 

time: 205 us -> 195 us (0.951)
  waiting for transfers between devices: 58.7 us -> 32.7 us
  blocking collectives: 18.7 us -> 43.2 us
  starting transfers between devices: 35 us -> 21.2 us
  Pallas kernels: 82.7 us -> 90.8 us
    all_to_all x0 -> x1, blocking collectives: none -> 24.7 us  [local(): lax.all_to_all(cols_part, 'col', split_axis=0, concat_axis=0, tiled=True)]
    all_to_all x1 -> x0, waiting for transfers between devices: 15 us -> none  [local(): lax.all_to_all(cols_part, 'col', split_axis=0, concat_axis=0, tiled=True)]
    ppermute x22, waiting for transfers between devices: 43.7 us -> 32.7 us  [the longest x6 25.9 us: local(): along_z = lambda value, step: lax.ppermute(value, 'col', ring_z(step))]
    ppermute x22, starting transfers between devices: 31.3 us -> 21.2 us  [the longest x6 8.08 us: local(): along_z = lambda value, step: lax.ppermute(value, 'col', ring_z(step))]
    pallas_call x1 -> x2, Pallas kernels: 20.8 us -> 29.2 us  [panel_product(): pl.pallas_call(kernel, out_shape=[out, out], grid_spec=pltpu.PrefetchScal...]
    all_to_all x1 -> x0, starting transfers between devices: 3.67 us -> none  [local(): lax.all_to_all(cols_part, 'col', split_axis=0, concat_axis=0, tiled=True)]
  transfers between devices with their start and end apart: 23 -> 22, of which waited for: 8 -> 9; matrix products, arithmetic and copies ran while one was open for 1% -> 1% of each run, Pallas kernels for 0% -> 7%
where the time goes in v3:
time: 195 us
  Pallas kernels  90.8 us (47%)
  blocking collectives  43.2 us (22%)
  waiting for transfers between devices  32.7 us (17%)
  starting transfers between devices  21.2 us (11%)
  other arithmetic  3.57 us (2%)
  local copies, waits for them, and re-layouts  2.23 us (1%)
    pallas_call x1, Pallas kernels, pair_elements(): pl.pallas_call(functools.partial(elements_kernel, row_blocks, col_blocks,...  61.6 us
    pallas_call x2, Pallas kernels, panel_product(): pl.pallas_call(kernel, out_shape=[out, out], grid_spec=pltpu.PrefetchScal...  29.2 us
    ppermute x6, waiting for transfers between devices, local(): along_z = lambda value, step: lax.ppermute(value, 'col', ring_z(step))  25.9 us
    all_to_all x1, blocking collectives, local(): lax.all_to_all(cols_part, 'col', split_axis=0, concat_axis=0, tiled=True)  24.7 us
    all_to_all x1, blocking collectives, local(): lax.all_to_all(rows_part, 'row', split_axis=0, concat_axis=0, tiled=True)  18.5 us
    ppermute x6, starting transfers between devices, local(): along_z = lambda value, step: lax.ppermute(value, 'col', ring_z(step))  8.08 us
    ppermute x8, starting transfers between devices, local(): cross = lambda value: lax.ppermute(value, 'col', swap_core)  6.18 us
    ppermute x6, starting transfers between devices, local(): along_y = lambda value, step: lax.ppermute(value, 'row', ring_y(step))  5.14 us
  transfers between devices with their start and end apart: 22, of which 9 were waited for; matrix products, arithmetic and copies ran while one was open for 1% of the time, Pallas kernels for 7%

profile of v3, /device:TPU:1, one launch (start us, length us, event | category | flops | bytes accessed | tf_op | source)
XLA Modules:
  0.0 194.8 jit_solution(4388571375999254429)
XLA Ops:
  0.6 1.2 and_select_fusion
  1.8 0.9 select_reduce_fusion
  3.7 1.4 fusion.3.where_row
  5.1 61.6 %shard_map.122 = (bf16[8,32,1280]{2,1,0:T(8,128)(2,1)}, bf16[16,32,640]{2,1,0:T(8,128)(2,1)}) custom-call(s32[16]{0:T(128)} %get-tuple-element.83.val_rows, s32[16]{0:T(128)} %get-tuple-element.82.cond_rows, s32[10240]{0:T(1024)} %fusion.3.where_row, bf16[8,524288]{1,0:T(8,128)(2,1)} %val_ref.1, bf16[8,524288]{1,0:T(8,128)(2,1)} %cond_ref.1, ...), custom_call_target="tpu_custom_call" | custom-call | tf_op jit(solution)/shard_map/pallas_call | solution.py:257
  66.7 18.5 %all_to_all.10.refs_0_ = bf16[8,32,1280]{2,1,0:T(8,128)(2,1)S(1)} all-to-all(bf16[8,32,1280]{2,1,0:T(8,128)(2,1)} %get-tuple-element.42), channel_id=1, replica_groups=mesh['row'=8,'col'=16] {'row'}, dimensions={0} | all-to-all | bytes 1310720 | tf_op jit(solution)/shard_map/all_to_all | solution.py:403
  85.2 4.1 %collective-permute-start.2 = (bf16[8,32,1280]{2,1,0:T(8,128)(2,1)S(1)}, bf16[8,32,1280]{2,1,0:T(8,128)(2,1)S(1)}, u32[]{:S(2)}, u32[]{:S(2)}) collective-permute-start(bf16[8,32,1280]{2,1,0:T(8,128)(2,1)S(1)} %all_to_all.10.refs_0_), channel_id=1, source_target_pairs={{0,12},{1,13},{2,14},{3,15},{4,0},{5,1},{6,2},{7,3},{8,4},{9,5},{1... | collective-permute-start | bytes 1966088 | tf_op jit(solution)/shard_map/ppermute | solution.py:398
  89.3 0.8 collective-permute-start
  90.1 24.7 %all_to_all.11.refs_12_.refs_16_ = bf16[16,32,640]{2,1,0:T(8,128)(2,1)S(1)} all-to-all(bf16[16,32,640]{2,1,0:T(8,128)(2,1)} %get-tuple-element.44), channel_id=1, replica_groups=mesh['row'=8,'col'=16] {'col'}, dimensions={0} | all-to-all | bytes 1310720 | tf_op jit(solution)/shard_map/all_to_all | solution.py:407
  115.5 0.9 collective-permute-start.3
  116.4 0.9 collective-permute-start.7
  117.9 1.0 collective-permute-start.5
  118.9 11.3 %collective-permute-done.4.refs_5_ = bf16[8,32,1280]{2,1,0:T(8,128)(2,1)} collective-permute-done((bf16[8,32,1280]{2,1,0:T(8,128)(2,1)S(1)}, bf16[8,32,1280]{2,1,0:T(8,128)(2,1)}, u32[]{:S(2)}, u32[]{:S(2)}) %collective-permute-start.4) | collective-permute-done | bytes 655392 | tf_op jit(solution)/shard_map/ppermute | solution.py:398
  130.2 2.2 %collective-permute-done.3.refs_4_ = bf16[8,32,1280]{2,1,0:T(8,128)(2,1)S(1)} collective-permute-done((bf16[8,32,1280]{2,1,0:T(8,128)(2,1)S(1)}, bf16[8,32,1280]{2,1,0:T(8,128)(2,1)S(1)}, u32[]{:S(2)}, u32[]{:S(2)}) %collective-permute-start.3) | collective-permute-done | bytes 655392 | tf_op jit(solution)/shard_map/ppermute | solution.py:398
  133.5 3.1 %collective-permute-start.12 = (bf16[8,32,1280]{2,1,0:T(8,128)(2,1)S(1)}, bf16[8,32,1280]{2,1,0:T(8,128)(2,1)S(1)}, u32[]{:S(2)}, u32[]{:S(2)}) collective-permute-start(bf16[8,32,1280]{2,1,0:T(8,128)(2,1)S(1)} %all_to_all.10.refs_0_), channel_id=1, source_target_pairs={{0,1},{1,0},{2,3},{3,2},{4,5},{5,4},{6,7},{7,6},{8,9},{9,8},{10,11... | collective-permute-start | bytes 1966088 | tf_op jit(solution)/shard_map/ppermute | solution.py:400
  138.3 1.8 collective-permute-start.9
  140.0 2.1 %collective-permute-start.11 = (bf16[16,32,640]{2,1,0:T(8,128)(2,1)S(1)}, bf16[16,32,640]{2,1,0:T(8,128)(2,1)}, u32[]{:S(2)}, u32[]{:S(2)}) collective-permute-start(bf16[16,32,640]{2,1,0:T(8,128)(2,1)S(1)} %collective-permute-done.5.refs_13_.refs_17_), channel_id=1, source_target_pairs={{0,48},{16,0},{32,16},{48,32},{64,112},{80,64},{96,80},{112,96},{1... | collective-permute-start | bytes 1966088 | tf_op jit(solution)/shard_map/ppermute | solution.py:399
  142.2 12.3 %collective-permute-done.9.refs_7_ = bf16[8,32,1280]{2,1,0:T(8,128)(2,1)} collective-permute-done((bf16[8,32,1280]{2,1,0:T(8,128)(2,1)}, bf16[8,32,1280]{2,1,0:T(8,128)(2,1)}, u32[]{:S(2)}, u32[]{:S(2)}) %collective-permute-start.9) | collective-permute-done | bytes 655392 | tf_op jit(solution)/shard_map/ppermute | solution.py:398
  154.5 1.1 collective-permute-done.11.refs_17_.refs_21_
  155.6 2.9 %collective-permute-done.10.refs_16_.refs_20_ = bf16[16,32,640]{2,1,0:T(8,128)(2,1)S(1)} collective-permute-done((bf16[16,32,640]{2,1,0:T(8,128)(2,1)S(1)}, bf16[16,32,640]{2,1,0:T(8,128)(2,1)S(1)}, u32[]{:S(2)}, u32[]{:S(2)}) %collective-permute-start.10) | collective-permute-done | bytes 655392 | tf_op jit(solution)/shard_map/ppermute | solution.py:399
  158.6 2.0 %collective-permute-start.16 = (bf16[8,32,1280]{2,1,0:T(8,128)(2,1)S(1)}, bf16[8,32,1280]{2,1,0:T(8,128)(2,1)S(1)}, u32[]{:S(2)}, u32[]{:S(2)}) collective-permute-start(bf16[8,32,1280]{2,1,0:T(8,128)(2,1)S(1)} %collective-permute-done.3.refs_4_), channel_id=1, source_target_pairs={{0,1},{1,0},{2,3},{3,2},{4,5},{5,4},{6,7},{7,6},{8,9},{9,8},{10,11... | collective-permute-start | bytes 1966088 | tf_op jit(solution)/shard_map/ppermute | solution.py:400
  161.1 1.2 collective-permute-done.16.refs_12_
  162.4 1.5 collective-permute-start.21
  165.4 13.9 %shard_map.123 = (f32[1280,640]{1,0:T(8,128)}, f32[1280,640]{1,0:T(8,128)}) custom-call(s32[8]{0:T(128)} %stack.112.chunk_row, s32[16]{0:T(128)} %stack.129.chunk_col, bf16[8,32,1280]{2,1,0:T(8,128)(2,1)} %copy-done, bf16[8,32,1280]{2,1,0:T(8,128)(2,1)} %copy-done.4, bf16[8,32,1280]{2,1,0:T(8,128)(2,1)} %copy-done.3, bf16[8,32,1280]{2,1,0:T(8,128)(2,1)} %copy-done.2, ...), custom_call_target="tpu_custom_call" | custom-call | tf_op jit(solution)/shard_map/pallas_call | solution.py:344
  179.4 15.3 %shard_map.124 = (f32[1280,640]{1,0:T(8,128)}, f32[1280,640]{1,0:T(8,128)}) custom-call(s32[8]{0:T(128)} %stack.112.chunk_row, s32[16]{0:T(128)} %stack.129.chunk_col, bf16[8,32,1280]{2,1,0:T(8,128)(2,1)} %copy-done, bf16[8,32,1280]{2,1,0:T(8,128)(2,1)} %copy-done.4, bf16[8,32,1280]{2,1,0:T(8,128)(2,1)} %copy-done.3, bf16[8,32,1280]{2,1,0:T(8,128)(2,1)} %copy-done.2, ...), custom_call_target="tpu_custom_call" | custom-call | tf_op jit(solution)/shard_map/pallas_call | solution.py:344
  (64 shorter events, 6.7 us)
Async XLA Ops:
  85.2 80.2 %copy-start = (bf16[8,32,1280]{2,1,0:T(8,128)(2,1)}, bf16[8,32,1280]{2,1,0:T(8,128)(2,1)S(1)}, u32[]{:S(2)}) copy-start(bf16[8,32,1280]{2,1,0:T(8,128)(2,1)S(1)} %all_to_all.10.refs_0_) | copy-start | bytes 1966084
  85.2 29.7 %collective-permute-start.2 = (bf16[8,32,1280]{2,1,0:T(8,128)(2,1)S(1)}, bf16[8,32,1280]{2,1,0:T(8,128)(2,1)S(1)}, u32[]{:S(2)}, u32[]{:S(2)}) collective-permute-start(bf16[8,32,1280]{2,1,0:T(8,128)(2,1)S(1)} %all_to_all.10.refs_0_), channel_id=1, source_target_pairs={{0,12},{1,13},{2,14},{3,15},{4,0},{5,1},{6,2},{7,3},{8,4},{9,5},{1... | collective-permute-start | bytes 1966088 | tf_op jit(solution)/shard_map/ppermute | solution.py:398
  89.3 25.5 %collective-permute-start.1 = (bf16[8,32,1280]{2,1,0:T(8,128)(2,1)S(1)}, bf16[8,32,1280]{2,1,0:T(8,128)(2,1)S(1)}, u32[]{:S(2)}, u32[]{:S(2)}) collective-permute-start(bf16[8,32,1280]{2,1,0:T(8,128)(2,1)S(1)} %all_to_all.10.refs_0_), channel_id=1, source_target_pairs={{0,4},{1,5},{2,6},{3,7},{4,8},{5,9},{6,10},{7,11},{8,12},{9,13},{1... | collective-permute-start | bytes 1966088 | tf_op jit(solution)/shard_map/ppermute | solution.py:398
  89.3 25.5 %collective-permute-start = (bf16[8,32,1280]{2,1,0:T(8,128)(2,1)S(1)}, bf16[8,32,1280]{2,1,0:T(8,128)(2,1)S(1)}, u32[]{:S(2)}, u32[]{:S(2)}) collective-permute-start(bf16[8,32,1280]{2,1,0:T(8,128)(2,1)S(1)} %all_to_all.10.refs_0_), channel_id=1, source_target_pairs={{0,2},{1,3},{2,0},{3,1},{4,6},{5,7},{6,4},{7,5},{8,10},{9,11},{10,... | collective-permute-start | bytes 1966088 | tf_op jit(solution)/shard_map/ppermute | solution.py:405
  114.8 50.6 %copy-start.1 = (bf16[16,32,640]{2,1,0:T(8,128)(2,1)}, bf16[16,32,640]{2,1,0:T(8,128)(2,1)S(1)}, u32[]{:S(2)}) copy-start(bf16[16,32,640]{2,1,0:T(8,128)(2,1)S(1)} %all_to_all.11.refs_12_.refs_16_) | copy-start | bytes 1966084
  114.9 15.4 %collective-permute-start.4 = (bf16[8,32,1280]{2,1,0:T(8,128)(2,1)S(1)}, bf16[8,32,1280]{2,1,0:T(8,128)(2,1)}, u32[]{:S(2)}, u32[]{:S(2)}) collective-permute-start(bf16[8,32,1280]{2,1,0:T(8,128)(2,1)S(1)} %collective-permute-done.refs_1_), channel_id=1, source_target_pairs={{0,12},{1,13},{2,14},{3,15},{4,0},{5,1},{6,2},{7,3},{8,4},{9,5},{1... | collective-permute-start | bytes 1966088 | tf_op jit(solution)/shard_map/ppermute | solution.py:398
  115.5 17.0 %collective-permute-start.3 = (bf16[8,32,1280]{2,1,0:T(8,128)(2,1)S(1)}, bf16[8,32,1280]{2,1,0:T(8,128)(2,1)S(1)}, u32[]{:S(2)}, u32[]{:S(2)}) collective-permute-start(bf16[8,32,1280]{2,1,0:T(8,128)(2,1)S(1)} %collective-permute-done.refs_1_), channel_id=1, source_target_pairs={{0,4},{1,5},{2,6},{3,7},{4,8},{5,9},{6,10},{7,11},{8,12},{9,13},{1... | collective-permute-start | bytes 1966088 | tf_op jit(solution)/shard_map/ppermute | solution.py:398
  116.4 16.1 %collective-permute-start.7 = (bf16[16,32,640]{2,1,0:T(8,128)(2,1)S(1)}, bf16[16,32,640]{2,1,0:T(8,128)(2,1)S(1)}, u32[]{:S(2)}, u32[]{:S(2)}) collective-permute-start(bf16[16,32,640]{2,1,0:T(8,128)(2,1)S(1)} %all_to_all.11.refs_12_.refs_16_), channel_id=1, source_target_pairs={{0,48},{16,0},{32,16},{48,32},{64,112},{80,64},{96,80},{112,96},{1... | collective-permute-start | bytes 1966088 | tf_op jit(solution)/shard_map/ppermute | solution.py:399
  117.3 15.7 %collective-permute-start.6 = (bf16[16,32,640]{2,1,0:T(8,128)(2,1)S(1)}, bf16[16,32,640]{2,1,0:T(8,128)(2,1)}, u32[]{:S(2)}, u32[]{:S(2)}) collective-permute-start(bf16[16,32,640]{2,1,0:T(8,128)(2,1)S(1)} %all_to_all.11.refs_12_.refs_16_), channel_id=1, source_target_pairs={{0,16},{16,32},{32,48},{48,0},{64,80},{80,96},{96,112},{112,64},{1... | collective-permute-start | bytes 1966088 | tf_op jit(solution)/shard_map/ppermute | solution.py:399
  117.9 15.6 %collective-permute-start.5 = (bf16[16,32,640]{2,1,0:T(8,128)(2,1)S(1)}, bf16[16,32,640]{2,1,0:T(8,128)(2,1)S(1)}, u32[]{:S(2)}, u32[]{:S(2)}) collective-permute-start(bf16[16,32,640]{2,1,0:T(8,128)(2,1)S(1)} %all_to_all.11.refs_12_.refs_16_), channel_id=1, source_target_pairs={{0,64},{16,80},{32,96},{48,112},{64,0},{80,16},{96,32},{112,48},{1... | collective-permute-start | bytes 1966088 | tf_op jit(solution)/shard_map/ppermute | solution.py:411
  133.5 4.8 %collective-permute-start.12 = (bf16[8,32,1280]{2,1,0:T(8,128)(2,1)S(1)}, bf16[8,32,1280]{2,1,0:T(8,128)(2,1)S(1)}, u32[]{:S(2)}, u32[]{:S(2)}) collective-permute-start(bf16[8,32,1280]{2,1,0:T(8,128)(2,1)S(1)} %all_to_all.10.refs_0_), channel_id=1, source_target_pairs={{0,1},{1,0},{2,3},{3,2},{4,5},{5,4},{6,7},{7,6},{8,9},{9,8},{10,11... | collective-permute-start | bytes 1966088 | tf_op jit(solution)/shard_map/ppermute | solution.py:400
  136.5 3.5 %collective-permute-start.13 = (bf16[8,32,1280]{2,1,0:T(8,128)(2,1)S(1)}, bf16[8,32,1280]{2,1,0:T(8,128)(2,1)S(1)}, u32[]{:S(2)}, u32[]{:S(2)}) collective-permute-start(bf16[8,32,1280]{2,1,0:T(8,128)(2,1)S(1)} %collective-permute-done.refs_1_), channel_id=1, source_target_pairs={{0,1},{1,0},{2,3},{3,2},{4,5},{5,4},{6,7},{7,6},{8,9},{9,8},{10,11... | collective-permute-start | bytes 1966088 | tf_op jit(solution)/shard_map/ppermute | solution.py:400
  136.5 5.6 %collective-permute-start.15 = (bf16[8,32,1280]{2,1,0:T(8,128)(2,1)S(1)}, bf16[8,32,1280]{2,1,0:T(8,128)(2,1)S(1)}, u32[]{:S(2)}, u32[]{:S(2)}) collective-permute-start(bf16[8,32,1280]{2,1,0:T(8,128)(2,1)S(1)} %collective-permute-done.2.refs_3_), channel_id=1, source_target_pairs={{0,1},{1,0},{2,3},{3,2},{4,5},{5,4},{6,7},{7,6},{8,9},{9,8},{10,11... | collective-permute-start | bytes 1966088 | tf_op jit(solution)/shard_map/ppermute | solution.py:400
  137.1 17.5 %collective-permute-start.14 = (bf16[8,32,1280]{2,1,0:T(8,128)(2,1)S(1)}, bf16[8,32,1280]{2,1,0:T(8,128)(2,1)S(1)}, u32[]{:S(2)}, u32[]{:S(2)}) collective-permute-start(bf16[8,32,1280]{2,1,0:T(8,128)(2,1)S(1)} %collective-permute-done.1.refs_2_), channel_id=1, source_target_pairs={{0,1},{1,0},{2,3},{3,2},{4,5},{5,4},{6,7},{7,6},{8,9},{9,8},{10,11... | collective-permute-start | bytes 1966088 | tf_op jit(solution)/shard_map/ppermute | solution.py:400
  137.1 17.5 %collective-permute-start.8 = (bf16[8,32,1280]{2,1,0:T(8,128)(2,1)S(1)}, bf16[8,32,1280]{2,1,0:T(8,128)(2,1)}, u32[]{:S(2)}, u32[]{:S(2)}) collective-permute-start(bf16[8,32,1280]{2,1,0:T(8,128)(2,1)S(1)} %collective-permute-done.1.refs_2_), channel_id=1, source_target_pairs={{0,4},{1,5},{2,6},{3,7},{4,8},{5,9},{6,10},{7,11},{8,12},{9,13},{1... | collective-permute-start | bytes 1966088 | tf_op jit(solution)/shard_map/ppermute | solution.py:398
  138.3 16.3 %collective-permute-start.9 = (bf16[8,32,1280]{2,1,0:T(8,128)(2,1)}, bf16[8,32,1280]{2,1,0:T(8,128)(2,1)}, u32[]{:S(2)}, u32[]{:S(2)}) collective-permute-start(bf16[8,32,1280]{2,1,0:T(8,128)(2,1)} %collective-permute-done.4.refs_5_), channel_id=1, source_target_pairs={{0,12},{1,13},{2,14},{3,15},{4,0},{5,1},{6,2},{7,3},{8,4},{9,5},{1... | collective-permute-start | bytes 1966088 | tf_op jit(solution)/shard_map/ppermute | solution.py:398
  140.0 15.6 %collective-permute-start.11 = (bf16[16,32,640]{2,1,0:T(8,128)(2,1)S(1)}, bf16[16,32,640]{2,1,0:T(8,128)(2,1)}, u32[]{:S(2)}, u32[]{:S(2)}) collective-permute-start(bf16[16,32,640]{2,1,0:T(8,128)(2,1)S(1)} %collective-permute-done.5.refs_13_.refs_17_), channel_id=1, source_target_pairs={{0,48},{16,0},{32,16},{48,32},{64,112},{80,64},{96,80},{112,96},{1... | collective-permute-start | bytes 1966088 | tf_op jit(solution)/shard_map/ppermute | solution.py:399
  142.2 16.4 %collective-permute-start.10 = (bf16[16,32,640]{2,1,0:T(8,128)(2,1)S(1)}, bf16[16,32,640]{2,1,0:T(8,128)(2,1)S(1)}, u32[]{:S(2)}, u32[]{:S(2)}) collective-permute-start(bf16[16,32,640]{2,1,0:T(8,128)(2,1)S(1)} %collective-permute-done.5.refs_13_.refs_17_), channel_id=1, source_target_pairs={{0,16},{16,32},{32,48},{48,0},{64,80},{80,96},{96,112},{112,64},{1... | collective-permute-start | bytes 1966088 | tf_op jit(solution)/shard_map/ppermute | solution.py:399
  158.6 3.8 %collective-permute-start.16 = (bf16[8,32,1280]{2,1,0:T(8,128)(2,1)S(1)}, bf16[8,32,1280]{2,1,0:T(8,128)(2,1)S(1)}, u32[]{:S(2)}, u32[]{:S(2)}) collective-permute-start(bf16[8,32,1280]{2,1,0:T(8,128)(2,1)S(1)} %collective-permute-done.3.refs_4_), channel_id=1, source_target_pairs={{0,1},{1,0},{2,3},{3,2},{4,5},{5,4},{6,7},{7,6},{8,9},{9,8},{10,11... | collective-permute-start | bytes 1966088 | tf_op jit(solution)/shard_map/ppermute | solution.py:400
  160.5 18.8 %collective-permute-start.17 = (bf16[8,32,1280]{2,1,0:T(8,128)(2,1)}, bf16[8,32,1280]{2,1,0:T(8,128)(2,1)}, u32[]{:S(2)}, u32[]{:S(2)}) collective-permute-start(bf16[8,32,1280]{2,1,0:T(8,128)(2,1)} %collective-permute-done.4.refs_5_), channel_id=1, source_target_pairs={{0,1},{1,0},{2,3},{3,2},{4,5},{5,4},{6,7},{7,6},{8,9},{9,8},{10,11... | collective-permute-start | bytes 1966088 | tf_op jit(solution)/shard_map/ppermute | solution.py:400
  160.6 18.7 %collective-permute-start.18 = (bf16[8,32,1280]{2,1,0:T(8,128)(2,1)}, bf16[8,32,1280]{2,1,0:T(8,128)(2,1)}, u32[]{:S(2)}, u32[]{:S(2)}) collective-permute-start(bf16[8,32,1280]{2,1,0:T(8,128)(2,1)} %collective-permute-done.8.refs_6_), channel_id=1, source_target_pairs={{0,1},{1,0},{2,3},{3,2},{4,5},{5,4},{6,7},{7,6},{8,9},{9,8},{10,11... | collective-permute-start | bytes 1966088 | tf_op jit(solution)/shard_map/ppermute | solution.py:400
  161.1 18.3 %collective-permute-start.19 = (bf16[8,32,1280]{2,1,0:T(8,128)(2,1)}, bf16[8,32,1280]{2,1,0:T(8,128)(2,1)}, u32[]{:S(2)}, u32[]{:S(2)}) collective-permute-start(bf16[8,32,1280]{2,1,0:T(8,128)(2,1)} %collective-permute-done.9.refs_7_), channel_id=1, source_target_pairs={{0,1},{1,0},{2,3},{3,2},{4,5},{5,4},{6,7},{7,6},{8,9},{9,8},{10,11... | collective-permute-start | bytes 1966088 | tf_op jit(solution)/shard_map/ppermute | solution.py:400
  161.1 18.2 %collective-permute-start.20 = (bf16[16,32,640]{2,1,0:T(8,128)(2,1)}, bf16[16,32,640]{2,1,0:T(8,128)(2,1)}, u32[]{:S(2)}, u32[]{:S(2)}) collective-permute-start(bf16[16,32,640]{2,1,0:T(8,128)(2,1)} %collective-permute-done.6.refs_14_.refs_18_), channel_id=1, source_target_pairs={{0,16},{16,32},{32,48},{48,0},{64,80},{80,96},{96,112},{112,64},{1... | collective-permute-start | bytes 1966088 | tf_op jit(solution)/shard_map/ppermute | solution.py:399
  162.4 17.0 %collective-permute-start.21 = (bf16[16,32,640]{2,1,0:T(8,128)(2,1)}, bf16[16,32,640]{2,1,0:T(8,128)(2,1)}, u32[]{:S(2)}, u32[]{:S(2)}) collective-permute-start(bf16[16,32,640]{2,1,0:T(8,128)(2,1)} %collective-permute-done.11.refs_17_.refs_21_), channel_id=1, source_target_pairs={{0,48},{16,0},{32,16},{48,32},{64,112},{80,64},{96,80},{112,96},{1... | collective-permute-start | bytes 1966088 | tf_op jit(solution)/shard_map/ppermute | solution.py:399
  (12 other events, 325.5 us)

commit v4 on v3

--- a/solution.py
+++ b/solution.py
@@ -22,7 +22,7 @@
 OCTS = KXP // 8
 KZP = 40
 SLOTS = NKY * OCTS
-XCH = 8
+XCH = 16
 STEPS = GX // XCH
 SPAN = XCH * GY + 8
 LANES = 128
@@ -110,15 +110,15 @@
     step = pl.program_id(0)
 
     def unpack(i, carry):
-        for j in range(16):
-            at = i * 16 + j
+        for j in range(64):
+            at = i * 64 + j
             columns = pl.ds(pl.multiple_of(at * LANES, LANES), LANES)
             rows = pl.ds(at, BANDS, stride=SPAN)
             uval[rows, :] = val_ref[:, columns].astype(jnp.float32)
             ucond[rows, :] = cond_ref[:, columns].astype(jnp.float32)
         return carry
 
-    lax.fori_loop(0, XCH * GY // 16, unpack, 0)
+    lax.fori_loop(0, XCH * GY // 64, unpack, 0)
 
     def pair_first(p, carry):
         vb = val_rows[p]
@@ -140,7 +140,7 @@
                 first[pl.ds(pl.multiple_of(at, 8), ROWS1), :] = out[:, k * LANES : (k + 1) * LANES]
         return carry
 
-    lax.fori_loop(0, PAIR_DEV, pair_first, 0, unroll=2)
+    lax.fori_loop(0, PAIR_DEV, pair_first, 0, unroll=8)
 
     @pl.when(step == STEPS - 1)
     def _():
@@ -168,7 +168,7 @@
                             ]
             return carry
 
-        lax.fori_loop(0, NKY, second_stage, 0)
+        lax.fori_loop(0, NKY, second_stage, 0, unroll=17)
 
         lane = lax.broadcasted_iota(jnp.int32, (1, GROUPS * LANES), 1) % LANES
         scale = scale_ref[...]
@@ -197,7 +197,7 @@
                 spectrum[k, pl.ds(pl.multiple_of(at + KZP, 8), KZP), :] = minus[:, part]
             return carry
 
-        lax.fori_loop(0, SLOTS, third_stage, 0, unroll=5)
+        lax.fori_loop(0, SLOTS, third_stage, 0, unroll=17)
 
         block = num_gvec // col_blocks
         per_row = col_blocks // row_blocks
@@ -205,11 +205,16 @@
         for b in range(col_blocks):
 
             def pick(i, carry):
-                for j in range(64):
-                    at = i * 64 + j
-                    row = where_row[b * block + at]
+                sublane = lax.broadcasted_iota(jnp.int32, (8, LANES), 0)
+                for j in range(0, 64, 8):
+                    at = pl.multiple_of(i * 64 + j, 8)
+                    rows = [where_row[b * block + at + n] for n in range(8)]
                     for k in range(GROUPS):
-                        picked[k, pl.ds(at, 1), :] = spectrum[k, pl.ds(row, 1), :]
+                        tile = jnp.broadcast_to(spectrum[k, pl.ds(rows[0], 1), :], (8, LANES))
+                        for n in range(1, 8):
+                            line = jnp.broadcast_to(spectrum[k, pl.ds(rows[n], 1), :], (8, LANES))
+                            tile = jnp.where(sublane == n, line, tile)
+                        picked[k, pl.ds(at, 8), :] = tile
                 return carry
 
             lax.fori_loop(0, block // 64, pick, 0)

time: 195 us -> 180 us (0.923)
  Pallas kernels: 90.8 us -> 74.6 us
    pallas_call x1, Pallas kernels: 61.6 us -> 45.4 us  [pair_elements(): pl.pallas_call(functools.partial(elements_kernel, row_blocks, col_blocks,...]
  transfers between devices with their start and end apart: 22 -> 22, of which waited for: 9 -> 9; matrix products, arithmetic and copies ran while one was open for 1% -> 1% of each run, Pallas kernels for 7% -> 8%
where the time goes in v4:
time: 180 us; the launch traced here: 179 us
  Pallas kernels  74.6 us (41%)
  blocking collectives  44.3 us (25%)
  waiting for transfers between devices  33 us (18%)
  starting transfers between devices  20.5 us (11%)
  other arithmetic  3.57 us (2%)
  local copies, waits for them, and re-layouts  2.23 us (1%)
    pallas_call x1, Pallas kernels, pair_elements(): pl.pallas_call(functools.partial(elements_kernel, row_blocks, col_blocks,...  45.4 us
    pallas_call x2, Pallas kernels, panel_product(): pl.pallas_call(kernel, out_shape=[out, out], grid_spec=pltpu.PrefetchScal...  29.2 us
    ppermute x6, waiting for transfers between devices, local(): along_z = lambda value, step: lax.ppermute(value, 'col', ring_z(step))  26.3 us
    all_to_all x1, blocking collectives, local(): lax.all_to_all(cols_part, 'col', split_axis=0, concat_axis=0, tiled=True)  25 us
    all_to_all x1, blocking collectives, local(): lax.all_to_all(rows_part, 'row', split_axis=0, concat_axis=0, tiled=True)  19.2 us
    ppermute x6, starting transfers between devices, local(): along_z = lambda value, step: lax.ppermute(value, 'col', ring_z(step))  8.07 us
    ppermute x8, starting transfers between devices, local(): cross = lambda value: lax.ppermute(value, 'col', swap_core)  6.18 us
    ppermute x6, starting transfers between devices, local(): along_y = lambda value, step: lax.ppermute(value, 'row', ring_y(step))  5.04 us
  transfers between devices with their start and end apart: 22, of which 9 were waited for; matrix products, arithmetic and copies ran while one was open for 1% of the time, Pallas kernels for 8%

profile of v4, /device:TPU:1, one launch (start us, length us, event | category | flops | bytes accessed | tf_op | source)
XLA Modules:
  0.0 179.2 jit_solution(11777128944770590723)
XLA Ops:
  0.6 1.2 and_select_fusion
  1.8 0.9 select_reduce_fusion
  3.0 0.7 tile.8.scale_ref
  3.7 1.4 fusion.3.where_row
  5.1 45.4 %shard_map.122 = (bf16[8,32,1280]{2,1,0:T(8,128)(2,1)}, bf16[16,32,640]{2,1,0:T(8,128)(2,1)}) custom-call(s32[16]{0:T(128)} %get-tuple-element.83.val_rows, s32[16]{0:T(128)} %get-tuple-element.82.cond_rows, s32[10240]{0:T(1024)} %fusion.3.where_row, bf16[8,524288]{1,0:T(8,128)(2,1)} %val_ref.1, bf16[8,524288]{1,0:T(8,128)(2,1)} %cond_ref.1, ...), custom_call_target="tpu_custom_call" | custom-call | tf_op jit(solution)/shard_map/pallas_call | solution.py:262
  50.5 19.2 %all_to_all.10.refs_0_ = bf16[8,32,1280]{2,1,0:T(8,128)(2,1)S(1)} all-to-all(bf16[8,32,1280]{2,1,0:T(8,128)(2,1)} %get-tuple-element.42), channel_id=1, replica_groups=mesh['row'=8,'col'=16] {'row'}, dimensions={0} | all-to-all | bytes 1310720 | tf_op jit(solution)/shard_map/all_to_all | solution.py:408
  69.7 4.1 %collective-permute-start.2 = (bf16[8,32,1280]{2,1,0:T(8,128)(2,1)S(1)}, bf16[8,32,1280]{2,1,0:T(8,128)(2,1)S(1)}, u32[]{:S(2)}, u32[]{:S(2)}) collective-permute-start(bf16[8,32,1280]{2,1,0:T(8,128)(2,1)S(1)} %all_to_all.10.refs_0_), channel_id=1, source_target_pairs={{0,12},{1,13},{2,14},{3,15},{4,0},{5,1},{6,2},{7,3},{8,4},{9,5},{1... | collective-permute-start | bytes 1966088 | tf_op jit(solution)/shard_map/ppermute | solution.py:403
  74.3 25.0 %all_to_all.11.refs_12_.refs_16_ = bf16[16,32,640]{2,1,0:T(8,128)(2,1)S(1)} all-to-all(bf16[16,32,640]{2,1,0:T(8,128)(2,1)} %get-tuple-element.44), channel_id=1, replica_groups=mesh['row'=8,'col'=16] {'col'}, dimensions={0} | all-to-all | bytes 1310720 | tf_op jit(solution)/shard_map/all_to_all | solution.py:412
  100.0 0.9 collective-permute-start.3
  100.9 0.8 collective-permute-start.7
  102.4 0.7 collective-permute-start.5
  103.1 11.7 %collective-permute-done.4.refs_5_ = bf16[8,32,1280]{2,1,0:T(8,128)(2,1)} collective-permute-done((bf16[8,32,1280]{2,1,0:T(8,128)(2,1)S(1)}, bf16[8,32,1280]{2,1,0:T(8,128)(2,1)}, u32[]{:S(2)}, u32[]{:S(2)}) %collective-permute-start.4) | collective-permute-done | bytes 655392 | tf_op jit(solution)/shard_map/ppermute | solution.py:403
  114.8 2.2 %collective-permute-done.3.refs_4_ = bf16[8,32,1280]{2,1,0:T(8,128)(2,1)S(1)} collective-permute-done((bf16[8,32,1280]{2,1,0:T(8,128)(2,1)S(1)}, bf16[8,32,1280]{2,1,0:T(8,128)(2,1)S(1)}, u32[]{:S(2)}, u32[]{:S(2)}) %collective-permute-start.3) | collective-permute-done | bytes 655392 | tf_op jit(solution)/shard_map/ppermute | solution.py:403
  118.0 3.1 %collective-permute-start.12 = (bf16[8,32,1280]{2,1,0:T(8,128)(2,1)S(1)}, bf16[8,32,1280]{2,1,0:T(8,128)(2,1)S(1)}, u32[]{:S(2)}, u32[]{:S(2)}) collective-permute-start(bf16[8,32,1280]{2,1,0:T(8,128)(2,1)S(1)} %all_to_all.10.refs_0_), channel_id=1, source_target_pairs={{0,1},{1,0},{2,3},{3,2},{4,5},{5,4},{6,7},{7,6},{8,9},{9,8},{10,11... | collective-permute-start | bytes 1966088 | tf_op jit(solution)/shard_map/ppermute | solution.py:405
  122.8 1.8 collective-permute-start.9
  124.5 2.0 %collective-permute-start.11 = (bf16[16,32,640]{2,1,0:T(8,128)(2,1)S(1)}, bf16[16,32,640]{2,1,0:T(8,128)(2,1)}, u32[]{:S(2)}, u32[]{:S(2)}) collective-permute-start(bf16[16,32,640]{2,1,0:T(8,128)(2,1)S(1)} %collective-permute-done.5.refs_13_.refs_17_), channel_id=1, source_target_pairs={{0,48},{16,0},{32,16},{48,32},{64,112},{80,64},{96,80},{112,96},{1... | collective-permute-start | bytes 1966088 | tf_op jit(solution)/shard_map/ppermute | solution.py:404
  126.6 12.4 %collective-permute-done.9.refs_7_ = bf16[8,32,1280]{2,1,0:T(8,128)(2,1)} collective-permute-done((bf16[8,32,1280]{2,1,0:T(8,128)(2,1)}, bf16[8,32,1280]{2,1,0:T(8,128)(2,1)}, u32[]{:S(2)}, u32[]{:S(2)}) %collective-permute-start.9) | collective-permute-done | bytes 655392 | tf_op jit(solution)/shard_map/ppermute | solution.py:403
  139.1 1.1 collective-permute-done.11.refs_17_.refs_21_
  140.1 2.8 %collective-permute-done.10.refs_16_.refs_20_ = bf16[16,32,640]{2,1,0:T(8,128)(2,1)S(1)} collective-permute-done((bf16[16,32,640]{2,1,0:T(8,128)(2,1)S(1)}, bf16[16,32,640]{2,1,0:T(8,128)(2,1)S(1)}, u32[]{:S(2)}, u32[]{:S(2)}) %collective-permute-start.10) | collective-permute-done | bytes 655392 | tf_op jit(solution)/shard_map/ppermute | solution.py:404
  143.0 2.0 %collective-permute-start.16 = (bf16[8,32,1280]{2,1,0:T(8,128)(2,1)S(1)}, bf16[8,32,1280]{2,1,0:T(8,128)(2,1)S(1)}, u32[]{:S(2)}, u32[]{:S(2)}) collective-permute-start(bf16[8,32,1280]{2,1,0:T(8,128)(2,1)S(1)} %collective-permute-done.3.refs_4_), channel_id=1, source_target_pairs={{0,1},{1,0},{2,3},{3,2},{4,5},{5,4},{6,7},{7,6},{8,9},{9,8},{10,11... | collective-permute-start | bytes 1966088 | tf_op jit(solution)/shard_map/ppermute | solution.py:405
  145.6 1.2 collective-permute-done.16.refs_12_
  146.8 1.5 collective-permute-start.21
  149.8 13.9 %shard_map.123 = (f32[1280,640]{1,0:T(8,128)}, f32[1280,640]{1,0:T(8,128)}) custom-call(s32[8]{0:T(128)} %stack.112.chunk_row, s32[16]{0:T(128)} %stack.129.chunk_col, bf16[8,32,1280]{2,1,0:T(8,128)(2,1)} %copy-done, bf16[8,32,1280]{2,1,0:T(8,128)(2,1)} %copy-done.4, bf16[8,32,1280]{2,1,0:T(8,128)(2,1)} %copy-done.3, bf16[8,32,1280]{2,1,0:T(8,128)(2,1)} %copy-done.2, ...), custom_call_target="tpu_custom_call" | custom-call | tf_op jit(solution)/shard_map/pallas_call | solution.py:349
  163.8 15.3 %shard_map.124 = (f32[1280,640]{1,0:T(8,128)}, f32[1280,640]{1,0:T(8,128)}) custom-call(s32[8]{0:T(128)} %stack.112.chunk_row, s32[16]{0:T(128)} %stack.129.chunk_col, bf16[8,32,1280]{2,1,0:T(8,128)(2,1)} %copy-done, bf16[8,32,1280]{2,1,0:T(8,128)(2,1)} %copy-done.4, bf16[8,32,1280]{2,1,0:T(8,128)(2,1)} %copy-done.3, bf16[8,32,1280]{2,1,0:T(8,128)(2,1)} %copy-done.2, ...), custom_call_target="tpu_custom_call" | custom-call | tf_op jit(solution)/shard_map/pallas_call | solution.py:349
  (64 shorter events, 6.6 us)
Async XLA Ops:
  69.7 80.1 %copy-start = (bf16[8,32,1280]{2,1,0:T(8,128)(2,1)}, bf16[8,32,1280]{2,1,0:T(8,128)(2,1)S(1)}, u32[]{:S(2)}) copy-start(bf16[8,32,1280]{2,1,0:T(8,128)(2,1)S(1)} %all_to_all.10.refs_0_) | copy-start | bytes 1966084
  69.7 29.6 %collective-permute-start.2 = (bf16[8,32,1280]{2,1,0:T(8,128)(2,1)S(1)}, bf16[8,32,1280]{2,1,0:T(8,128)(2,1)S(1)}, u32[]{:S(2)}, u32[]{:S(2)}) collective-permute-start(bf16[8,32,1280]{2,1,0:T(8,128)(2,1)S(1)} %all_to_all.10.refs_0_), channel_id=1, source_target_pairs={{0,12},{1,13},{2,14},{3,15},{4,0},{5,1},{6,2},{7,3},{8,4},{9,5},{1... | collective-permute-start | bytes 1966088 | tf_op jit(solution)/shard_map/ppermute | solution.py:403
  73.8 25.5 %collective-permute-start.1 = (bf16[8,32,1280]{2,1,0:T(8,128)(2,1)S(1)}, bf16[8,32,1280]{2,1,0:T(8,128)(2,1)S(1)}, u32[]{:S(2)}, u32[]{:S(2)}) collective-permute-start(bf16[8,32,1280]{2,1,0:T(8,128)(2,1)S(1)} %all_to_all.10.refs_0_), channel_id=1, source_target_pairs={{0,4},{1,5},{2,6},{3,7},{4,8},{5,9},{6,10},{7,11},{8,12},{9,13},{1... | collective-permute-start | bytes 1966088 | tf_op jit(solution)/shard_map/ppermute | solution.py:403
  73.8 25.5 %collective-permute-start = (bf16[8,32,1280]{2,1,0:T(8,128)(2,1)S(1)}, bf16[8,32,1280]{2,1,0:T(8,128)(2,1)S(1)}, u32[]{:S(2)}, u32[]{:S(2)}) collective-permute-start(bf16[8,32,1280]{2,1,0:T(8,128)(2,1)S(1)} %all_to_all.10.refs_0_), channel_id=1, source_target_pairs={{0,2},{1,3},{2,0},{3,1},{4,6},{5,7},{6,4},{7,5},{8,10},{9,11},{10,... | collective-permute-start | bytes 1966088 | tf_op jit(solution)/shard_map/ppermute | solution.py:410
  99.4 50.5 %copy-start.1 = (bf16[16,32,640]{2,1,0:T(8,128)(2,1)}, bf16[16,32,640]{2,1,0:T(8,128)(2,1)S(1)}, u32[]{:S(2)}) copy-start(bf16[16,32,640]{2,1,0:T(8,128)(2,1)S(1)} %all_to_all.11.refs_12_.refs_16_) | copy-start | bytes 1966084
  99.4 15.4 %collective-permute-start.4 = (bf16[8,32,1280]{2,1,0:T(8,128)(2,1)S(1)}, bf16[8,32,1280]{2,1,0:T(8,128)(2,1)}, u32[]{:S(2)}, u32[]{:S(2)}) collective-permute-start(bf16[8,32,1280]{2,1,0:T(8,128)(2,1)S(1)} %collective-permute-done.refs_1_), channel_id=1, source_target_pairs={{0,12},{1,13},{2,14},{3,15},{4,0},{5,1},{6,2},{7,3},{8,4},{9,5},{1... | collective-permute-start | bytes 1966088 | tf_op jit(solution)/shard_map/ppermute | solution.py:403
  100.0 17.0 %collective-permute-start.3 = (bf16[8,32,1280]{2,1,0:T(8,128)(2,1)S(1)}, bf16[8,32,1280]{2,1,0:T(8,128)(2,1)S(1)}, u32[]{:S(2)}, u32[]{:S(2)}) collective-permute-start(bf16[8,32,1280]{2,1,0:T(8,128)(2,1)S(1)} %collective-permute-done.refs_1_), channel_id=1, source_target_pairs={{0,4},{1,5},{2,6},{3,7},{4,8},{5,9},{6,10},{7,11},{8,12},{9,13},{1... | collective-permute-start | bytes 1966088 | tf_op jit(solution)/shard_map/ppermute | solution.py:403
  100.9 16.1 %collective-permute-start.7 = (bf16[16,32,640]{2,1,0:T(8,128)(2,1)S(1)}, bf16[16,32,640]{2,1,0:T(8,128)(2,1)S(1)}, u32[]{:S(2)}, u32[]{:S(2)}) collective-permute-start(bf16[16,32,640]{2,1,0:T(8,128)(2,1)S(1)} %all_to_all.11.refs_12_.refs_16_), channel_id=1, source_target_pairs={{0,48},{16,0},{32,16},{48,32},{64,112},{80,64},{96,80},{112,96},{1... | collective-permute-start | bytes 1966088 | tf_op jit(solution)/shard_map/ppermute | solution.py:404
  101.8 15.7 %collective-permute-start.6 = (bf16[16,32,640]{2,1,0:T(8,128)(2,1)S(1)}, bf16[16,32,640]{2,1,0:T(8,128)(2,1)}, u32[]{:S(2)}, u32[]{:S(2)}) collective-permute-start(bf16[16,32,640]{2,1,0:T(8,128)(2,1)S(1)} %all_to_all.11.refs_12_.refs_16_), channel_id=1, source_target_pairs={{0,16},{16,32},{32,48},{48,0},{64,80},{80,96},{96,112},{112,64},{1... | collective-permute-start | bytes 1966088 | tf_op jit(solution)/shard_map/ppermute | solution.py:404
  102.4 15.6 %collective-permute-start.5 = (bf16[16,32,640]{2,1,0:T(8,128)(2,1)S(1)}, bf16[16,32,640]{2,1,0:T(8,128)(2,1)S(1)}, u32[]{:S(2)}, u32[]{:S(2)}) collective-permute-start(bf16[16,32,640]{2,1,0:T(8,128)(2,1)S(1)} %all_to_all.11.refs_12_.refs_16_), channel_id=1, source_target_pairs={{0,64},{16,80},{32,96},{48,112},{64,0},{80,16},{96,32},{112,48},{1... | collective-permute-start | bytes 1966088 | tf_op jit(solution)/shard_map/ppermute | solution.py:416
  118.0 4.8 %collective-permute-start.12 = (bf16[8,32,1280]{2,1,0:T(8,128)(2,1)S(1)}, bf16[8,32,1280]{2,1,0:T(8,128)(2,1)S(1)}, u32[]{:S(2)}, u32[]{:S(2)}) collective-permute-start(bf16[8,32,1280]{2,1,0:T(8,128)(2,1)S(1)} %all_to_all.10.refs_0_), channel_id=1, source_target_pairs={{0,1},{1,0},{2,3},{3,2},{4,5},{5,4},{6,7},{7,6},{8,9},{9,8},{10,11... | collective-permute-start | bytes 1966088 | tf_op jit(solution)/shard_map/ppermute | solution.py:405
  121.1 3.5 %collective-permute-start.13 = (bf16[8,32,1280]{2,1,0:T(8,128)(2,1)S(1)}, bf16[8,32,1280]{2,1,0:T(8,128)(2,1)S(1)}, u32[]{:S(2)}, u32[]{:S(2)}) collective-permute-start(bf16[8,32,1280]{2,1,0:T(8,128)(2,1)S(1)} %collective-permute-done.refs_1_), channel_id=1, source_target_pairs={{0,1},{1,0},{2,3},{3,2},{4,5},{5,4},{6,7},{7,6},{8,9},{9,8},{10,11... | collective-permute-start | bytes 1966088 | tf_op jit(solution)/shard_map/ppermute | solution.py:405
  121.1 5.5 %collective-permute-start.15 = (bf16[8,32,1280]{2,1,0:T(8,128)(2,1)S(1)}, bf16[8,32,1280]{2,1,0:T(8,128)(2,1)S(1)}, u32[]{:S(2)}, u32[]{:S(2)}) collective-permute-start(bf16[8,32,1280]{2,1,0:T(8,128)(2,1)S(1)} %collective-permute-done.2.refs_3_), channel_id=1, source_target_pairs={{0,1},{1,0},{2,3},{3,2},{4,5},{5,4},{6,7},{7,6},{8,9},{9,8},{10,11... | collective-permute-start | bytes 1966088 | tf_op jit(solution)/shard_map/ppermute | solution.py:405
  121.6 17.5 %collective-permute-start.14 = (bf16[8,32,1280]{2,1,0:T(8,128)(2,1)S(1)}, bf16[8,32,1280]{2,1,0:T(8,128)(2,1)S(1)}, u32[]{:S(2)}, u32[]{:S(2)}) collective-permute-start(bf16[8,32,1280]{2,1,0:T(8,128)(2,1)S(1)} %collective-permute-done.1.refs_2_), channel_id=1, source_target_pairs={{0,1},{1,0},{2,3},{3,2},{4,5},{5,4},{6,7},{7,6},{8,9},{9,8},{10,11... | collective-permute-start | bytes 1966088 | tf_op jit(solution)/shard_map/ppermute | solution.py:405
  121.6 17.5 %collective-permute-start.8 = (bf16[8,32,1280]{2,1,0:T(8,128)(2,1)S(1)}, bf16[8,32,1280]{2,1,0:T(8,128)(2,1)}, u32[]{:S(2)}, u32[]{:S(2)}) collective-permute-start(bf16[8,32,1280]{2,1,0:T(8,128)(2,1)S(1)} %collective-permute-done.1.refs_2_), channel_id=1, source_target_pairs={{0,4},{1,5},{2,6},{3,7},{4,8},{5,9},{6,10},{7,11},{8,12},{9,13},{1... | collective-permute-start | bytes 1966088 | tf_op jit(solution)/shard_map/ppermute | solution.py:403
  122.8 16.3 %collective-permute-start.9 = (bf16[8,32,1280]{2,1,0:T(8,128)(2,1)}, bf16[8,32,1280]{2,1,0:T(8,128)(2,1)}, u32[]{:S(2)}, u32[]{:S(2)}) collective-permute-start(bf16[8,32,1280]{2,1,0:T(8,128)(2,1)} %collective-permute-done.4.refs_5_), channel_id=1, source_target_pairs={{0,12},{1,13},{2,14},{3,15},{4,0},{5,1},{6,2},{7,3},{8,4},{9,5},{1... | collective-permute-start | bytes 1966088 | tf_op jit(solution)/shard_map/ppermute | solution.py:403
  124.5 15.6 %collective-permute-start.11 = (bf16[16,32,640]{2,1,0:T(8,128)(2,1)S(1)}, bf16[16,32,640]{2,1,0:T(8,128)(2,1)}, u32[]{:S(2)}, u32[]{:S(2)}) collective-permute-start(bf16[16,32,640]{2,1,0:T(8,128)(2,1)S(1)} %collective-permute-done.5.refs_13_.refs_17_), channel_id=1, source_target_pairs={{0,48},{16,0},{32,16},{48,32},{64,112},{80,64},{96,80},{112,96},{1... | collective-permute-start | bytes 1966088 | tf_op jit(solution)/shard_map/ppermute | solution.py:404
  126.6 16.4 %collective-permute-start.10 = (bf16[16,32,640]{2,1,0:T(8,128)(2,1)S(1)}, bf16[16,32,640]{2,1,0:T(8,128)(2,1)S(1)}, u32[]{:S(2)}, u32[]{:S(2)}) collective-permute-start(bf16[16,32,640]{2,1,0:T(8,128)(2,1)S(1)} %collective-permute-done.5.refs_13_.refs_17_), channel_id=1, source_target_pairs={{0,16},{16,32},{32,48},{48,0},{64,80},{80,96},{96,112},{112,64},{1... | collective-permute-start | bytes 1966088 | tf_op jit(solution)/shard_map/ppermute | solution.py:404
  143.0 3.8 %collective-permute-start.16 = (bf16[8,32,1280]{2,1,0:T(8,128)(2,1)S(1)}, bf16[8,32,1280]{2,1,0:T(8,128)(2,1)S(1)}, u32[]{:S(2)}, u32[]{:S(2)}) collective-permute-start(bf16[8,32,1280]{2,1,0:T(8,128)(2,1)S(1)} %collective-permute-done.3.refs_4_), channel_id=1, source_target_pairs={{0,1},{1,0},{2,3},{3,2},{4,5},{5,4},{6,7},{7,6},{8,9},{9,8},{10,11... | collective-permute-start | bytes 1966088 | tf_op jit(solution)/shard_map/ppermute | solution.py:405
  145.0 18.8 %collective-permute-start.17 = (bf16[8,32,1280]{2,1,0:T(8,128)(2,1)}, bf16[8,32,1280]{2,1,0:T(8,128)(2,1)}, u32[]{:S(2)}, u32[]{:S(2)}) collective-permute-start(bf16[8,32,1280]{2,1,0:T(8,128)(2,1)} %collective-permute-done.4.refs_5_), channel_id=1, source_target_pairs={{0,1},{1,0},{2,3},{3,2},{4,5},{5,4},{6,7},{7,6},{8,9},{9,8},{10,11... | collective-permute-start | bytes 1966088 | tf_op jit(solution)/shard_map/ppermute | solution.py:405
  145.0 18.7 %collective-permute-start.18 = (bf16[8,32,1280]{2,1,0:T(8,128)(2,1)}, bf16[8,32,1280]{2,1,0:T(8,128)(2,1)}, u32[]{:S(2)}, u32[]{:S(2)}) collective-permute-start(bf16[8,32,1280]{2,1,0:T(8,128)(2,1)} %collective-permute-done.8.refs_6_), channel_id=1, source_target_pairs={{0,1},{1,0},{2,3},{3,2},{4,5},{5,4},{6,7},{7,6},{8,9},{9,8},{10,11... | collective-permute-start | bytes 1966088 | tf_op jit(solution)/shard_map/ppermute | solution.py:405
  145.5 18.3 %collective-permute-start.19 = (bf16[8,32,1280]{2,1,0:T(8,128)(2,1)}, bf16[8,32,1280]{2,1,0:T(8,128)(2,1)}, u32[]{:S(2)}, u32[]{:S(2)}) collective-permute-start(bf16[8,32,1280]{2,1,0:T(8,128)(2,1)} %collective-permute-done.9.refs_7_), channel_id=1, source_target_pairs={{0,1},{1,0},{2,3},{3,2},{4,5},{5,4},{6,7},{7,6},{8,9},{9,8},{10,11... | collective-permute-start | bytes 1966088 | tf_op jit(solution)/shard_map/ppermute | solution.py:405
  145.6 18.2 %collective-permute-start.20 = (bf16[16,32,640]{2,1,0:T(8,128)(2,1)}, bf16[16,32,640]{2,1,0:T(8,128)(2,1)}, u32[]{:S(2)}, u32[]{:S(2)}) collective-permute-start(bf16[16,32,640]{2,1,0:T(8,128)(2,1)} %collective-permute-done.6.refs_14_.refs_18_), channel_id=1, source_target_pairs={{0,16},{16,32},{32,48},{48,0},{64,80},{80,96},{96,112},{112,64},{1... | collective-permute-start | bytes 1966088 | tf_op jit(solution)/shard_map/ppermute | solution.py:404
  146.8 17.0 %collective-permute-start.21 = (bf16[16,32,640]{2,1,0:T(8,128)(2,1)}, bf16[16,32,640]{2,1,0:T(8,128)(2,1)}, u32[]{:S(2)}, u32[]{:S(2)}) collective-permute-start(bf16[16,32,640]{2,1,0:T(8,128)(2,1)} %collective-permute-done.11.refs_17_.refs_21_), channel_id=1, source_target_pairs={{0,48},{16,0},{32,16},{48,32},{64,112},{80,64},{96,80},{112,96},{1... | collective-permute-start | bytes 1966088 | tf_op jit(solution)/shard_map/ppermute | solution.py:404
  (12 other events, 324.6 us)

commit v5 on v4

--- a/solution.py
+++ b/solution.py
@@ -87,8 +87,9 @@
     row_blocks,
     col_blocks,
     num_gvec,
-    val_rows,
-    cond_rows,
+    pairs_all,
+    val_band,
+    cond_band,
     where_row,
     val_ref,
     cond_ref,
@@ -96,7 +97,8 @@
     t2_ref,
     t3_ref,
     perm_ref,
-    scale_ref,
+    val_energy,
+    cond_energy,
     gvec_ref,
     rows_ref,
     cols_ref,
@@ -121,8 +123,8 @@
     lax.fori_loop(0, XCH * GY // 64, unpack, 0)
 
     def pair_first(p, carry):
-        vb = val_rows[p]
-        cb = cond_rows[p]
+        vb = val_band[p] & (BANDS - 1)
+        cb = cond_band[p] & (BANDS - 1)
         for half in range(XCH // 2):
             parts = []
             for x in (2 * half, 2 * half + 1):
@@ -171,7 +173,17 @@
         lax.fori_loop(0, NKY, second_stage, 0, unroll=17)
 
         lane = lax.broadcasted_iota(jnp.int32, (1, GROUPS * LANES), 1) % LANES
-        scale = scale_ref[...]
+        every = lax.broadcasted_iota(jnp.int32, val_energy.shape, 1)
+        place = lax.broadcasted_iota(jnp.int32, (1, GROUPS * LANES), 1)
+        owner = (place >> 7) * GROUP + ((place & (LANES // 2 - 1)) >> 3)
+        gap = jnp.ones((1, GROUPS * LANES), jnp.float32)
+        for p in range(PAIR_DEV):
+            upper = jnp.where(every == cond_band[p], cond_energy[...], 0.0)
+            lower = jnp.where(every == val_band[p], val_energy[...], 0.0)
+            found = jnp.sum(upper - lower, axis=1, keepdims=True)
+            gap = jnp.where(owner == p, found, gap)
+        factor = 4.0 / (math.sqrt(pairs_all) * gap)
+        scale = jnp.sqrt(factor) * (1.0 / math.sqrt(GX * GY * GZ))
         swapped = jnp.where(lane < LANES // 2, scale, -scale)
 
         def third_stage(b, carry):
@@ -246,12 +258,13 @@
     return kx * flip + HX, ky * flip, kz * flip, flip
 
 
-def pair_elements(val_rows, cond_rows, scale, val, cond, gvec, row_blocks, col_blocks):
+def pair_elements(
+    val_band, cond_band, val, cond, val_energy, cond_energy, gvec, row_blocks, col_blocks
+):
+    pairs_all = val_band.shape[0] * row_blocks * col_blocks
     num_gvec = gvec.shape[0]
     kx, ky, kz, _ = signed_parts(gvec)
     where_row = (ky * OCTS + (kx >> 3)) * 2 * KZP + jnp.where(kz < 0, KZP - kz, kz)
-    lanes = jnp.repeat(scale, 8).reshape(GROUPS, 1, -1)
-    lanes = jnp.tile(lanes, (1, 2, 1)).reshape(1, -1)
     t1, t2, t3, perm = tables()
     whole = lambda shape: pl.BlockSpec(shape, lambda i, *_: (0,) * len(shape))
     width = XCH * GY * GZ
@@ -260,7 +273,7 @@
         jax.ShapeDtypeStruct((col_blocks, 2 * PAIR_DEV, num_gvec // col_blocks), jnp.bfloat16),
     ]
     return pl.pallas_call(
-        functools.partial(elements_kernel, row_blocks, col_blocks, num_gvec),
+        functools.partial(elements_kernel, row_blocks, col_blocks, num_gvec, pairs_all),
         out_shape=outs,
         grid_spec=pltpu.PrefetchScalarGridSpec(
             num_scalar_prefetch=3,
@@ -272,7 +285,8 @@
                 whole(t2.shape),
                 whole(t3.shape),
                 whole(perm.shape),
-                whole((1, GROUPS * LANES)),
+                whole((1, val_energy.shape[0])),
+                whole((1, cond_energy.shape[0])),
                 whole((1, num_gvec)),
             ],
             out_specs=[whole(o.shape) for o in outs],
@@ -286,19 +300,31 @@
             ],
         ),
         compiler_params=pltpu.CompilerParams(vmem_limit_bytes=60 * 1024 * 1024),
-    )(val_rows, cond_rows, where_row, val, cond, t1, t2, t3, perm, lanes, gvec[None, :])
-
-
-def product_kernel(pairs, chunk_row, chunk_col, *refs):
-    lefts, rights, before = refs[: len(LEFT)], refs[len(LEFT) : COUNT], refs[COUNT:-4]
+    )(
+        val_band,
+        cond_band,
+        where_row,
+        val,
+        cond,
+        t1,
+        t2,
+        t3,
+        perm,
+        val_energy[None, :],
+        cond_energy[None, :],
+        gvec[None, :],
+    )
+
+
+def product_kernel(pairs, chunk_row, chunk_col, lefts, rights, width, *refs):
+    before = refs[:-4]
     real_ref, imag_ref, lhs, table = refs[-4:]
-    width = rights[0].shape[2]
     rows = 2 * PAIR_DEV
 
     @pl.when(pl.program_id(0) == 0)
     def _():
         for at, (i, k) in enumerate(pairs):
-            value = rights[k][chunk_col[i]]
+            value = rights(k, i, chunk_col)
             first = slice(at * rows, at * rows + PAIR_DEV)
             last = slice(at * rows + PAIR_DEV, (at + 1) * rows)
             table[first, :width] = -value[:PAIR_DEV]
@@ -307,7 +333,7 @@
             table[last, width:] = -value[:PAIR_DEV]
 
     for at, (i, k) in enumerate(pairs):
-        lhs[at * rows : (at + 1) * rows, :] = lefts[i][chunk_row[k]]
+        lhs[at * rows : (at + 1) * rows, :] = lefts(i, k, chunk_row)
     out = mm(lhs[...], table[...], (((0,), (0,)), ((), ())))
     real, imag = out[:, :width], out[:, width:]
     if before:
@@ -320,44 +346,68 @@
 HALF = [(0, 0), (0, 1), (-1, 0), (1, 0), (-1, 1), (1, 1), (2, 0), (2, 1)]
 LEFT = [(dz, dx, core) for core in range(2) for dz, dx in HALF]
 RIGHT = [(dx, dy) for dy, dx in HALF]
-COUNT = len(LEFT) + len(RIGHT)
-TILE = 256
-
-
-def panel_product(lefts, rights, pairs, before=()):
+FEW = 2
+
+
+def panel_product(lefts, rights, pairs, tile, before=()):
     row, col = lax.axis_index("row"), lax.axis_index("col")
     chunk_col = jnp.stack(
         [(col // 4 + dz) % 4 * 4 + (col // 2 % 2 ^ dx) * 2 + (col % 2 ^ dc) for dz, dx, dc in LEFT]
     )
     chunk_row = jnp.stack([(row // 4 ^ dx) * 4 + (row % 4 + dy) % 4 for dx, dy in RIGHT])
-    left_at, right_at = sorted({i for i, _ in pairs}), sorted({k for _, k in pairs})
     sources, rows, height = lefts[0].shape
     width = rights[0].shape[2]
     depth = len(pairs) * rows
     out = jax.ShapeDtypeStruct((height, width), jnp.float32)
-    out_spec = pl.BlockSpec((TILE, width), lambda m, *_: (m, 0))
+    out_spec = pl.BlockSpec((tile, width), lambda m, *_: (m, 0))
+
+    keys, specs = [], []
+    for i in sorted({i for i, _ in pairs}):
+        used = [k for j, k in pairs if j == i]
+        if len(used) > FEW:
+            keys.append(("left", i))
+            specs.append(pl.BlockSpec((sources, rows, tile), lambda m, *_: (0, 0, m)))
+        for k in used if len(used) <= FEW else []:
+            keys.append(("left", i, k))
+            specs.append(pl.BlockSpec((1, rows, tile), lambda m, at, _, k=k: (at[k], 0, m)))
+    for k in sorted({k for _, k in pairs}):
+        used = [i for i, j in pairs if j == k]
+        if len(used) > 2 * FEW:
+            keys.append(("right", k))
+            specs.append(pl.BlockSpec(rights[0].shape, lambda m, *_: (0, 0, 0)))
+        for i in used if len(used) <= 2 * FEW else []:
+            keys.append(("right", k, i))
+            specs.append(pl.BlockSpec((1, rows, width), lambda m, _, at, i=i: (at[i], 0, 0)))
+    arrays = [(lefts if key[0] == "left" else rights)[key[1]] for key in keys]
 
     def kernel(chunk_row, chunk_col, *refs):
-        left_refs = dict(zip(left_at, refs))
-        refs = refs[len(left_at) :]
-        right_refs = dict(zip(right_at, refs))
-        refs = refs[len(right_at) :]
-        all_left = [left_refs.get(i) for i in range(len(LEFT))]
-        all_right = [right_refs.get(k) for k in range(len(RIGHT))]
-        product_kernel(pairs, chunk_row, chunk_col, *all_left, *all_right, *refs)
+        held = dict(zip(keys, refs))
+
+        def part(side, chunk, other, at):
+            if (side, chunk) in held:
+                return held[side, chunk][at[other]]
+            return held[side, chunk, other][0]
+
+        product_kernel(
+            pairs,
+            chunk_row,
+            chunk_col,
+            functools.partial(part, "left"),
+            functools.partial(part, "right"),
+            width,
+            *refs[len(keys) :],
+        )
 
     return pl.pallas_call(
         kernel,
         out_shape=[out, out],
         grid_spec=pltpu.PrefetchScalarGridSpec(
             num_scalar_prefetch=2,
-            grid=(height // TILE,),
-            in_specs=[pl.BlockSpec((sources, rows, TILE), lambda m, *_: (0, 0, m))] * len(left_at)
-            + [pl.BlockSpec(rights[0].shape, lambda m, *_: (0, 0, 0))] * len(right_at)
-            + [out_spec] * len(before),
+            grid=(height // tile,),
+            in_specs=specs + [out_spec] * len(before),
             out_specs=[out_spec] * 2,
             scratch_shapes=[
-                pltpu.VMEM((depth, TILE), jnp.bfloat16),
+                pltpu.VMEM((depth, tile), jnp.bfloat16),
                 pltpu.VMEM((depth, 2 * width), jnp.bfloat16),
             ],
         ),
@@ -365,8 +415,7 @@
     )(
         chunk_row,
         chunk_col,
-        *[lefts[i] for i in left_at],
-        *[rights[k] for k in right_at],
+        *arrays,
         *before,
     )
 
@@ -377,25 +426,21 @@
 
 def ring_y(step):
     return [(r, r // 4 * 4 + (r + step) % 4) for r in range(8)]
-
-
-def pick_values(indices, values):
-    match = indices[:, None] == jnp.arange(values.shape[0], dtype=jnp.int32)[None, :]
-    return jnp.sum(jnp.where(match, values[None, :], 0.0), axis=1)
 
 
 def local(val_band, cond_band, val_orbitals, cond_orbitals, val_energy, cond_energy, gvec_index):
     row_count = lax.axis_size("row")
     col_count = lax.axis_size("col")
-    pair_dev = val_band.shape[0]
-    pairs_all = pair_dev * row_count * col_count
-    energy_gap = pick_values(cond_band, cond_energy) - pick_values(val_band, val_energy)
-    factor = 4.0 / (math.sqrt(pairs_all) * energy_gap)
-    scale = jnp.sqrt(factor) / math.sqrt(GX * GY * GZ)
-    val_rows = val_band % val_orbitals.shape[0]
-    cond_rows = cond_band % cond_orbitals.shape[0]
     rows_part, cols_part = pair_elements(
-        val_rows, cond_rows, scale, val_orbitals, cond_orbitals, gvec_index, row_count, col_count
+        val_band,
+        cond_band,
+        val_orbitals,
+        cond_orbitals,
+        val_energy,
+        cond_energy,
+        gvec_index,
+        row_count,
+        col_count,
     )
     swap_core = [(c, c ^ 1) for c in range(col_count)]
     swap_low = [(c, c ^ 2) for c in range(col_count)]
@@ -423,8 +468,8 @@
     crossed_last = [cross(value) for value in left[4:]]
     early = [(i, k) for i in range(12) for k in range(6)]
     late = [(i, k) for i in range(16) for k in range(8) if (i, k) not in early]
-    partial = panel_product(left + crossed, right, early)
-    real, imag = panel_product(left + crossed + crossed_last, right + right_ends, late, partial)
+    partial = panel_product(left + crossed, right, early, 256)
+    real, imag = panel_product(left + crossed + crossed_last, right + right_ends, late, 640, partial)
     return (real, imag)
 
 

time: 180 us -> 175 us (0.972)
  Pallas kernels: 74.6 us -> 72.3 us
  other arithmetic: 3.57 us -> 1.43 us
    pallas_call x2, Pallas kernels: 29.2 us -> 27 us  [panel_product(): pl.pallas_call(kernel, out_shape=[out, out], grid_spec=pltpu.PrefetchScal...]
where the time goes in v5:
time: 175 us
  Pallas kernels  72.3 us (41%)
  blocking collectives  44.2 us (25%)
  waiting for transfers between devices  33.9 us (19%)
  starting transfers between devices  20.2 us (12%)
    pallas_call x1, Pallas kernels, pair_elements(): pl.pallas_call(functools.partial(elements_kernel, row_blocks, col_blocks,...  45.3 us
    pallas_call x2, Pallas kernels, panel_product(): pl.pallas_call(kernel, out_shape=[out, out], grid_spec=pltpu.PrefetchScal...  27 us
    ppermute x6, waiting for transfers between devices, local(): along_z = lambda value, step: lax.ppermute(value, 'col', ring_z(step))  26.4 us
    all_to_all x1, blocking collectives, local(): lax.all_to_all(cols_part, 'col', split_axis=0, concat_axis=0, tiled=True)  25.5 us
    all_to_all x1, blocking collectives, local(): lax.all_to_all(rows_part, 'row', split_axis=0, concat_axis=0, tiled=True)  18.7 us
    ppermute x6, starting transfers between devices, local(): along_z = lambda value, step: lax.ppermute(value, 'col', ring_z(step))  9.11 us
    ppermute x8, starting transfers between devices, local(): cross = lambda value: lax.ppermute(value, 'col', swap_core)  6.1 us
    ppermute x6, starting transfers between devices, local(): along_y = lambda value, step: lax.ppermute(value, 'row', ring_y(step))  4.26 us
  transfers between devices with their start and end apart: 22, of which 9 were waited for; matrix products, arithmetic and copies ran while one was open for 1% of the time, Pallas kernels for 8%

profile of v5, /device:TPU:1, one launch (start us, length us, event | category | flops | bytes accessed | tf_op | source)
XLA Modules:
  0.0 174.6 jit_solution(4910855066161281312)
XLA Ops:
  0.6 1.4 fusion.3.where_row
  2.1 45.3 %shard_map.122 = (bf16[8,32,1280]{2,1,0:T(8,128)(2,1)}, bf16[16,32,640]{2,1,0:T(8,128)(2,1)}) custom-call(s32[16]{0:T(128)} %val_band.1, s32[16]{0:T(128)} %cond_band.1, s32[10240]{0:T(1024)} %fusion.3.where_row, bf16[8,524288]{1,0:T(8,128)(2,1)} %val_ref.1, bf16[8,524288]{1,0:T(8,128)(2,1)} %cond_ref.1, bf16[80,128]{1,0:T(8,128)(2,1)} %constant.521.clone.t1_ref, ...), custom_call_target="tpu_custom_call" | custom-call | tf_op jit(solution)/shard_map/pallas_call | solution.py:275
  47.4 18.7 %all_to_all.10.refs_0_.refs_1_ = bf16[8,32,1280]{2,1,0:T(8,128)(2,1)S(1)} all-to-all(bf16[8,32,1280]{2,1,0:T(8,128)(2,1)} %get-tuple-element.42), channel_id=1, replica_groups=mesh['row'=8,'col'=16] {'row'}, dimensions={0} | all-to-all | bytes 1310720 | tf_op jit(solution)/shard_map/all_to_all | solution.py:453
  66.1 5.2 %collective-permute-start.2 = (bf16[8,32,1280]{2,1,0:T(8,128)(2,1)S(1)}, bf16[8,32,1280]{2,1,0:T(8,128)(2,1)S(1)}, u32[]{:S(2)}, u32[]{:S(2)}) collective-permute-start(bf16[8,32,1280]{2,1,0:T(8,128)(2,1)S(1)} %all_to_all.10.refs_0_.refs_1_), channel_id=1, source_target_pairs={{0,12},{1,13},{2,14},{3,15},{4,0},{5,1},{6,2},{7,3},{8,4},{9,5},{1... | collective-permute-start | bytes 1966088 | tf_op jit(solution)/shard_map/ppermute | solution.py:448
  71.3 25.5 %all_to_all.11.refs_12_.refs_28_.refs_29_.refs_30_.refs_31_ = bf16[16,32,640]{2,1,0:T(8,128)(2,1)S(1)} all-to-all(bf16[16,32,640]{2,1,0:T(8,128)(2,1)} %get-tuple-element.44), channel_id=1, replica_groups=mesh['row'=8,'col'=16] {'col'}, dimensions={0} | all-to-all | bytes 1310720 | tf_op jit(solution)/shard_map/all_to_all | solution.py:457
  97.4 0.9 collective-permute-start.3
  99.0 0.8 collective-permute-start.6
  99.8 0.7 collective-permute-start.5
  100.5 11.6 %collective-permute-done.4.refs_5_.refs_10_.refs_11_ = bf16[8,32,1280]{2,1,0:T(8,128)(2,1)} collective-permute-done((bf16[8,32,1280]{2,1,0:T(8,128)(2,1)S(1)}, bf16[8,32,1280]{2,1,0:T(8,128)(2,1)}, u32[]{:S(2)}, u32[]{:S(2)}) %collective-permute-start.4) | collective-permute-done | bytes 655392 | tf_op jit(solution)/shard_map/ppermute | solution.py:448
  112.2 2.1 %collective-permute-done.3.refs_4_.refs_8_.refs_9_ = bf16[8,32,1280]{2,1,0:T(8,128)(2,1)S(1)} collective-permute-done((bf16[8,32,1280]{2,1,0:T(8,128)(2,1)S(1)}, bf16[8,32,1280]{2,1,0:T(8,128)(2,1)S(1)}, u32[]{:S(2)}, u32[]{:S(2)}) %collective-permute-start.3) | collective-permute-done | bytes 655392 | tf_op jit(solution)/shard_map/ppermute | solution.py:448
  114.6 0.8 collective-permute-done.5.refs_13_.refs_32_.refs_33_.refs_34_.refs_35_
  115.4 3.1 %collective-permute-start.12 = (bf16[8,32,1280]{2,1,0:T(8,128)(2,1)S(1)}, bf16[8,32,1280]{2,1,0:T(8,128)(2,1)S(1)}, u32[]{:S(2)}, u32[]{:S(2)}) collective-permute-start(bf16[8,32,1280]{2,1,0:T(8,128)(2,1)S(1)} %all_to_all.10.refs_0_.refs_1_), channel_id=1, source_target_pairs={{0,1},{1,0},{2,3},{3,2},{4,5},{5,4},{6,7},{7,6},{8,9},{9,8},{10,11... | collective-permute-start | bytes 1966088 | tf_op jit(solution)/shard_map/ppermute | solution.py:450
  119.0 0.7 collective-permute-start.8
  120.2 1.8 %collective-permute-start.9 = (bf16[8,32,1280]{2,1,0:T(8,128)(2,1)}, bf16[8,32,1280]{2,1,0:T(8,128)(2,1)}, u32[]{:S(2)}, u32[]{:S(2)}) collective-permute-start(bf16[8,32,1280]{2,1,0:T(8,128)(2,1)} %collective-permute-done.4.refs_5_.refs_10_.refs_11_), channel_id=1, source_target_pairs={{0,12},{1,13},{2,14},{3,15},{4,0},{5,1},{6,2},{7,3},{8,4},{9,5},{1... | collective-permute-start | bytes 1966088 | tf_op jit(solution)/shard_map/ppermute | solution.py:448
  122.0 1.8 %collective-permute-start.11 = (bf16[16,32,640]{2,1,0:T(8,128)(2,1)S(1)}, bf16[16,32,640]{2,1,0:T(8,128)(2,1)S(1)}, u32[]{:S(2)}, u32[]{:S(2)}) collective-permute-start(bf16[16,32,640]{2,1,0:T(8,128)(2,1)S(1)} %collective-permute-done.5.refs_13_.refs_32_.refs_33_.refs_34_.refs_35_), channel_id=1, source_target_pairs={{0,48},{16,0},{32,16},{48,32},{64,112},{80,64},{96,80},{112,96},{1... | collective-permute-start | bytes 1966088 | tf_op jit(solution)/shard_map/ppermute | solution.py:449
  123.9 12.6 %collective-permute-done.9.refs_7_.refs_14_.refs_15_ = bf16[8,32,1280]{2,1,0:T(8,128)(2,1)} collective-permute-done((bf16[8,32,1280]{2,1,0:T(8,128)(2,1)}, bf16[8,32,1280]{2,1,0:T(8,128)(2,1)}, u32[]{:S(2)}, u32[]{:S(2)}) %collective-permute-start.9) | collective-permute-done | bytes 655392 | tf_op jit(solution)/shard_map/ppermute | solution.py:448
  136.5 1.0 collective-permute-done.11.refs_17_.refs_48_.refs_49_.refs_50_.refs_51_
  137.4 2.8 %collective-permute-done.10.refs_16_.refs_44_.refs_45_.refs_46_.refs_47_ = bf16[16,32,640]{2,1,0:T(8,128)(2,1)S(1)} collective-permute-done((bf16[16,32,640]{2,1,0:T(8,128)(2,1)S(1)}, bf16[16,32,640]{2,1,0:T(8,128)(2,1)S(1)}, u32[]{:S(2)}, u32[]{:S(2)}) %collective-permute-start.10) | collective-permute-done | bytes 655392 | tf_op jit(solution)/shard_map/ppermute | solution.py:449
  140.3 2.0 %collective-permute-start.16 = (bf16[8,32,1280]{2,1,0:T(8,128)(2,1)S(1)}, bf16[8,32,1280]{2,1,0:T(8,128)(2,1)S(1)}, u32[]{:S(2)}, u32[]{:S(2)}) collective-permute-start(bf16[8,32,1280]{2,1,0:T(8,128)(2,1)S(1)} %collective-permute-done.3.refs_4_.refs_8_.refs_9_), channel_id=1, source_target_pairs={{0,1},{1,0},{2,3},{3,2},{4,5},{5,4},{6,7},{7,6},{8,9},{9,8},{10,11... | collective-permute-start | bytes 1966088 | tf_op jit(solution)/shard_map/ppermute | solution.py:450
  142.8 2.1 %collective-permute-done.16.refs_24_ = bf16[8,32,1280]{2,1,0:T(8,128)(2,1)S(1)} collective-permute-done((bf16[8,32,1280]{2,1,0:T(8,128)(2,1)S(1)}, bf16[8,32,1280]{2,1,0:T(8,128)(2,1)S(1)}, u32[]{:S(2)}, u32[]{:S(2)}) %collective-permute-start.16) | collective-permute-done | bytes 655392 | tf_op jit(solution)/shard_map/ppermute | solution.py:450
  144.9 0.9 collective-permute-start.21
  146.6 0.7 stack.129.chunk_col
  147.3 13.9 %shard_map.123 = (f32[1280,640]{1,0:T(8,128)}, f32[1280,640]{1,0:T(8,128)}) custom-call(s32[8]{0:T(128)} %stack.112.chunk_row, s32[16]{0:T(128)} %stack.129.chunk_col, bf16[8,32,1280]{2,1,0:T(8,128)(2,1)} %copy-done.6, bf16[8,32,1280]{2,1,0:T(8,128)(2,1)} %copy-done.9, bf16[8,32,1280]{2,1,0:T(8,128)(2,1)} %copy-done.8, bf16[8,32,1280]{2,1,0:T(8,128)(2,1)} %copy-done.7, ...), custom_call_target="tpu_custom_call" | custom-call | tf_op jit(solution)/shard_map/pallas_call | solution.py:401
  161.3 13.1 %shard_map.124 = (f32[1280,640]{1,0:T(8,128)}, f32[1280,640]{1,0:T(8,128)}) custom-call(s32[8]{0:T(128)} %stack.112.chunk_row, s32[16]{0:T(128)} %stack.129.chunk_col, bf16[8,32,1280]{2,1,0:T(8,128)(2,1)} %copy-done.6, bf16[8,32,1280]{2,1,0:T(8,128)(2,1)} %copy-done.6, bf16[8,32,1280]{2,1,0:T(8,128)(2,1)} %copy-done.9, bf16[8,32,1280]{2,1,0:T(8,128)(2,1)} %copy-done.9, ...), custom_call_target="tpu_custom_call" | custom-call | tf_op jit(solution)/shard_map/pallas_call | solution.py:401
  (60 shorter events, 3.9 us)
Async XLA Ops:
  66.1 57.7 %copy-start.6 = (bf16[8,32,1280]{2,1,0:T(8,128)(2,1)}, bf16[8,32,1280]{2,1,0:T(8,128)(2,1)S(1)}, u32[]{:S(2)}) copy-start(bf16[8,32,1280]{2,1,0:T(8,128)(2,1)S(1)} %all_to_all.10.refs_0_.refs_1_) | copy-start | bytes 1966084
  66.1 30.7 %collective-permute-start.2 = (bf16[8,32,1280]{2,1,0:T(8,128)(2,1)S(1)}, bf16[8,32,1280]{2,1,0:T(8,128)(2,1)S(1)}, u32[]{:S(2)}, u32[]{:S(2)}) collective-permute-start(bf16[8,32,1280]{2,1,0:T(8,128)(2,1)S(1)} %all_to_all.10.refs_0_.refs_1_), channel_id=1, source_target_pairs={{0,12},{1,13},{2,14},{3,15},{4,0},{5,1},{6,2},{7,3},{8,4},{9,5},{1... | collective-permute-start | bytes 1966088 | tf_op jit(solution)/shard_map/ppermute | solution.py:448
  71.3 25.5 %collective-permute-start.1 = (bf16[8,32,1280]{2,1,0:T(8,128)(2,1)S(1)}, bf16[8,32,1280]{2,1,0:T(8,128)(2,1)S(1)}, u32[]{:S(2)}, u32[]{:S(2)}) collective-permute-start(bf16[8,32,1280]{2,1,0:T(8,128)(2,1)S(1)} %all_to_all.10.refs_0_.refs_1_), channel_id=1, source_target_pairs={{0,4},{1,5},{2,6},{3,7},{4,8},{5,9},{6,10},{7,11},{8,12},{9,13},{1... | collective-permute-start | bytes 1966088 | tf_op jit(solution)/shard_map/ppermute | solution.py:448
  71.3 25.5 %collective-permute-start = (bf16[8,32,1280]{2,1,0:T(8,128)(2,1)S(1)}, bf16[8,32,1280]{2,1,0:T(8,128)(2,1)S(1)}, u32[]{:S(2)}, u32[]{:S(2)}) collective-permute-start(bf16[8,32,1280]{2,1,0:T(8,128)(2,1)S(1)} %all_to_all.10.refs_0_.refs_1_), channel_id=1, source_target_pairs={{0,2},{1,3},{2,0},{3,1},{4,6},{5,7},{6,4},{7,5},{8,10},{9,11},{10,... | collective-permute-start | bytes 1966088 | tf_op jit(solution)/shard_map/ppermute | solution.py:455
  96.8 50.5 %copy-start = (bf16[16,32,640]{2,1,0:T(8,128)(2,1)}, bf16[16,32,640]{2,1,0:T(8,128)(2,1)S(1)}, u32[]{:S(2)}) copy-start(bf16[16,32,640]{2,1,0:T(8,128)(2,1)S(1)} %all_to_all.11.refs_12_.refs_28_.refs_29_.refs_30_.refs_31_) | copy-start | bytes 1966084
  96.8 15.4 %collective-permute-start.4 = (bf16[8,32,1280]{2,1,0:T(8,128)(2,1)S(1)}, bf16[8,32,1280]{2,1,0:T(8,128)(2,1)}, u32[]{:S(2)}, u32[]{:S(2)}) collective-permute-start(bf16[8,32,1280]{2,1,0:T(8,128)(2,1)S(1)} %collective-permute-done.refs_1_.refs_2_.refs_3_), channel_id=1, source_target_pairs={{0,12},{1,13},{2,14},{3,15},{4,0},{5,1},{6,2},{7,3},{8,4},{9,5},{1... | collective-permute-start | bytes 1966088 | tf_op jit(solution)/shard_map/ppermute | solution.py:448
  97.4 16.9 %collective-permute-start.3 = (bf16[8,32,1280]{2,1,0:T(8,128)(2,1)S(1)}, bf16[8,32,1280]{2,1,0:T(8,128)(2,1)S(1)}, u32[]{:S(2)}, u32[]{:S(2)}) collective-permute-start(bf16[8,32,1280]{2,1,0:T(8,128)(2,1)S(1)} %collective-permute-done.refs_1_.refs_2_.refs_3_), channel_id=1, source_target_pairs={{0,4},{1,5},{2,6},{3,7},{4,8},{5,9},{6,10},{7,11},{8,12},{9,13},{1... | collective-permute-start | bytes 1966088 | tf_op jit(solution)/shard_map/ppermute | solution.py:448
  98.4 16.0 %collective-permute-start.7 = (bf16[16,32,640]{2,1,0:T(8,128)(2,1)S(1)}, bf16[16,32,640]{2,1,0:T(8,128)(2,1)S(1)}, u32[]{:S(2)}, u32[]{:S(2)}) collective-permute-start(bf16[16,32,640]{2,1,0:T(8,128)(2,1)S(1)} %all_to_all.11.refs_12_.refs_28_.refs_29_.refs_30_.refs_31_), channel_id=1, source_target_pairs={{0,48},{16,0},{32,16},{48,32},{64,112},{80,64},{96,80},{112,96},{1... | collective-permute-start | bytes 1966088 | tf_op jit(solution)/shard_map/ppermute | solution.py:449
  99.0 15.6 %collective-permute-start.6 = (bf16[16,32,640]{2,1,0:T(8,128)(2,1)S(1)}, bf16[16,32,640]{2,1,0:T(8,128)(2,1)S(1)}, u32[]{:S(2)}, u32[]{:S(2)}) collective-permute-start(bf16[16,32,640]{2,1,0:T(8,128)(2,1)S(1)} %all_to_all.11.refs_12_.refs_28_.refs_29_.refs_30_.refs_31_), channel_id=1, source_target_pairs={{0,16},{16,32},{32,48},{48,0},{64,80},{80,96},{96,112},{112,64},{1... | collective-permute-start | bytes 1966088 | tf_op jit(solution)/shard_map/ppermute | solution.py:449
  99.8 15.6 %collective-permute-start.5 = (bf16[16,32,640]{2,1,0:T(8,128)(2,1)S(1)}, bf16[16,32,640]{2,1,0:T(8,128)(2,1)S(1)}, u32[]{:S(2)}, u32[]{:S(2)}) collective-permute-start(bf16[16,32,640]{2,1,0:T(8,128)(2,1)S(1)} %all_to_all.11.refs_12_.refs_28_.refs_29_.refs_30_.refs_31_), channel_id=1, source_target_pairs={{0,64},{16,80},{32,96},{48,112},{64,0},{80,16},{96,32},{112,48},{1... | collective-permute-start | bytes 1966088 | tf_op jit(solution)/shard_map/ppermute | solution.py:461
  115.4 4.8 %collective-permute-start.12 = (bf16[8,32,1280]{2,1,0:T(8,128)(2,1)S(1)}, bf16[8,32,1280]{2,1,0:T(8,128)(2,1)S(1)}, u32[]{:S(2)}, u32[]{:S(2)}) collective-permute-start(bf16[8,32,1280]{2,1,0:T(8,128)(2,1)S(1)} %all_to_all.10.refs_0_.refs_1_), channel_id=1, source_target_pairs={{0,1},{1,0},{2,3},{3,2},{4,5},{5,4},{6,7},{7,6},{8,9},{9,8},{10,11... | collective-permute-start | bytes 1966088 | tf_op jit(solution)/shard_map/ppermute | solution.py:450
  118.5 3.5 %collective-permute-start.13 = (bf16[8,32,1280]{2,1,0:T(8,128)(2,1)S(1)}, bf16[8,32,1280]{2,1,0:T(8,128)(2,1)S(1)}, u32[]{:S(2)}, u32[]{:S(2)}) collective-permute-start(bf16[8,32,1280]{2,1,0:T(8,128)(2,1)S(1)} %collective-permute-done.refs_1_.refs_2_.refs_3_), channel_id=1, source_target_pairs={{0,1},{1,0},{2,3},{3,2},{4,5},{5,4},{6,7},{7,6},{8,9},{9,8},{10,11... | collective-permute-start | bytes 1966088 | tf_op jit(solution)/shard_map/ppermute | solution.py:450
  118.5 5.3 %collective-permute-start.15 = (bf16[8,32,1280]{2,1,0:T(8,128)(2,1)S(1)}, bf16[8,32,1280]{2,1,0:T(8,128)(2,1)S(1)}, u32[]{:S(2)}, u32[]{:S(2)}) collective-permute-start(bf16[8,32,1280]{2,1,0:T(8,128)(2,1)S(1)} %collective-permute-done.2.refs_3_.refs_6_.refs_7_), channel_id=1, source_target_pairs={{0,1},{1,0},{2,3},{3,2},{4,5},{5,4},{6,7},{7,6},{8,9},{9,8},{10,11... | collective-permute-start | bytes 1966088 | tf_op jit(solution)/shard_map/ppermute | solution.py:450
  119.0 17.5 %collective-permute-start.14 = (bf16[8,32,1280]{2,1,0:T(8,128)(2,1)S(1)}, bf16[8,32,1280]{2,1,0:T(8,128)(2,1)S(1)}, u32[]{:S(2)}, u32[]{:S(2)}) collective-permute-start(bf16[8,32,1280]{2,1,0:T(8,128)(2,1)S(1)} %collective-permute-done.1.refs_2_.refs_4_.refs_5_), channel_id=1, source_target_pairs={{0,1},{1,0},{2,3},{3,2},{4,5},{5,4},{6,7},{7,6},{8,9},{9,8},{10,11... | collective-permute-start | bytes 1966088 | tf_op jit(solution)/shard_map/ppermute | solution.py:450
  119.0 17.5 %collective-permute-start.8 = (bf16[8,32,1280]{2,1,0:T(8,128)(2,1)S(1)}, bf16[8,32,1280]{2,1,0:T(8,128)(2,1)}, u32[]{:S(2)}, u32[]{:S(2)}) collective-permute-start(bf16[8,32,1280]{2,1,0:T(8,128)(2,1)S(1)} %collective-permute-done.1.refs_2_.refs_4_.refs_5_), channel_id=1, source_target_pairs={{0,4},{1,5},{2,6},{3,7},{4,8},{5,9},{6,10},{7,11},{8,12},{9,13},{1... | collective-permute-start | bytes 1966088 | tf_op jit(solution)/shard_map/ppermute | solution.py:448
  120.2 16.3 %collective-permute-start.9 = (bf16[8,32,1280]{2,1,0:T(8,128)(2,1)}, bf16[8,32,1280]{2,1,0:T(8,128)(2,1)}, u32[]{:S(2)}, u32[]{:S(2)}) collective-permute-start(bf16[8,32,1280]{2,1,0:T(8,128)(2,1)} %collective-permute-done.4.refs_5_.refs_10_.refs_11_), channel_id=1, source_target_pairs={{0,12},{1,13},{2,14},{3,15},{4,0},{5,1},{6,2},{7,3},{8,4},{9,5},{1... | collective-permute-start | bytes 1966088 | tf_op jit(solution)/shard_map/ppermute | solution.py:448
  122.0 15.5 %collective-permute-start.11 = (bf16[16,32,640]{2,1,0:T(8,128)(2,1)S(1)}, bf16[16,32,640]{2,1,0:T(8,128)(2,1)S(1)}, u32[]{:S(2)}, u32[]{:S(2)}) collective-permute-start(bf16[16,32,640]{2,1,0:T(8,128)(2,1)S(1)} %collective-permute-done.5.refs_13_.refs_32_.refs_33_.refs_34_.refs_35_), channel_id=1, source_target_pairs={{0,48},{16,0},{32,16},{48,32},{64,112},{80,64},{96,80},{112,96},{1... | collective-permute-start | bytes 1966088 | tf_op jit(solution)/shard_map/ppermute | solution.py:449
  123.8 16.4 %collective-permute-start.10 = (bf16[16,32,640]{2,1,0:T(8,128)(2,1)S(1)}, bf16[16,32,640]{2,1,0:T(8,128)(2,1)S(1)}, u32[]{:S(2)}, u32[]{:S(2)}) collective-permute-start(bf16[16,32,640]{2,1,0:T(8,128)(2,1)S(1)} %collective-permute-done.5.refs_13_.refs_32_.refs_33_.refs_34_.refs_35_), channel_id=1, source_target_pairs={{0,16},{16,32},{32,48},{48,0},{64,80},{80,96},{96,112},{112,64},{1... | collective-permute-start | bytes 1966088 | tf_op jit(solution)/shard_map/ppermute | solution.py:449
  140.3 4.6 %collective-permute-start.16 = (bf16[8,32,1280]{2,1,0:T(8,128)(2,1)S(1)}, bf16[8,32,1280]{2,1,0:T(8,128)(2,1)S(1)}, u32[]{:S(2)}, u32[]{:S(2)}) collective-permute-start(bf16[8,32,1280]{2,1,0:T(8,128)(2,1)S(1)} %collective-permute-done.3.refs_4_.refs_8_.refs_9_), channel_id=1, source_target_pairs={{0,1},{1,0},{2,3},{3,2},{4,5},{5,4},{6,7},{7,6},{8,9},{9,8},{10,11... | collective-permute-start | bytes 1966088 | tf_op jit(solution)/shard_map/ppermute | solution.py:450
  142.3 19.0 %collective-permute-start.17 = (bf16[8,32,1280]{2,1,0:T(8,128)(2,1)}, bf16[8,32,1280]{2,1,0:T(8,128)(2,1)}, u32[]{:S(2)}, u32[]{:S(2)}) collective-permute-start(bf16[8,32,1280]{2,1,0:T(8,128)(2,1)} %collective-permute-done.4.refs_5_.refs_10_.refs_11_), channel_id=1, source_target_pairs={{0,1},{1,0},{2,3},{3,2},{4,5},{5,4},{6,7},{7,6},{8,9},{9,8},{10,11... | collective-permute-start | bytes 1966088 | tf_op jit(solution)/shard_map/ppermute | solution.py:450
  142.3 19.0 %collective-permute-start.18 = (bf16[8,32,1280]{2,1,0:T(8,128)(2,1)}, bf16[8,32,1280]{2,1,0:T(8,128)(2,1)}, u32[]{:S(2)}, u32[]{:S(2)}) collective-permute-start(bf16[8,32,1280]{2,1,0:T(8,128)(2,1)} %collective-permute-done.8.refs_6_.refs_12_.refs_13_), channel_id=1, source_target_pairs={{0,1},{1,0},{2,3},{3,2},{4,5},{5,4},{6,7},{7,6},{8,9},{9,8},{10,11... | collective-permute-start | bytes 1966088 | tf_op jit(solution)/shard_map/ppermute | solution.py:450
  142.8 18.5 %collective-permute-start.19 = (bf16[8,32,1280]{2,1,0:T(8,128)(2,1)}, bf16[8,32,1280]{2,1,0:T(8,128)(2,1)}, u32[]{:S(2)}, u32[]{:S(2)}) collective-permute-start(bf16[8,32,1280]{2,1,0:T(8,128)(2,1)} %collective-permute-done.9.refs_7_.refs_14_.refs_15_), channel_id=1, source_target_pairs={{0,1},{1,0},{2,3},{3,2},{4,5},{5,4},{6,7},{7,6},{8,9},{9,8},{10,11... | collective-permute-start | bytes 1966088 | tf_op jit(solution)/shard_map/ppermute | solution.py:450
  142.8 18.5 %collective-permute-start.20 = (bf16[16,32,640]{2,1,0:T(8,128)(2,1)S(1)}, bf16[16,32,640]{2,1,0:T(8,128)(2,1)}, u32[]{:S(2)}, u32[]{:S(2)}) collective-permute-start(bf16[16,32,640]{2,1,0:T(8,128)(2,1)S(1)} %collective-permute-done.6.refs_14_.refs_36_.refs_37_.refs_38_.refs_39_), channel_id=1, source_target_pairs={{0,16},{16,32},{32,48},{48,0},{64,80},{80,96},{96,112},{112,64},{1... | collective-permute-start | bytes 1966088 | tf_op jit(solution)/shard_map/ppermute | solution.py:449
  144.9 16.4 %collective-permute-start.21 = (bf16[16,32,640]{2,1,0:T(8,128)(2,1)S(1)}, bf16[16,32,640]{2,1,0:T(8,128)(2,1)}, u32[]{:S(2)}, u32[]{:S(2)}) collective-permute-start(bf16[16,32,640]{2,1,0:T(8,128)(2,1)S(1)} %collective-permute-done.11.refs_17_.refs_48_.refs_49_.refs_50_.refs_51_), channel_id=1, source_target_pairs={{0,48},{16,0},{32,16},{48,32},{64,112},{80,64},{96,80},{112,96},{1... | collective-permute-start | bytes 1966088 | tf_op jit(solution)/shard_map/ppermute | solution.py:449
  (14 other events, 369.1 us)
